TPU v7x, 32 devices: a whole 2x2x4 slice. The times are simulated.
32 devices in a mesh: dp: 2 (over core), ctx: 4 (over y, x), expert: 4 (over z).
Axes of the slice: x: 2, y: 2, z: 4, core: 2. Of those that a mesh axis runs over, the one named last changes fastest.
Arguments:
- tokens: bfloat16 [2, 2048, 768], P('dp', ('ctx', 'expert')), may hold values from -6 to 6
- lengths: int32 [2], P('dp'), may hold values from 512 to 2048, as said below
- routes: int32 [2, 2048, 2], P('dp', ('ctx', 'expert')), may hold values from 0 to 15, all different within a row; in each aligned block of 128 rows (0 to 127, 128 to 255, ..., all dimensions but the last counted through in order) at most 22 rows name the same one
- norm1_gain: float32 [768], replicated, may hold values from 0.5 to 1.5
- query_weight: bfloat16 [768, 768], replicated, may hold values from -0.21875 to 0.21875
- key_weight: bfloat16 [768, 768], replicated, may hold values from -0.21875 to 0.21875
- value_weight: bfloat16 [768, 768], replicated, may hold values from -0.21875 to 0.21875
- output_weight: bfloat16 [768, 768], replicated, may hold values from -6 to 6
- norm2_gain: float32 [768], replicated, may hold values from 0.5 to 1.5
- router_weight: bfloat16 [768, 16], replicated, may hold values from -0.21875 to 0.21875
- expert_gate: bfloat16 [16, 768, 2048], P('expert'), may hold values from -0.21875 to 0.21875
- expert_up: bfloat16 [16, 768, 2048], P('expert'), may hold values from -0.21875 to 0.21875
- expert_down: bfloat16 [16, 2048, 768], P('expert'), may hold values from -0.125 to 0.125
- shared_gate: bfloat16 [768, 2048], replicated, may hold values from -0.21875 to 0.21875
- shared_up: bfloat16 [768, 2048], replicated, may hold values from -0.21875 to 0.21875
- shared_down: bfloat16 [2048, 768], replicated, may hold values from -0.125 to 0.125
- cotangent: bfloat16 [2, 2048, 768], P('dp', ('ctx', 'expert')), may hold values from -6 to 6
Outputs:
- output_rows: bfloat16 [2, 2048, 768], P('dp', ('ctx', 'expert'))
- input_grad: bfloat16 [2, 2048, 768], P('dp', ('ctx', 'expert'))
- norm1_gain_grad: float32 [768], P(('dp', 'ctx', 'expert'))
- query_weight_grad: float32 [768, 768], P(('dp', 'ctx', 'expert'))
- key_weight_grad: float32 [768, 768], P(('dp', 'ctx', 'expert'))
- value_weight_grad: float32 [768, 768], P(('dp', 'ctx', 'expert'))
- output_weight_grad: float32 [768, 768], P(('dp', 'ctx', 'expert'))
- norm2_gain_grad: float32 [768], P(('dp', 'ctx', 'expert'))
- router_weight_grad: float32 [768, 16], P(('dp', 'ctx', 'expert'))
- expert_gate_grad: float32 [16, 768, 2048], P('expert', None, ('dp', 'ctx'))
- expert_up_grad: float32 [16, 768, 2048], P('expert', None, ('dp', 'ctx'))
- expert_down_grad: float32 [16, 2048, 768], P('expert', ('dp', 'ctx'))
- shared_gate_grad: float32 [768, 2048], P(('dp', 'ctx', 'expert'))
- shared_up_grad: float32 [768, 2048], P(('dp', 'ctx', 'expert'))
- shared_down_grad: float32 [2048, 768], P(('dp', 'ctx', 'expert'))
Inputs may be any that keep to these rules, and one draw needn't show every extreme that they name: `lengths`: one slot, drawn from the seed, is valid over all 2048 places; the others over a prefix of at least 512. `routes`: within the 128 tokens of one device (aligned blocks), no expert is named by more than 22 tokens; a token's two experts differ.
All inputs are finite; a program needn't handle non-finite values.
Results may differ from a plain program's by a relative error of at most 0.025.
Values may be sent and summed in bfloat16 or wider, within the bound.
A program may use at most 256 MiB of HBM per device.

v0:
```python
import jax
import jax.numpy as jnp
from jax import lax
from jax.sharding import PartitionSpec as P

HEAD_DIM = 64
EXPERTS = 16
TOP = 2
CAP = 22


norm_epsilon = 1e-06
rope_base = 10000.0
score_scale = 0.125
masked_value = -1e30


def shifted_2(array, axis, by):
    count = lax.axis_size(axis)
    return lax.ppermute(array, axis, [(i, (i + by) % count) for i in range(count)])


def rms_norm(values, gain_vector):
    scale_rows = lax.rsqrt(jnp.mean(values * values, axis=-1, keepdims=True) + norm_epsilon)
    return values * scale_rows * gain_vector


def rotate(values, positions):
    half_dim = values.shape[-1] // 2
    exponent = jnp.arange(half_dim, dtype=jnp.float32) * (2.0 / values.shape[-1])
    inverse_freq = rope_base ** (-exponent)
    angles = positions[:, None] * inverse_freq[None, :]
    cosine = jnp.cos(angles)[:, None, :]
    sine = jnp.sin(angles)[:, None, :]
    first_half = values[..., :half_dim]
    second_half = values[..., half_dim:]
    return jnp.concatenate(
        [first_half * cosine - second_half * sine, second_half * cosine + first_half * sine],
        axis=-1,
    )


def gated_unit(gate_lin, up_lin):
    return jax.nn.silu(gate_lin) * up_lin


def pair_softmax(chosen):
    shifted = chosen - jnp.max(chosen, axis=-1, keepdims=True)
    exponentials = jnp.exp(shifted)
    return exponentials / jnp.sum(exponentials, axis=-1, keepdims=True)


def local(
    tokens,
    lengths,
    routes,
    norm1_gain,
    query_weight,
    key_weight,
    value_weight,
    output_weight,
    norm2_gain,
    router_weight,
    expert_gate,
    expert_up,
    expert_down,
    shared_gate,
    shared_up,
    shared_down,
    cotangent,
):
    expert_size = lax.axis_size("expert")
    ctx_size = lax.axis_size("ctx")
    tok_rows = tokens.shape[1]
    model_width = tokens.shape[2]
    head_count = model_width // HEAD_DIM
    group_rows = tok_rows * expert_size
    first_row = (lax.axis_index("ctx") * expert_size + lax.axis_index("expert")) * tok_rows
    positions = first_row + jnp.arange(tok_rows, dtype=jnp.int32)
    length = lengths[0]
    live_rows = positions < length
    valid_rows = live_rows.astype(jnp.float32)[:, None]
    inputs = tokens[0].astype(jnp.float32)
    angle_pos = positions.astype(jnp.float32)

    def rotate_rows(lin_rows):
        return rotate(lin_rows.reshape(tok_rows, head_count, HEAD_DIM), angle_pos)

    normed, norm_one_back = jax.vjp(rms_norm, inputs, norm1_gain)
    normed_low = normed.astype(jnp.bfloat16)
    query_lin = jnp.dot(normed_low, query_weight, preferred_element_type=jnp.float32)
    key_lin = jnp.dot(normed_low, key_weight, preferred_element_type=jnp.float32)
    value_lin = jnp.dot(normed_low, value_weight, preferred_element_type=jnp.float32)
    query_rot, query_back = jax.vjp(rotate_rows, query_lin)
    key_rot, key_back = jax.vjp(rotate_rows, key_lin)
    query = query_rot.astype(jnp.bfloat16)
    key_own = key_rot.astype(jnp.bfloat16)
    value_own = value_lin.astype(jnp.bfloat16).reshape(tok_rows, head_count, HEAD_DIM)
    key_group, value_group = (
        lax.all_gather(key_own, "expert", axis=0, tiled=True),
        lax.all_gather(value_own, "expert", axis=0, tiled=True),
    )

    def masked_scores(key_rows, offset):
        scores = (
            jnp.einsum("qhd,khd->hqk", query, key_rows, preferred_element_type=jnp.float32)
            * score_scale
        )
        key_pos = offset + jnp.arange(key_rows.shape[0], dtype=jnp.int32)
        allowed = (key_pos[None, :] <= positions[:, None]) & (key_pos < length)[None, :]
        return jnp.where(allowed[None], scores, masked_value)

    def absorb_block(running, key_rows, value_rows, offset):
        running_max, running_sum, running_out = running
        scores = masked_scores(key_rows, offset)
        new_max = jnp.maximum(running_max, jnp.max(scores, axis=-1))
        shrink = jnp.exp(running_max - new_max)
        weights = jnp.exp(scores - new_max[..., None])
        running_sum = running_sum * shrink + jnp.sum(weights, axis=-1)
        running_out = running_out * jnp.transpose(shrink)[:, :, None] + jnp.einsum(
            "hqk,khd->qhd",
            weights.astype(jnp.bfloat16),
            value_rows,
            preferred_element_type=jnp.float32,
        )
        return (new_max, running_sum, running_out)

    start_state = (
        jnp.full((head_count, tok_rows), masked_value, jnp.float32),
        jnp.zeros((head_count, tok_rows), jnp.float32),
        jnp.zeros((tok_rows, head_count, HEAD_DIM), jnp.float32),
    )
    key_rows = lax.all_gather(key_group, "ctx", axis=0, tiled=True)
    value_rows = lax.all_gather(value_group, "ctx", axis=0, tiled=True)
    span_rows = key_rows.shape[0]
    sub_rows = min(span_rows, 2048)

    def absorb_sub(sub_index, inner_state):
        sub_offset = sub_index * sub_rows
        sub_keys = lax.dynamic_slice_in_dim(key_rows, sub_offset, sub_rows, 0)
        sub_values = lax.dynamic_slice_in_dim(value_rows, sub_offset, sub_rows, 0)
        return absorb_block(inner_state, sub_keys, sub_values, sub_offset)

    final_max, final_sum, final_out = lax.fori_loop(
        0, span_rows // sub_rows, absorb_sub, start_state
    )
    log_total = final_max + jnp.log(final_sum)
    attended_heads = final_out / jnp.transpose(final_sum)[:, :, None]
    attended = attended_heads.reshape(tok_rows, model_width).astype(jnp.bfloat16)
    attn_out = jnp.dot(attended, output_weight, preferred_element_type=jnp.float32)
    hidden_in = inputs + valid_rows * attn_out
    normed_two, norm_two_back = jax.vjp(rms_norm, hidden_in, norm2_gain)
    normed_two_low = normed_two.astype(jnp.bfloat16)
    route_ids = routes[0]
    expert_range = jnp.arange(EXPERTS, dtype=jnp.int32)
    picked = (route_ids[:, :, None] == expert_range).astype(jnp.float32)
    logits = jnp.dot(normed_two_low, router_weight, preferred_element_type=jnp.float32)
    chosen = jnp.sum(picked * logits[:, None, :], axis=-1)
    gate_weights, gate_back = jax.vjp(pair_softmax, chosen)
    expert_hits = (
        ((route_ids[:, :, None] == expert_range) & live_rows[:, None, None])
        .astype(jnp.int32)
        .reshape(tok_rows * TOP, EXPERTS)
    )
    places = jnp.sum((jnp.cumsum(expert_hits, axis=0) - 1) * expert_hits, axis=-1)
    live_pairs = jnp.broadcast_to(live_rows[:, None], (tok_rows, TOP)).reshape(-1)
    slot_ids = jnp.where(live_pairs, route_ids.reshape(-1) * CAP + places, -1)
    dispatch = (
        (slot_ids[:, None] == jnp.arange(EXPERTS * CAP, dtype=jnp.int32)[None, :])
        .astype(jnp.bfloat16)
        .reshape(tok_rows, TOP, EXPERTS * CAP)
    )
    send_rows = (
        jnp.einsum("tks,td->sd", dispatch, normed_two_low, preferred_element_type=jnp.float32)
        .astype(jnp.bfloat16)
        .reshape(EXPERTS, CAP, model_width)
    )
    expert_rows = lax.all_to_all(send_rows, "expert", split_axis=0, concat_axis=1, tiled=True)
    gate_lin = jnp.einsum(
        "erd,edf->erf", expert_rows, expert_gate, preferred_element_type=jnp.float32
    )
    up_lin = jnp.einsum("erd,edf->erf", expert_rows, expert_up, preferred_element_type=jnp.float32)
    hidden, hidden_back = jax.vjp(gated_unit, gate_lin, up_lin)
    hidden_low = hidden.astype(jnp.bfloat16)
    expert_result = jnp.einsum(
        "erf,efd->erd", hidden_low, expert_down, preferred_element_type=jnp.float32
    ).astype(jnp.bfloat16)
    returned = lax.all_to_all(
        expert_result, "expert", split_axis=1, concat_axis=0, tiled=True
    ).reshape(EXPERTS * CAP, model_width)
    per_choice = jnp.einsum("tks,sd->tkd", dispatch, returned, preferred_element_type=jnp.float32)
    mixed = jnp.sum(gate_weights[:, :, None] * per_choice, axis=1)
    shared_gate_lin = jnp.dot(normed_two_low, shared_gate, preferred_element_type=jnp.float32)
    shared_up_lin = jnp.dot(normed_two_low, shared_up, preferred_element_type=jnp.float32)
    shared_hidden, shared_back = jax.vjp(gated_unit, shared_gate_lin, shared_up_lin)
    shared_low = shared_hidden.astype(jnp.bfloat16)
    shared_out = jnp.dot(shared_low, shared_down, preferred_element_type=jnp.float32)
    output_rows = (hidden_in + valid_rows * (mixed + shared_out)).astype(jnp.bfloat16)[None]
    upstream = cotangent[0].astype(jnp.float32)
    d_branch = valid_rows * upstream
    d_branch_low = d_branch.astype(jnp.bfloat16)
    d_shared_down = jnp.einsum(
        "tf,td->fd", shared_low, d_branch_low, preferred_element_type=jnp.float32
    )
    d_shared_hidden = jnp.einsum(
        "td,fd->tf", d_branch_low, shared_down, preferred_element_type=jnp.float32
    )
    d_sg, d_su = shared_back(d_shared_hidden)
    d_sg_low = d_sg.astype(jnp.bfloat16)
    d_su_low = d_su.astype(jnp.bfloat16)
    d_shared_gate = jnp.einsum(
        "td,tf->df", normed_two_low, d_sg_low, preferred_element_type=jnp.float32
    )
    d_shared_up = jnp.einsum(
        "td,tf->df", normed_two_low, d_su_low, preferred_element_type=jnp.float32
    )
    d_normed_two = jnp.einsum(
        "tf,df->td", d_sg_low, shared_gate, preferred_element_type=jnp.float32
    )
    d_normed_two = d_normed_two + jnp.einsum(
        "tf,df->td", d_su_low, shared_up, preferred_element_type=jnp.float32
    )
    d_choice_out = (gate_weights[:, :, None] * d_branch[:, None, :]).astype(jnp.bfloat16)
    grad_send = (
        jnp.einsum("tks,tkd->sd", dispatch, d_choice_out, preferred_element_type=jnp.float32)
        .astype(jnp.bfloat16)
        .reshape(EXPERTS, CAP, model_width)
    )
    d_gates = jnp.sum(per_choice * d_branch[:, None, :], axis=-1)
    d_chosen = gate_back(d_gates)[0]
    d_logits = jnp.sum(picked * d_chosen[:, :, None], axis=1).astype(jnp.bfloat16)
    d_router = jnp.einsum("td,te->de", normed_two_low, d_logits, preferred_element_type=jnp.float32)
    d_normed_two = d_normed_two + jnp.einsum(
        "te,de->td", d_logits, router_weight, preferred_element_type=jnp.float32
    )
    grad_recv = lax.all_to_all(grad_send, "expert", split_axis=0, concat_axis=1, tiled=True)
    d_expert_down = jnp.einsum(
        "erf,erd->efd", hidden_low, grad_recv, preferred_element_type=jnp.float32
    )
    d_hidden = jnp.einsum(
        "erd,efd->erf", grad_recv, expert_down, preferred_element_type=jnp.float32
    )
    d_gate_lin, d_up_lin = hidden_back(d_hidden)
    d_gate_low = d_gate_lin.astype(jnp.bfloat16)
    d_up_low = d_up_lin.astype(jnp.bfloat16)
    d_expert_gate = jnp.einsum(
        "erd,erf->edf", expert_rows, d_gate_low, preferred_element_type=jnp.float32
    )
    d_expert_up = jnp.einsum(
        "erd,erf->edf", expert_rows, d_up_low, preferred_element_type=jnp.float32
    )
    d_expert_rows = jnp.einsum(
        "erf,edf->erd", d_gate_low, expert_gate, preferred_element_type=jnp.float32
    )
    d_expert_rows = (
        d_expert_rows
        + jnp.einsum("erf,edf->erd", d_up_low, expert_up, preferred_element_type=jnp.float32)
    ).astype(jnp.bfloat16)
    d_returned = lax.all_to_all(
        d_expert_rows, "expert", split_axis=1, concat_axis=0, tiled=True
    ).reshape(EXPERTS * CAP, model_width)
    d_normed_two = d_normed_two + jnp.einsum(
        "tks,sd->td", dispatch, d_returned, preferred_element_type=jnp.float32
    )
    d_hidden_norm, d_gain_two = norm_two_back(d_normed_two)
    d_hidden_in = upstream + d_hidden_norm
    d_attn_low = (valid_rows * d_hidden_in).astype(jnp.bfloat16)
    d_output_weight = jnp.einsum(
        "td,te->de", attended, d_attn_low, preferred_element_type=jnp.float32
    )
    d_attended = jnp.einsum(
        "te,de->td", d_attn_low, output_weight, preferred_element_type=jnp.float32
    )
    d_attended_low = d_attended.astype(jnp.bfloat16).reshape(tok_rows, head_count, HEAD_DIM)
    row_delta = jnp.einsum("qhd,qhd->hq", d_attended_low.astype(jnp.float32), attended_heads)

    def contribute(key_rows, value_rows, offset):
        scores = masked_scores(key_rows, offset)
        probabilities = jnp.exp(scores - log_total[..., None])
        d_weights = jnp.einsum(
            "qhd,khd->hqk", d_attended_low, value_rows, preferred_element_type=jnp.float32
        )
        d_scores = (probabilities * (d_weights - row_delta[..., None])).astype(jnp.bfloat16)
        query_add = jnp.einsum(
            "hqk,khd->qhd", d_scores, key_rows, preferred_element_type=jnp.float32
        )
        key_add = jnp.einsum("hqk,qhd->khd", d_scores, query, preferred_element_type=jnp.float32)
        value_add = jnp.einsum(
            "hqk,qhd->khd",
            probabilities.astype(jnp.bfloat16),
            d_attended_low,
            preferred_element_type=jnp.float32,
        )
        return (query_add, key_add, value_add)

    zero_grad = jnp.zeros((group_rows, head_count, HEAD_DIM), jnp.float32)
    ctx_index = lax.axis_index("ctx")

    def cycle_turn(turn_index, state):
        key_rows, value_rows, key_grad, value_grad, query_grad = state
        owner_ctx = (ctx_index - turn_index) % ctx_size
        visit_keys = key_rows
        visit_values = value_rows
        query_add, key_add, value_add = contribute(visit_keys, visit_values, owner_ctx * group_rows)
        key_grad = key_grad + key_add
        value_grad = value_grad + value_add
        key_wide, value_wide, key_grad, value_grad = (
            shifted_2(key_rows.astype(jnp.float32).astype(jnp.bfloat16), "ctx", 1).astype(
                jnp.float32
            ),
            shifted_2(value_rows.astype(jnp.float32).astype(jnp.bfloat16), "ctx", 1).astype(
                jnp.float32
            ),
            shifted_2(key_grad.astype(jnp.bfloat16), "ctx", 1).astype(key_grad.dtype),
            shifted_2(value_grad.astype(jnp.bfloat16), "ctx", 1).astype(value_grad.dtype),
        )
        key_rows = key_wide.astype(jnp.bfloat16)
        value_rows = value_wide.astype(jnp.bfloat16)
        return (key_rows, value_rows, key_grad, value_grad, query_grad + query_add)

    cycle_state = lax.fori_loop(
        0,
        ctx_size,
        cycle_turn,
        (
            key_group,
            value_group,
            zero_grad,
            zero_grad,
            jnp.zeros((tok_rows, head_count, HEAD_DIM), jnp.float32),
        ),
    )
    key_grad = cycle_state[2]
    value_grad = cycle_state[3]
    query_grad = cycle_state[4]
    key_grad, value_grad = (
        lax.psum_scatter(
            key_grad.astype(jnp.bfloat16), "expert", scatter_dimension=0, tiled=True
        ).astype(jnp.float32),
        lax.psum_scatter(
            value_grad.astype(jnp.bfloat16), "expert", scatter_dimension=0, tiled=True
        ).astype(jnp.float32),
    )
    d_query_lin = query_back(query_grad * score_scale)[0].astype(jnp.bfloat16)
    d_key_lin = key_back(key_grad * score_scale)[0].astype(jnp.bfloat16)
    d_value_lin = value_grad.reshape(tok_rows, model_width).astype(jnp.bfloat16)
    d_query_weight = jnp.einsum(
        "td,te->de", normed_low, d_query_lin, preferred_element_type=jnp.float32
    )
    d_key_weight = jnp.einsum(
        "td,te->de", normed_low, d_key_lin, preferred_element_type=jnp.float32
    )
    d_value_weight = jnp.einsum(
        "td,te->de", normed_low, d_value_lin, preferred_element_type=jnp.float32
    )
    d_normed = jnp.einsum(
        "te,de->td", d_query_lin, query_weight, preferred_element_type=jnp.float32
    )
    d_normed = d_normed + jnp.einsum(
        "te,de->td", d_key_lin, key_weight, preferred_element_type=jnp.float32
    )
    d_normed = d_normed + jnp.einsum(
        "te,de->td", d_value_lin, value_weight, preferred_element_type=jnp.float32
    )
    d_input_norm, d_gain_one = norm_one_back(d_normed)
    input_grad = (d_hidden_in + d_input_norm).astype(jnp.bfloat16)[None]
    dense_sums = (
        lax.psum_scatter(d_gain_one, ("dp", "ctx", "expert"), scatter_dimension=0, tiled=True),
        lax.psum_scatter(d_query_weight, ("dp", "ctx", "expert"), scatter_dimension=0, tiled=True),
        lax.psum_scatter(d_key_weight, ("dp", "ctx", "expert"), scatter_dimension=0, tiled=True),
        lax.psum_scatter(d_value_weight, ("dp", "ctx", "expert"), scatter_dimension=0, tiled=True),
        lax.psum_scatter(d_output_weight, ("dp", "ctx", "expert"), scatter_dimension=0, tiled=True),
        lax.psum_scatter(d_gain_two, ("dp", "ctx", "expert"), scatter_dimension=0, tiled=True),
        lax.psum_scatter(d_router, ("dp", "ctx", "expert"), scatter_dimension=0, tiled=True),
        lax.psum_scatter(d_shared_gate, ("dp", "ctx", "expert"), scatter_dimension=0, tiled=True),
        lax.psum_scatter(d_shared_up, ("dp", "ctx", "expert"), scatter_dimension=0, tiled=True),
        lax.psum_scatter(d_shared_down, ("dp", "ctx", "expert"), scatter_dimension=0, tiled=True),
    )
    gate_sum, up_sum = (
        lax.psum_scatter(
            d_expert_gate.astype(jnp.bfloat16), ("dp", "ctx"), scatter_dimension=2, tiled=True
        ).astype(jnp.float32),
        lax.psum_scatter(
            d_expert_up.astype(jnp.bfloat16), ("dp", "ctx"), scatter_dimension=2, tiled=True
        ).astype(jnp.float32),
    )
    down_sum = lax.psum_scatter(
        d_expert_down.astype(jnp.bfloat16), ("dp", "ctx"), scatter_dimension=1, tiled=True
    ).astype(jnp.float32)
    return (
        output_rows,
        input_grad,
        dense_sums[0],
        dense_sums[1],
        dense_sums[2],
        dense_sums[3],
        dense_sums[4],
        dense_sums[5],
        dense_sums[6],
        gate_sum,
        up_sum,
        down_sum,
        dense_sums[7],
        dense_sums[8],
        dense_sums[9],
    )


def solution(mesh):
    placed = (
        P("dp", ("ctx", "expert"), None),
        P("dp"),
        P("dp", ("ctx", "expert"), None),
        P(),
        P(),
        P(),
        P(),
        P(),
        P(),
        P(),
        P("expert", None, None),
        P("expert", None, None),
        P("expert", None, None),
        P(),
        P(),
        P(),
        P("dp", ("ctx", "expert"), None),
    )
    return jax.shard_map(
        local,
        mesh=mesh,
        in_specs=placed,
        out_specs=(
            P("dp", ("ctx", "expert"), None),
            P("dp", ("ctx", "expert"), None),
            P(("dp", "ctx", "expert")),
            P(("dp", "ctx", "expert"), None),
            P(("dp", "ctx", "expert"), None),
            P(("dp", "ctx", "expert"), None),
            P(("dp", "ctx", "expert"), None),
            P(("dp", "ctx", "expert")),
            P(("dp", "ctx", "expert"), None),
            P("expert", None, ("dp", "ctx")),
            P("expert", None, ("dp", "ctx")),
            P("expert", ("dp", "ctx"), None),
            P(("dp", "ctx", "expert"), None),
            P(("dp", "ctx", "expert"), None),
            P(("dp", "ctx", "expert"), None),
        ),
        check_vma=False,
    )
```

profile of v0, /device:TPU:0, one launch (start us, length us, event | category | flops | bytes accessed | tf_op | source)
XLA Modules:
  0.0 1709.8 jit_solution(950315294655352657)
XLA Ops:
  18.0 20.8 %all_gather.12 = bf16[512,12,64]{0,2,1:T(8,128)(2,1)} all-gather(bf16[128,12,64]{0,2,1:T(8,128)(2,1)S(1)} %pad_maximum_fusion.1), channel_id=1, replica_groups=mesh['dp'=2,'ctx'=4,'expert'=4] {'expert'}, dimensions={0}, use_global_device_ids=true | all-gather | bytes 983040 | tf_op jit(solution)/shard_map/all_gather | solution.py:100
  42.3 17.2 %all_gather.14 = bf16[512,12,64]{0,2,1:T(8,128)(2,1)} all-gather(bf16[128,12,64]{0,2,1:T(8,128)(2,1)S(1)} %bitcast.266), channel_id=1, replica_groups=mesh['dp'=2,'ctx'=4,'expert'=4] {'expert'}, dimensions={0}, use_global_device_ids=true | all-gather | bytes 983040 | tf_op jit(solution)/shard_map/all_gather | solution.py:101
  67.3 14.2 all-gather.3.cloned.1.call-done
  91.8 35.2 %all-gather.5.cloned.1.call-done = bf16[2048,12,64]{0,2,1:T(8,128)(2,1)} async-done(((bf16[512,12,64]{0,2,1:T(8,128)(2,1)}), bf16[2048,12,64]{0,2,1:T(8,128)(2,1)}) %all-gather.5.cloned.1.call-update) | async-done | bytes 3145744 | tf_op jit(solution)/shard_map/all_gather | solution.py:134
  272.0 314.0 %while.7 = (s32[]{:T(128)}, bf16[512,12,64]{0,2,1:T(8,128)(2,1)}, bf16[512,12,64]{0,2,1:T(8,128)(2,1)}, f32[512,12,64]{0,2,1:T(8,128)}, f32[512,12,64]{0,2,1:T(8...) while((s32[]{:T(128)}, bf16[512,12,64]{0,2,1:T(8,128)(2,1)}, ...), condition=%wide.region_19.20_spmd.clone, body=%wide.region_18.19_spmd.clone.sunk | while | flops 514655872 | bytes 63160936 | solution.py:321
  306.6 14.4 collective-permute-done.3
  323.5 14.4 collective-permute-done
  386.5 14.4 collective-permute-done.3
  403.4 14.4 collective-permute-done
  465.5 14.4 collective-permute-done.3
  482.3 14.4 collective-permute-done
  543.5 14.4 collective-permute-done.3
  560.3 14.4 collective-permute-done
  663.9 37.9 %all-reduce.7 = (f32[768]{0:T(1024)S(1)}, f32[768]{0:T(1024)S(1)}, f32[768,16]{0,1:T(8,128)S(1)}) all-reduce(f32[768]{0:T(1024)S(1)} %get-tuple-element.421, f32[768]{0:T(1024)S(1)} %copy-done.44, f32[768,16]{0,1:T(8,128)S(1)} %copy-done.33), channel_id=4, replica_groups=mesh['dp'=2,'ctx'=4,'expert'=4] {'dp','ctx','expert'}, use_global_device_ids=true, to_apply=%region_24.25.clone | all-reduce | flops 13824 | bytes 110592
  705.7 27.1 %reduce-scatter.26.cloned.1.call-done = bf16[4,768,256]{2,1,0:T(8,128)(2,1)} async-done(((bf16[4,768,2048]{2,1,0:T(8,128)(2,1)}), bf16[4,768,256]{2,1,0:T(8,128)(2,1)}) %reduce-scatter.26.cloned.1.call-update) | async-done | bytes 1572880 | tf_op jit(solution)/shard_map/reduce_scatter | solution.py:380
  736.2 92.4 %reduce-scatter.28.cloned.1.call-done = bf16[4,768,256]{2,1,0:T(8,128)(2,1)} async-done(((bf16[4,768,2048]{2,1,0:T(8,128)(2,1)}), bf16[4,768,256]{2,1,0:T(8,128)(2,1)}) %reduce-scatter.28.cloned.1.call-update) | async-done | bytes 1572880 | tf_op jit(solution)/shard_map/reduce_scatter | solution.py:383
  831.9 92.6 %reduce-scatter.30.cloned.1.call-done = bf16[4,256,768]{2,1,0:T(8,128)(2,1)} async-done(((bf16[4,2048,768]{2,1,0:T(8,128)(2,1)}), bf16[4,256,768]{2,1,0:T(8,128)(2,1)}) %reduce-scatter.30.cloned.1.call-update) | async-done | bytes 1572880 | tf_op jit(solution)/shard_map/reduce_scatter | solution.py:387
  927.9 101.6 %reduce-scatter.24.cloned.1.call-done = f32[24,768]{1,0:T(8,128)} async-done(((f32[768,768]{1,0:T(8,128)}), f32[24,768]{1,0:T(8,128)}) %reduce-scatter.24.cloned.1.call-update) | async-done | bytes 73744 | tf_op jit(solution)/shard_map/reduce_scatter | solution.py:372
  1029.5 104.8 %reduce-scatter.18.cloned.1.call-done = f32[24,768]{1,0:T(8,128)} async-done(((f32[768,768]{1,0:T(8,128)}), f32[24,768]{1,0:T(8,128)}) %reduce-scatter.18.cloned.1.call-update) | async-done | bytes 73744 | tf_op jit(solution)/shard_map/reduce_scatter | solution.py:369
  1134.2 103.8 %reduce-scatter.20.cloned.1.call-done = f32[24,768]{1,0:T(8,128)} async-done(((f32[768,768]{1,0:T(8,128)}), f32[24,768]{1,0:T(8,128)}) %reduce-scatter.20.cloned.1.call-update) | async-done | bytes 73744 | tf_op jit(solution)/shard_map/reduce_scatter | solution.py:370
  1238.1 104.8 %reduce-scatter.22.cloned.1.call-done = f32[24,768]{1,0:T(8,128)} async-done(((f32[768,768]{1,0:T(8,128)}), f32[24,768]{1,0:T(8,128)}) %reduce-scatter.22.cloned.1.call-update) | async-done | bytes 73744 | tf_op jit(solution)/shard_map/reduce_scatter | solution.py:371
  1342.8 119.5 %reduce-scatter.32.cloned.1.call-done = f32[24,2048]{1,0:T(8,128)} async-done(((f32[768,2048]{1,0:T(8,128)}), f32[24,2048]{1,0:T(8,128)}) %reduce-scatter.32.cloned.1.call-update) | async-done | bytes 196624 | tf_op jit(solution)/shard_map/reduce_scatter | solution.py:375
  1462.3 120.9 %reduce-scatter.34.cloned.1.call-done = f32[24,2048]{1,0:T(8,128)} async-done(((f32[768,2048]{1,0:T(8,128)}), f32[24,2048]{1,0:T(8,128)}) %reduce-scatter.34.cloned.1.call-update) | async-done | bytes 196624 | tf_op jit(solution)/shard_map/reduce_scatter | solution.py:376
  1583.3 119.6 %reduce-scatter.36.cloned.1.call-done = f32[64,768]{1,0:T(8,128)} async-done(((f32[2048,768]{1,0:T(8,128)}), f32[64,768]{1,0:T(8,128)}) %reduce-scatter.36.cloned.1.call-update) | async-done | bytes 196624 | tf_op jit(solution)/shard_map/reduce_scatter | solution.py:377
  (377 shorter events, 466.3 us)
Async XLA Ops:
  7.2 74.2 %all-gather.3.cloned.1.call-start = ((), (), s32[]{:S(2)}) async-start(), calls=%async_computation.16 | async-start | bytes 3932160 | tf_op jit(solution)/shard_map/all_gather | solution.py:133
  38.8 88.3 %all-gather.5.cloned.1.call-start = ((), (), s32[]{:S(2)}) async-start(), calls=%async_computation.17 | async-start | bytes 3932160 | tf_op jit(solution)/shard_map/all_gather | solution.py:134
  240.6 389.7 %reduce-scatter.38.cloned.1.call-start = ((), (), s32[]{:S(2)}) async-start(), calls=%async_computation.28 | async-start | bytes 983040
  287.4 50.5 %collective-permute-start = (bf16[512,12,64]{0,2,1:T(8,128)(2,1)}, bf16[512,12,64]{0,2,1:T(8,128)(2,1)}, u32[]{:S(2)}, u32[]{:S(2)}) collective-permute-start(bf16[512,12,64]{0,2,1:T(8,128)(2,1)} %copy.155), channel_id=1, source_target_pairs={{0,4},{4,8},{8,12},{12,0},{1,5},{5,9},{9,13},{13,1},{2,6},{6,10},{... | collective-permute-start | bytes 2359304 | tf_op jit(solution)/shard_map/while/body/eval_jaxpr/ppermute | solution.py:20
  288.4 63.5 %collective-permute-start.1 = (bf16[512,12,64]{0,2,1:T(8,128)(2,1)}, bf16[512,12,64]{0,2,1:T(8,128)(2,1)}, u32[]{:S(2)}, u32[]{:S(2)}) collective-permute-start(bf16[512,12,64]{0,2,1:T(8,128)(2,1)} %copy.156), channel_id=1, source_target_pairs={{0,4},{4,8},{8,12},{12,0},{1,5},{5,9},{9,13},{13,1},{2,6},{6,10},{... | collective-permute-start | bytes 2359304 | tf_op jit(solution)/shard_map/while/body/eval_jaxpr/ppermute | solution.py:20
  365.3 35.6 %collective-permute-start.3 = (bf16[512,12,64]{0,2,1:T(8,128)(2,1)}, bf16[512,12,64]{0,2,1:T(8,128)(2,1)}, u32[]{:S(2)}, u32[]{:S(2)}) collective-permute-start(bf16[512,12,64]{0,2,1:T(8,128)(2,1)} %fusion.227), channel_id=1, source_target_pairs={{0,4},{4,8},{8,12},{12,0},{1,5},{5,9},{9,13},{13,1},{2,6},{6,10},{... | collective-permute-start | bytes 2359304 | tf_op jit(solution)/shard_map/while/body/eval_jaxpr/ppermute | solution.py:20
  367.3 50.4 %collective-permute-start = (bf16[512,12,64]{0,2,1:T(8,128)(2,1)}, bf16[512,12,64]{0,2,1:T(8,128)(2,1)}, u32[]{:S(2)}, u32[]{:S(2)}) collective-permute-start(bf16[512,12,64]{0,2,1:T(8,128)(2,1)} %copy.155), channel_id=1, source_target_pairs={{0,4},{4,8},{8,12},{12,0},{1,5},{5,9},{9,13},{13,1},{2,6},{6,10},{... | collective-permute-start | bytes 2359304 | tf_op jit(solution)/shard_map/while/body/eval_jaxpr/ppermute | solution.py:20
  368.3 62.5 %collective-permute-start.1 = (bf16[512,12,64]{0,2,1:T(8,128)(2,1)}, bf16[512,12,64]{0,2,1:T(8,128)(2,1)}, u32[]{:S(2)}, u32[]{:S(2)}) collective-permute-start(bf16[512,12,64]{0,2,1:T(8,128)(2,1)} %copy.156), channel_id=1, source_target_pairs={{0,4},{4,8},{8,12},{12,0},{1,5},{5,9},{9,13},{13,1},{2,6},{6,10},{... | collective-permute-start | bytes 2359304 | tf_op jit(solution)/shard_map/while/body/eval_jaxpr/ppermute | solution.py:20
  444.3 35.6 %collective-permute-start.3 = (bf16[512,12,64]{0,2,1:T(8,128)(2,1)}, bf16[512,12,64]{0,2,1:T(8,128)(2,1)}, u32[]{:S(2)}, u32[]{:S(2)}) collective-permute-start(bf16[512,12,64]{0,2,1:T(8,128)(2,1)} %fusion.227), channel_id=1, source_target_pairs={{0,4},{4,8},{8,12},{12,0},{1,5},{5,9},{9,13},{13,1},{2,6},{6,10},{... | collective-permute-start | bytes 2359304 | tf_op jit(solution)/shard_map/while/body/eval_jaxpr/ppermute | solution.py:20
  446.2 50.4 %collective-permute-start = (bf16[512,12,64]{0,2,1:T(8,128)(2,1)}, bf16[512,12,64]{0,2,1:T(8,128)(2,1)}, u32[]{:S(2)}, u32[]{:S(2)}) collective-permute-start(bf16[512,12,64]{0,2,1:T(8,128)(2,1)} %copy.155), channel_id=1, source_target_pairs={{0,4},{4,8},{8,12},{12,0},{1,5},{5,9},{9,13},{13,1},{2,6},{6,10},{... | collective-permute-start | bytes 2359304 | tf_op jit(solution)/shard_map/while/body/eval_jaxpr/ppermute | solution.py:20
  447.2 61.6 %collective-permute-start.1 = (bf16[512,12,64]{0,2,1:T(8,128)(2,1)}, bf16[512,12,64]{0,2,1:T(8,128)(2,1)}, u32[]{:S(2)}, u32[]{:S(2)}) collective-permute-start(bf16[512,12,64]{0,2,1:T(8,128)(2,1)} %copy.156), channel_id=1, source_target_pairs={{0,4},{4,8},{8,12},{12,0},{1,5},{5,9},{9,13},{13,1},{2,6},{6,10},{... | collective-permute-start | bytes 2359304 | tf_op jit(solution)/shard_map/while/body/eval_jaxpr/ppermute | solution.py:20
  524.3 50.4 %collective-permute-start = (bf16[512,12,64]{0,2,1:T(8,128)(2,1)}, bf16[512,12,64]{0,2,1:T(8,128)(2,1)}, u32[]{:S(2)}, u32[]{:S(2)}) collective-permute-start(bf16[512,12,64]{0,2,1:T(8,128)(2,1)} %copy.155), channel_id=1, source_target_pairs={{0,4},{4,8},{8,12},{12,0},{1,5},{5,9},{9,13},{13,1},{2,6},{6,10},{... | collective-permute-start | bytes 2359304 | tf_op jit(solution)/shard_map/while/body/eval_jaxpr/ppermute | solution.py:20
  525.2 60.7 %collective-permute-start.1 = (bf16[512,12,64]{0,2,1:T(8,128)(2,1)}, bf16[512,12,64]{0,2,1:T(8,128)(2,1)}, u32[]{:S(2)}, u32[]{:S(2)}) collective-permute-start(bf16[512,12,64]{0,2,1:T(8,128)(2,1)} %copy.156), channel_id=1, source_target_pairs={{0,4},{4,8},{8,12},{12,0},{1,5},{5,9},{9,13},{13,1},{2,6},{6,10},{... | collective-permute-start | bytes 2359304 | tf_op jit(solution)/shard_map/while/body/eval_jaxpr/ppermute | solution.py:20
  590.7 47.0 %reduce-scatter.40.cloned.1.call-start = ((), (), s32[]{:S(2)}) async-start(), calls=%async_computation.29 | async-start | bytes 983040 | tf_op jit(solution)/shard_map/convert_element_type | solution.py:346
  595.5 137.3 %reduce-scatter.26.cloned.1.call-start = ((), (), s32[]{:S(2)}) async-start(), calls=%async_computation.22 | async-start | bytes 14155776 | tf_op jit(solution)/shard_map/reduce_scatter | solution.py:380
  605.1 223.5 %reduce-scatter.28.cloned.1.call-start = ((), (), s32[]{:S(2)}) async-start(), calls=%async_computation.23 | async-start | bytes 14155776 | tf_op jit(solution)/shard_map/reduce_scatter | solution.py:383
  614.9 309.6 %reduce-scatter.30.cloned.1.call-start = ((), (), s32[]{:S(2)}) async-start(), calls=%async_computation.24 | async-start | bytes 14155776 | tf_op jit(solution)/shard_map/reduce_scatter | solution.py:387
  624.6 404.9 %reduce-scatter.24.cloned.1.call-start = ((), (), s32[]{:S(2)}) async-start(), calls=%async_computation.21 | async-start | bytes 2433024 | tf_op jit(solution)/shard_map/reduce_scatter | solution.py:372
  628.5 505.8 %reduce-scatter.18.cloned.1.call-start = ((), (), s32[]{:S(2)}) async-start(), calls=%async_computation.18 | async-start | bytes 2433024 | tf_op jit(solution)/shard_map/reduce_scatter | solution.py:369
  635.4 602.6 %reduce-scatter.20.cloned.1.call-start = ((), (), s32[]{:S(2)}) async-start(), calls=%async_computation.19 | async-start | bytes 2433024 | tf_op jit(solution)/shard_map/reduce_scatter | solution.py:370
  637.6 705.3 %reduce-scatter.22.cloned.1.call-start = ((), (), s32[]{:S(2)}) async-start(), calls=%async_computation.20 | async-start | bytes 2433024 | tf_op jit(solution)/shard_map/reduce_scatter | solution.py:371
  640.6 821.8 %reduce-scatter.32.cloned.1.call-start = ((), (), s32[]{:S(2)}) async-start(), calls=%async_computation.25 | async-start | bytes 6488064 | tf_op jit(solution)/shard_map/reduce_scatter | solution.py:375
  645.8 937.5 %reduce-scatter.34.cloned.1.call-start = ((), (), s32[]{:S(2)}) async-start(), calls=%async_computation.26 | async-start | bytes 6488064 | tf_op jit(solution)/shard_map/reduce_scatter | solution.py:376
  651.8 1051.0 %reduce-scatter.36.cloned.1.call-start = ((), (), s32[]{:S(2)}) async-start(), calls=%async_computation.27 | async-start | bytes 6488064 | tf_op jit(solution)/shard_map/reduce_scatter | solution.py:377
  (79 other events, 832.7 us)
Sparse Core Ops, SparseCore 0:
  38.9 42.4 all-gather.2
  83.3 43.7 all-gather.4
  590.8 20.5 reduce-scatter.37
  614.1 22.5 reduce-scatter.39
  640.0 92.7 reduce-scatter.25
  736.2 92.3 reduce-scatter.27
  832.1 92.3 reduce-scatter.29
  930.4 99.0 reduce-scatter.23
  1036.2 98.0 reduce-scatter.17
  1140.0 98.0 reduce-scatter.19
  1244.8 97.9 reduce-scatter.21
  1348.9 113.3 reduce-scatter.31
  1469.5 113.7 reduce-scatter.33
  1589.3 113.4 reduce-scatter.35
where the time goes:
time: 1720 us; the launch traced here: 1710 us
  waiting for transfers between devices  1260 us (73%)
  matrix products  201 us (12%)
  blocking collectives  75.9 us (4%)
  other arithmetic  64 us (4%)
  local copies, waits for them, and re-layouts  59.3 us (3%)
  starting transfers between devices  37.8 us (2%)
    ppermute x16, waiting for transfers between devices, shifted_2(): lax.ppermute(array, axis, [(i, (i + by) % count) for i in range(count)])  212 us
    reduce_scatter x1, waiting for transfers between devices, local(): lax.psum_scatter(d_shared_up, ('dp', 'ctx', 'expert'), scatter_dimension=...  121 us
    reduce_scatter x1, waiting for transfers between devices, local(): lax.psum_scatter(d_shared_down, ('dp', 'ctx', 'expert'), scatter_dimensio...  120 us
    reduce_scatter x1, waiting for transfers between devices, local(): lax.psum_scatter(d_shared_gate, ('dp', 'ctx', 'expert'), scatter_dimensio...  120 us
    reduce_scatter x1, waiting for transfers between devices, local(): lax.psum_scatter(d_query_weight, ('dp', 'ctx', 'expert'), scatter_dimensi...  105 us
    reduce_scatter x1, waiting for transfers between devices, local(): lax.psum_scatter(d_value_weight, ('dp', 'ctx', 'expert'), scatter_dimensi...  105 us
    reduce_scatter x1, waiting for transfers between devices, local(): lax.psum_scatter(d_key_weight, ('dp', 'ctx', 'expert'), scatter_dimension...  104 us
    reduce_scatter x1, waiting for transfers between devices, local(): lax.psum_scatter(d_output_weight, ('dp', 'ctx', 'expert'), scatter_dimens...  102 us
  transfers between devices with their start and end apart: 34, of which 30 were waited for; matrix products, arithmetic and copies ran while one was open for 12% of the time, Pallas kernels for 0%

commit v1 on v0

v1 whole, which is shorter than its diff:
```python
import functools

import jax
import jax.numpy as jnp
from jax import lax
from jax.experimental import pallas as pl
from jax.experimental.pallas import tpu as pltpu
from jax.sharding import PartitionSpec as P

HEAD_DIM = 64
EXPERTS = 16
TOP = 2
CAP = 22
PLACES = 24

norm_epsilon = 1e-06
rope_base = 10000.0
score_scale = 0.125
masked_value = -1e30
PLANE = ("dp", "ctx")
SLOT = ("ctx", "expert")
bf16 = jnp.bfloat16
f32 = jnp.float32


def rms_scale(values):
    return lax.rsqrt(jnp.mean(values * values, axis=-1, keepdims=True) + norm_epsilon)


def rms_back(normal, scale, gain, upstream):
    lifted = upstream * gain
    return scale * (lifted - normal * jnp.mean(lifted * normal, axis=-1, keepdims=True))


def rope_tables(positions):
    half = HEAD_DIM // 2
    exponent = jnp.arange(half, dtype=f32) * (2.0 / HEAD_DIM)
    inverse_freq = rope_base ** (-exponent)
    angles = inverse_freq[:, None] * positions[None, :].astype(f32)
    return jnp.cos(angles), jnp.sin(angles)


def head_rows(qkv_ref, first, count):
    return jnp.concatenate(
        [qkv_ref[block, first : first + count, :] for block in range(qkv_ref.shape[0])], axis=1
    )


def live_keys(key_t, length):
    span = key_t.shape[1]
    place = lax.broadcasted_iota(jnp.int32, (8, span), 1)
    row = lax.broadcasted_iota(jnp.int32, (8, span), 0)
    bias = jnp.where((place >= length) & (row == 0), masked_value, 0.0)
    padded = jnp.concatenate(
        [key_t.astype(f32), bias, jnp.zeros((HEAD_DIM - 8, span), f32)], axis=0
    )
    return jnp.transpose(padded).astype(bf16)


def scaled_queries(query_t):
    span = query_t.shape[1]
    row = lax.broadcasted_iota(jnp.int32, (HEAD_DIM, span), 0)
    ones = jnp.where(row == 0, 1.0, 0.0)
    return jnp.concatenate([query_t.astype(f32) * score_scale, ones], axis=0).astype(bf16)


def causal(scores):
    key = lax.broadcasted_iota(jnp.int32, scores.shape, 0)
    query = lax.broadcasted_iota(jnp.int32, scores.shape, 1)
    return jnp.where(key <= query, scores, masked_value)


def attend_kernel(step, length_ref, qkv_ref, out_ref, total_ref, key_ref, query_ref, value_ref):
    span = qkv_ref.shape[0] * qkv_ref.shape[2]
    key_ref[...] = live_keys(head_rows(qkv_ref, HEAD_DIM, HEAD_DIM), length_ref[0])
    query_ref[...] = scaled_queries(head_rows(qkv_ref, 0, HEAD_DIM))
    value_ref[...] = head_rows(qkv_ref, 2 * HEAD_DIM, HEAD_DIM)

    def query_block(q, carry):
        here = pl.ds(pl.multiple_of(q * step, step), step)
        query = query_ref[:, here]

        def absorb(k, state, masked):
            top, total, out = state
            there = pl.ds(pl.multiple_of(k * step, step), step)
            scores = jnp.dot(key_ref[there, :], query, preferred_element_type=f32)
            if masked:
                scores = causal(scores)
            new_top = jnp.maximum(top, jnp.max(scores, axis=0, keepdims=True))
            shrink = jnp.exp(top - new_top)
            weights = jnp.exp(scores - new_top)
            total = total * shrink + jnp.sum(weights, axis=0, keepdims=True)
            out = out * shrink + jnp.dot(
                value_ref[:, there], weights.astype(bf16), preferred_element_type=f32
            )
            return new_top, total, out

        state = (
            jnp.full((1, step), masked_value, f32),
            jnp.zeros((1, step), f32),
            jnp.zeros((HEAD_DIM, step), f32),
        )
        state = absorb(q, state, True)
        top, total, out = lax.fori_loop(0, q, lambda k, s: absorb(k, s, False), state)
        out_ref[:, here] = out / total
        total_ref[:, here] = top + jnp.log(total)
        return carry

    lax.fori_loop(0, span // step, query_block, 0)


def attend(qkv, length):
    blocks, _, rows = qkv.shape
    span = blocks * rows
    step = min(512, span)
    return pl.pallas_call(
        functools.partial(attend_kernel, step),
        out_shape=(
            jax.ShapeDtypeStruct((HEAD_DIM, span), f32),
            jax.ShapeDtypeStruct((1, span), f32),
        ),
        in_specs=[
            pl.BlockSpec(memory_space=pltpu.SMEM),
            pl.BlockSpec(memory_space=pltpu.VMEM),
        ],
        out_specs=(pl.BlockSpec(memory_space=pltpu.VMEM),) * 2,
        scratch_shapes=[
            pltpu.VMEM((span, 2 * HEAD_DIM), bf16),
            pltpu.VMEM((2 * HEAD_DIM, span), bf16),
            pltpu.VMEM((HEAD_DIM, span), bf16),
        ],
        compiler_params=pltpu.CompilerParams(vmem_limit_bytes=48 << 20),
    )(length, qkv)


def unrotate(grad_t, cosine, sine):
    half = HEAD_DIM // 2
    first, second = grad_t[:half], grad_t[half:]
    return jnp.concatenate(
        [first * cosine + second * sine, second * cosine - first * sine], axis=0
    )


def attend_back_kernel(
    step,
    length_ref,
    qkv_ref,
    out_ref,
    total_ref,
    upstream_ref,
    cosine_ref,
    sine_ref,
    grad_ref,
    key_ref,
    query_ref,
    value_ref,
    key_t_ref,
    query_sum,
    key_sum,
    value_sum,
    delta_ref,
    up_ref,
):
    blocks, _, rows = qkv_ref.shape
    span = blocks * rows
    key_t = head_rows(qkv_ref, HEAD_DIM, HEAD_DIM)
    key_ref[...] = live_keys(key_t, length_ref[0])
    key_t_ref[...] = key_t
    query_ref[...] = scaled_queries(head_rows(qkv_ref, 0, HEAD_DIM))
    value_t = head_rows(qkv_ref, 2 * HEAD_DIM, HEAD_DIM)
    value_ref[...] = jnp.transpose(value_t.astype(f32)).astype(bf16)
    upstream = head_rows(upstream_ref, 0, HEAD_DIM)
    up_ref[...] = upstream
    delta_ref[...] = jnp.sum(upstream.astype(f32) * out_ref[...], axis=0, keepdims=True)
    query_sum[...] = jnp.zeros_like(query_sum)

    def key_block(k, carry):
        there = pl.ds(pl.multiple_of(k * step, step), step)
        key, value, key_flat = key_ref[there, :], value_ref[there, :], key_t_ref[:, there]

        def meet(q, sums, masked):
            key_add, value_add = sums
            here = pl.ds(pl.multiple_of(q * step, step), step)
            query, up = query_ref[:, here], up_ref[:, here]
            scores = jnp.dot(key, query, preferred_element_type=f32)
            if masked:
                scores = causal(scores)
            probs = jnp.exp(scores - total_ref[:, here])
            d_probs = jnp.dot(value, up, preferred_element_type=f32)
            d_scores = (probs * (d_probs - delta_ref[:, here])).astype(bf16)
            query_sum[:, here] += jnp.dot(key_flat, d_scores, preferred_element_type=f32)
            contract = (((1,), (1,)), ((), ()))
            key_add = key_add + lax.dot_general(
                query[:HEAD_DIM], d_scores, contract, preferred_element_type=f32
            )
            value_add = value_add + lax.dot_general(
                up, probs.astype(bf16), contract, preferred_element_type=f32
            )
            return key_add, value_add

        zero = jnp.zeros((HEAD_DIM, step), f32)
        sums = meet(k, (zero, zero), True)
        key_add, value_add = lax.fori_loop(
            k + 1, span // step, lambda q, s: meet(q, s, False), sums
        )
        key_sum[:, there] = key_add
        value_sum[:, there] = value_add
        return carry

    lax.fori_loop(0, span // step, key_block, 0)
    cosine, sine = cosine_ref[...], sine_ref[...]
    d_query = unrotate(query_sum[...] * score_scale, cosine, sine).astype(bf16)
    d_key = unrotate(key_sum[...], cosine, sine).astype(bf16)
    d_value = value_sum[...].astype(bf16)
    for block in range(blocks):
        at = slice(block * rows, (block + 1) * rows)
        grad_ref[block, :HEAD_DIM, :] = d_query[:, at]
        grad_ref[block, HEAD_DIM : 2 * HEAD_DIM, :] = d_key[:, at]
        grad_ref[block, 2 * HEAD_DIM :, :] = d_value[:, at]


def attend_back(qkv, length, out, total, upstream, cosine, sine):
    blocks, _, rows = qkv.shape
    span = blocks * rows
    step = min(512, span)
    return pl.pallas_call(
        functools.partial(attend_back_kernel, step),
        out_shape=jax.ShapeDtypeStruct(qkv.shape, bf16),
        in_specs=[pl.BlockSpec(memory_space=pltpu.SMEM)]
        + [pl.BlockSpec(memory_space=pltpu.VMEM)] * 6,
        out_specs=pl.BlockSpec(memory_space=pltpu.VMEM),
        scratch_shapes=[
            pltpu.VMEM((span, 2 * HEAD_DIM), bf16),
            pltpu.VMEM((2 * HEAD_DIM, span), bf16),
            pltpu.VMEM((span, HEAD_DIM), bf16),
            pltpu.VMEM((HEAD_DIM, span), bf16),
            pltpu.VMEM((HEAD_DIM, span), f32),
            pltpu.VMEM((HEAD_DIM, span), f32),
            pltpu.VMEM((HEAD_DIM, span), f32),
            pltpu.VMEM((1, span), f32),
            pltpu.VMEM((HEAD_DIM, span), bf16),
        ],
        compiler_params=pltpu.CompilerParams(vmem_limit_bytes=56 << 20),
    )(length, qkv, out, total, upstream, cosine, sine)


def local(
    tokens,
    lengths,
    routes,
    norm1_gain,
    query_weight,
    key_weight,
    value_weight,
    output_weight,
    norm2_gain,
    router_weight,
    expert_gate,
    expert_up,
    expert_down,
    shared_gate,
    shared_up,
    shared_down,
    cotangent,
):
    dp_size, ctx_size, expert_size = (lax.axis_size(a) for a in ("dp", "ctx", "expert"))
    plane_size, slot_size = dp_size * ctx_size, ctx_size * expert_size
    rows, width = tokens.shape[1:]
    heads = width // HEAD_DIM
    own = EXPERTS // expert_size
    hidden_width = expert_gate.shape[2]
    part = hidden_width // plane_size
    plane = lax.axis_index("dp") * ctx_size + lax.axis_index("ctx")
    first_row = (lax.axis_index("ctx") * expert_size + lax.axis_index("expert")) * rows
    positions = first_row + jnp.arange(rows, dtype=jnp.int32)
    length = lengths[0]
    live_rows = positions < length
    valid = live_rows.astype(f32)[:, None]
    inputs = tokens[0].astype(f32)
    upstream = cotangent[0].astype(f32)
    d_branch = valid * upstream
    d_branch_low = d_branch.astype(bf16)

    route_ids = routes[0]
    expert_range = jnp.arange(EXPERTS, dtype=jnp.int32)
    picked = (route_ids[:, :, None] == expert_range).astype(f32)
    expert_hits = (
        ((route_ids[:, :, None] == expert_range) & live_rows[:, None, None])
        .astype(jnp.int32)
        .reshape(rows * TOP, EXPERTS)
    )
    places = jnp.sum((jnp.cumsum(expert_hits, axis=0) - 1) * expert_hits, axis=-1)
    live_pairs = jnp.broadcast_to(live_rows[:, None], (rows, TOP)).reshape(-1)
    slot_ids = jnp.where(live_pairs, route_ids.reshape(-1) * PLACES + places, -1)
    dispatch = (
        slot_ids[:, None] == jnp.arange(EXPERTS * PLACES, dtype=jnp.int32)[None, :]
    ).reshape(rows, TOP, EXPERTS * PLACES)
    either = jnp.any(dispatch, axis=1).astype(bf16)

    def to_experts(flat):
        return lax.all_to_all(
            flat.reshape((expert_size, -1) + flat.shape[1:]), "expert", 0, 0
        )

    def spread(flat):
        placed = jnp.einsum("ts,td->sd", either, flat, preferred_element_type=f32).astype(bf16)
        mine = to_experts(placed).reshape(-1, width)
        return lax.all_gather(jnp.concatenate([mine, flat], axis=0), PLANE, axis=0)

    up_all = spread(d_branch_low)

    scale_one = rms_scale(inputs)
    normal_one = inputs * scale_one
    normed_low = (normal_one * norm1_gain).astype(bf16)
    normed_all = lax.all_gather(normed_low, SLOT, axis=0, tiled=True)
    cosine, sine = rope_tables(positions)

    def project(weight):
        lin = jnp.dot(normed_low, weight, preferred_element_type=f32)
        return jnp.transpose(lin).reshape(heads, HEAD_DIM, rows)

    def rotated(lin_t):
        half = HEAD_DIM // 2
        first, second = lin_t[:, :half], lin_t[:, half:]
        return jnp.concatenate(
            [first * cosine - second * sine, second * cosine + first * sine], axis=1
        )

    query = rotated(project(query_weight)).astype(bf16)
    key = rotated(project(key_weight)).astype(bf16)
    value = project(value_weight).astype(bf16)

    def to_heads(blocks):
        spare = jnp.zeros((slot_size - heads,) + blocks.shape[1:], blocks.dtype)
        return lax.all_to_all(jnp.concatenate([blocks, spare], axis=0), SLOT, 0, 0)

    def from_heads(blocks):
        return lax.all_to_all(blocks, SLOT, 0, 0)[:heads]

    def by_block(flat_t):
        return jnp.transpose(flat_t.reshape(-1, slot_size, rows), (1, 0, 2))

    qkv = to_heads(jnp.concatenate([query, key, value], axis=1))
    out_t, log_total = attend(qkv, lengths)
    attended = jnp.transpose(
        from_heads(by_block(out_t.astype(bf16))).reshape(width, rows)
    )
    attn_out = jnp.dot(attended, output_weight, preferred_element_type=f32)
    hidden_in = inputs + valid * attn_out

    scale_two = rms_scale(hidden_in)
    normal_two = hidden_in * scale_two
    normed_two_low = (normal_two * norm2_gain).astype(bf16)
    logits = jnp.dot(normed_two_low, router_weight, preferred_element_type=f32)
    chosen = jnp.sum(picked * logits[:, None, :], axis=-1)
    shifted = jnp.exp(chosen - jnp.max(chosen, axis=-1, keepdims=True))
    gate_weights = shifted / jnp.sum(shifted, axis=-1, keepdims=True)

    in_all = spread(normed_two_low)
    gate_rows = jnp.sum(jnp.where(dispatch, gate_weights[:, :, None], 0.0), axis=(0, 1))
    gate_all = lax.all_gather(to_experts(gate_rows).reshape(-1), PLANE, axis=0)
    placed_rows = EXPERTS * PLACES

    def by_expert(both):
        cut = both[:, :placed_rows].reshape((plane_size * expert_size, own, PLACES) + both.shape[2:])
        return jnp.swapaxes(cut, 0, 1).reshape((own, -1) + both.shape[2:])

    def by_source(flat):
        cut = flat.reshape((own, plane_size * expert_size, PLACES) + flat.shape[2:])
        return jnp.swapaxes(cut, 0, 1).reshape((plane_size, placed_rows) + flat.shape[2:])

    def column(weight):
        return lax.dynamic_slice_in_dim(weight, plane * part, part, weight.ndim - 1)

    def row(weight):
        return lax.dynamic_slice_in_dim(weight, plane * part, part, weight.ndim - 2)

    def branch(rows_in, up, gate_w, up_w, down_w, weight):
        def dot(spec, a, b):
            return jnp.einsum(spec, a, b, preferred_element_type=f32)

        gate_lin, up_lin = dot("erd,edf->erf", rows_in, gate_w), dot("erd,edf->erf", rows_in, up_w)
        sigmoid = 1.0 / (1.0 + jnp.exp(-gate_lin))
        silu = gate_lin * sigmoid
        hidden = (silu * up_lin).astype(bf16)
        result = dot("erf,efd->erd", hidden, down_w)
        d_out = (weight * up.astype(f32)).astype(bf16)
        d_hidden = dot("erd,efd->erf", d_out, down_w)
        d_gate = (d_hidden * up_lin * (sigmoid + silu * (1.0 - sigmoid))).astype(bf16)
        d_up = (d_hidden * silu).astype(bf16)
        d_in = dot("erf,edf->erd", d_gate, gate_w) + dot("erf,edf->erd", d_up, up_w)
        grads = (
            dot("erd,erf->edf", rows_in, d_gate),
            dot("erd,erf->edf", rows_in, d_up),
            dot("erf,erd->efd", hidden, d_out),
        )
        return result, d_in, grads

    gate_factor = by_expert(gate_all)[:, :, None]
    up_rows = by_expert(up_all)
    result, d_rows, expert_grads = branch(
        by_expert(in_all), up_rows, column(expert_gate), column(expert_up), row(expert_down),
        gate_factor,
    )
    d_gate_part = by_source(jnp.sum(result * up_rows.astype(f32), axis=-1))
    shared_result, shared_d, shared_grads = branch(
        in_all[:, placed_rows:].reshape(1, -1, width),
        up_all[:, placed_rows:].reshape(1, -1, width),
        column(shared_gate)[None],
        column(shared_up)[None],
        row(shared_down)[None],
        1.0,
    )

    def home(expert_part, shared_part):
        both = jnp.concatenate(
            [by_source(expert_part), shared_part.reshape(plane_size, rows, width)], axis=1
        ).astype(bf16)
        both = lax.psum_scatter(both, "dp", scatter_dimension=0, tiled=True)
        both = lax.psum_scatter(both, "ctx", scatter_dimension=0, tiled=True)[0]
        back = to_experts(both[:placed_rows]).reshape(placed_rows, width)
        spread_rows = jnp.dot(either, back, preferred_element_type=f32)
        return spread_rows + both[placed_rows:].astype(f32)

    d_gate_rows = lax.psum_scatter(d_gate_part, PLANE, scatter_dimension=0, tiled=True)[0]
    d_gate_rows = to_experts(d_gate_rows).reshape(-1)
    d_gates = jnp.sum(jnp.where(dispatch, d_gate_rows, 0.0), axis=-1)
    d_chosen = gate_weights * (
        d_gates - jnp.sum(gate_weights * d_gates, axis=-1, keepdims=True)
    )
    d_logits = jnp.sum(picked * d_chosen[:, :, None], axis=1).astype(bf16)
    d_router = jnp.einsum("td,te->de", normed_two_low, d_logits, preferred_element_type=f32)
    d_normed_two = home(d_rows, shared_d) + jnp.einsum(
        "te,de->td", d_logits, router_weight, preferred_element_type=f32
    )
    output_rows = hidden_in + valid * home(result * gate_factor, shared_result)
    output_rows = output_rows.astype(bf16)[None]
    d_gain_two = jnp.sum(d_normed_two * normal_two, axis=0)
    d_hidden_in = upstream + rms_back(normal_two, scale_two, norm2_gain, d_normed_two)

    d_attn_low = (valid * d_hidden_in).astype(bf16)
    d_output_weight = jnp.einsum("td,te->de", attended, d_attn_low, preferred_element_type=f32)
    d_attended = jnp.einsum("te,de->dt", d_attn_low, output_weight, preferred_element_type=f32)
    d_attended = to_heads(d_attended.astype(bf16).reshape(heads, HEAD_DIM, rows))
    all_cosine, all_sine = rope_tables(jnp.arange(slot_size * rows, dtype=jnp.int32))
    d_qkv = attend_back(qkv, lengths, out_t, log_total, d_attended, all_cosine, all_sine)
    head_grad = jnp.einsum(
        "bet,btd->ed", d_qkv, normed_all.reshape(slot_size, rows, width), preferred_element_type=f32
    )
    d_own = jnp.swapaxes(from_heads(d_qkv).reshape(heads, 3, HEAD_DIM, rows), 0, 1)
    d_own = d_own.reshape(3, width, rows)
    d_normed = jnp.zeros((width, rows), f32)
    for weight, grad in zip((query_weight, key_weight, value_weight), d_own):
        d_normed = d_normed + jnp.dot(weight, grad, preferred_element_type=f32)
    d_normed = jnp.transpose(d_normed)
    d_gain_one = jnp.sum(d_normed * normal_one, axis=0)
    input_grad = d_hidden_in + rms_back(normal_one, scale_one, norm1_gain, d_normed)
    input_grad = input_grad.astype(bf16)[None]

    shard = width // (dp_size * slot_size)
    head_grad = jnp.transpose(head_grad).reshape(-1, 3 * HEAD_DIM)
    head_grad = lax.psum_scatter(head_grad, "dp", scatter_dimension=0, tiled=True)
    head_grad = lax.all_to_all(head_grad.reshape(slot_size, shard, 3 * HEAD_DIM), SLOT, 0, 0)
    head_grad = jnp.transpose(
        head_grad[:heads].reshape(heads, shard, 3, HEAD_DIM), (2, 1, 0, 3)
    ).reshape(3, shard, width)

    def scatter(grad):
        for axis in ("dp", "ctx", "expert"):
            grad = lax.psum_scatter(grad, axis, scatter_dimension=0, tiled=True)
        return grad

    output_grad = scatter(d_output_weight.astype(bf16)).astype(f32)
    small = lax.psum(
        jnp.concatenate([d_router, d_gain_one[:, None], d_gain_two[:, None]], axis=1),
        ("dp", "ctx", "expert"),
    )
    linear = plane * expert_size + lax.axis_index("expert")
    small = lax.dynamic_slice_in_dim(small, linear * shard, shard, 0)

    def shared_columns(grad):
        grad = grad[0].reshape(plane_size, expert_size, shard, part).astype(bf16)
        grad = lax.psum_scatter(grad, "expert", scatter_dimension=1, tiled=True)[:, 0]
        grad = lax.all_to_all(grad, PLANE, 0, 0)
        return jnp.swapaxes(grad, 0, 1).reshape(shard, hidden_width).astype(f32)

    shared_down_grad = lax.psum_scatter(
        shared_grads[2][0].astype(bf16), "expert", scatter_dimension=0, tiled=True
    ).astype(f32)
    return (
        output_rows,
        input_grad,
        small[:, EXPERTS],
        head_grad[0],
        head_grad[1],
        head_grad[2],
        output_grad,
        small[:, EXPERTS + 1],
        small[:, :EXPERTS],
        expert_grads[0],
        expert_grads[1],
        expert_grads[2],
        shared_columns(shared_grads[0]),
        shared_columns(shared_grads[1]),
        shared_down_grad,
    )


def solution(mesh):
    tokens = P("dp", ("ctx", "expert"), None)
    whole = P()
    experts = P("expert", None, None)
    everywhere = ("dp", "ctx", "expert")
    return jax.shard_map(
        local,
        mesh=mesh,
        in_specs=(tokens, P("dp"), tokens)
        + (whole,) * 7
        + (experts,) * 3
        + (whole,) * 3
        + (tokens,),
        out_specs=(tokens, tokens, P(everywhere))
        + (P(everywhere, None),) * 4
        + (P(everywhere), P(everywhere, None))
        + (P("expert", None, PLANE),) * 2
        + (P("expert", PLANE, None),)
        + (P(everywhere, None),) * 3,
        check_vma=False,
    )
```

time: 1720 us -> 699 us (0.41)
  waiting for transfers between devices: 1260 us -> 247 us
  matrix products: 201 us -> 96.8 us
  blocking collectives: 75.9 us -> 164 us
  other arithmetic: 64 us -> 43.2 us
  Pallas kernels: 0 us -> 18.8 us
    reduce_scatter x10 -> x7, waiting for transfers between devices: 987 us -> 23.6 us  [the longest x2 13.7 us: home(): both = lax.psum_scatter(both, 'dp', scatter_dimension=0, tiled=True)]
    ppermute x16 -> x0, waiting for transfers between devices: 212 us -> none  [shifted_2(): lax.ppermute(array, axis, [(i, (i + by) % count) for i in range(count)])]
    unnamed x15 -> x14, waiting for transfers between devices: 0.23 us -> 136 us
    dot_general x58 -> x34, matrix products: 201 us -> 96.1 us  [the longest x18 70.6 us: dot(): return jnp.einsum(spec, a, b, preferred_element_type=f32)]
    all_to_all x0 -> x4, blocking collectives: none -> 76.2 us  [the longest x2 38 us: to_experts(): lax.all_to_all(flat.reshape((expert_size, -1) + flat.shape[1:]), 'expert'...]
    all_to_all x4 -> x9, waiting for transfers between devices: 6.71 us -> 58.1 us  [the longest x4 36.6 us: to_experts(): lax.all_to_all(flat.reshape((expert_size, -1) + flat.shape[1:]), 'expert'...]
    psum x0 -> x1, blocking collectives: none -> 41.6 us  [local(): lax.psum(jnp.concatenate([d_router, d_gain_one[:, None], d_gain_two[:, No...]
    slice x1 -> x15, local copies, waits for them, and re-layouts: 0.18 us -> 22.9 us  [the longest x2 6.05 us: by_expert(): both[:, :placed_rows]]
  transfers between devices with their start and end apart: 34 -> 21, of which waited for: 30 -> 12; matrix products, arithmetic and copies ran while one was open for 12% -> 21% of each run, Pallas kernels for 0% -> 3%
where the time goes in v1:
time: 699 us; the launch traced here: 691 us
  waiting for transfers between devices  247 us (35%)
  blocking collectives  164 us (23%)
  matrix products  96.8 us (14%)
  local copies, waits for them, and re-layouts  66.4 us (9%)
  other arithmetic  43.2 us (6%)
  starting transfers between devices  37.8 us (5%)
  Pallas kernels  18.8 us (3%)
  between operations  17.2 us (2%)
    unnamed x14, waiting for transfers between devices  136 us
    dot_general x18, matrix products, dot(): return jnp.einsum(spec, a, b, preferred_element_type=f32)  70.6 us
    psum x1, blocking collectives, local(): lax.psum(jnp.concatenate([d_router, d_gain_one[:, None], d_gain_two[:, No...  41.6 us
    all_to_all x2, blocking collectives, to_experts(): lax.all_to_all(flat.reshape((expert_size, -1) + flat.shape[1:]), 'expert'...  38 us
    all_to_all x4, waiting for transfers between devices, to_experts(): lax.all_to_all(flat.reshape((expert_size, -1) + flat.shape[1:]), 'expert'...  36.6 us
    all_gather x2, waiting for transfers between devices, spread(): return lax.all_gather(jnp.concatenate([mine, flat], axis=0), PLANE, axis=0)  28.7 us
    unnamed x1, blocking collectives  26.5 us
    all_to_all x1, blocking collectives, to_heads(): return lax.all_to_all(jnp.concatenate([blocks, spare], axis=0), SLOT, 0, 0)  25.8 us
  transfers between devices with their start and end apart: 21, of which 12 were waited for; matrix products, arithmetic and copies ran while one was open for 21% of the time, Pallas kernels for 3%

profile of v1, /device:TPU:0, one launch (start us, length us, event | category | flops | bytes accessed | tf_op | source)
XLA Modules:
  0.0 691.1 jit_solution(678342377848669119)
XLA Ops:
  13.3 22.0 %all_to_all.73 = bf16[4,96,768]{2,1,0:T(8,128)(2,1)S(1)} all-to-all(bf16[4,96,768]{2,1,0:T(8,128)(2,1)S(1)} %bitcast.241), channel_id=1, replica_groups=mesh['dp'=2,'ctx'=4,'expert'=4] {'expert'}, dimensions={0} | all-to-all | bytes 1179648 | tf_op jit(solution)/shard_map/all_to_all | solution.py:301
  54.0 25.8 %all_to_all.74.qkv_ref = bf16[16,192,128]{2,1,0:T(8,128)(2,1)S(1)} all-to-all(bf16[16,192,128]{2,1,0:T(8,128)(2,1)S(1)} %concatenate.32), channel_id=1, replica_groups=mesh['dp'=2,'ctx'=4,'expert'=4] {'ctx','expert'}, dimensions={0} | all-to-all | bytes 1572864 | tf_op jit(solution)/shard_map/all_to_all | solution.py:335
  79.8 6.4 shard_map.280
  86.3 12.4 %all_to_all.75 = bf16[16,64,128]{2,1,0:T(8,128)(2,1)S(1)} all-to-all(bf16[16,64,128]{2,1,0:T(8,128)(2,1)S(1)} %bitcast_bitcast_fusion), channel_id=1, replica_groups=mesh['dp'=2,'ctx'=4,'expert'=4] {'ctx','expert'}, dimensions={0} | all-to-all | bytes 524288 | tf_op jit(solution)/shard_map/all_to_all | solution.py:338
  99.8 16.0 %all_to_all.76 = bf16[4,96,768]{2,1,0:T(8,128)(2,1)S(1)} all-to-all(bf16[4,96,768]{2,1,0:T(8,128)(2,1)S(1)} %bitcast.242), channel_id=1, replica_groups=mesh['dp'=2,'ctx'=4,'expert'=4] {'expert'}, dimensions={0} | all-to-all | bytes 1179648 | tf_op jit(solution)/shard_map/all_to_all | solution.py:301
  132.8 28.7 %all-gather.9.cloned.1.call-done = bf16[4096,768]{1,0:T(8,128)(2,1)} async-done(((bf16[512,768]{1,0:T(8,128)(2,1)}), bf16[4096,768]{1,0:T(8,128)(2,1)}) %all-gather.9.cloned.1.call-update) | async-done | bytes 6291472 | tf_op jit(solution)/shard_map/all_gather | solution.py:308
  175.9 6.0 multiply_convert_fusion.3
  182.0 7.1 %fusion.1 = (f32[4,768]{1,0:T(4,128)S(1)}, f32[4,768,768]{2,1,0:T(8,128)}) fusion(f32[4,32,24,768]{3,2,1,0:T(8,128)S(1)} %bitcast.211, bf16[4,768,256]{2,1,0:T(8,128)(2,1)S(1)} %get-tuple-element.52, bf16[4,2048,768]{2,1,0:T(8,128)(2,1)} %param.29, s32[]{:T(128)S(6)} %select_n.28), kind=kOutput, calls=%fused_computation.4 | convolution fusion | flops 1212675072 | bytes 22032388 | tf_op jit(solution)/shard_map/erf,efd->erd/dot_general | solution.py:380
  192.2 26.5 %all-reduce.4 = f32[8,384]{1,0:T(8,128)} all-reduce(f32[8,384]{1,0:T(8,128)S(1)} %reshape.518), channel_id=8, replica_groups=mesh['dp'=2,'ctx'=4,'expert'=4] {'dp','ctx'}, use_global_device_ids=true, to_apply=%region_15.16.clone | all-reduce | flops 3072 | bytes 24576
  244.0 19.8 %all-gather.2 = f32[8,1,384]{2,1,0:T(1,128)S(1)} all-gather(f32[1,1,384]{2,1,0:T(1,128)S(1)} %reshape.535), channel_id=1, replica_groups=mesh['dp'=2,'ctx'=4,'expert'=4] {'dp','ctx'}, dimensions={0}, use_global_device_ids=true | all-gather | bytes 13824 | tf_op jit(solution)/shard_map/all_gather | solution.py:361
  264.1 9.3 %fusion = (bf16[4,768,768]{2,1,0:T(8,128)(2,1)}, bf16[4,768,768]{2,1,0:T(8,128)(2,1)S(1)}) fusion(f32[4,32,24,768]{3,2,1,0:T(8,128)} %copy.136, f32[4,768]{1,0:T(4,128)S(1)} %mul.379, f32[4,768,768]{2,1,0:T(8,128)} %get-tuple-element.55), kind=kLoop, calls=%fused_computation.3 | loop fusion | flops 9437184 | bytes 28323840 | tf_op jit(solution)/shard_map/convert_element_type | solution.py:387
  282.0 6.0 multiply_convert_fusion.1
  298.2 13.7 %reduce-scatter.12.cloned.1.call-done = bf16[4,512,768]{2,1,0:T(8,128)(2,1)} async-done(((bf16[8,512,768]{2,1,0:T(8,128)(2,1)}), bf16[4,512,768]{2,1,0:T(8,128)(2,1)}) %reduce-scatter.12.cloned.1.call-update) | async-done | bytes 3145744 | tf_op jit(solution)/shard_map/reduce_scatter | solution.py:419
  321.4 135.7 %all-reduce.14.cloned.1.call-done = (bf16[4,512,768]{2,1,0:T(8,128)(2,1)}, bf16[4,512,768]{2,1,0:T(8,128)(2,1)}) async-done(((bf16[4,512,768]{2,1,0:T(8,128)(2,1)}, bf16[4,512,768]{2,1,0:T(8,128)(2,1)}), (bf16[4,512,768]{2,1,0:T(8,128)(2,1)}, bf16[4,512,768]{2,1,0:T(8,128)(2,1)})) %all-reduce.14.cloned.1.call-update) | async-done | bytes 6291472
  468.9 24.1 %all-to-all-done.6 = bf16[4,96,768]{2,1,0:T(8,128)(2,1)} async-done(((bf16[4,96,768]{2,1,0:T(8,128)(2,1)}), bf16[4,96,768]{2,1,0:T(8,128)(2,1)}, u32[]{:S(2)}, u32[]{:S(2)}) %all-to-all-start.6) | async-done | bytes 589856 | tf_op jit(solution)/shard_map/all_to_all | solution.py:301
  506.9 14.7 %all-to-all-done.8.upstream_ref = bf16[16,64,128]{2,1,0:T(8,128)(2,1)S(1)} async-done(((bf16[16,64,128]{2,1,0:T(8,128)(2,1)}), bf16[16,64,128]{2,1,0:T(8,128)(2,1)S(1)}, u32[]{:S(2)}, u32[]{:S(2)}) %all-to-all-start.8) | async-done | bytes 262176 | tf_op jit(solution)/shard_map/all_to_all | solution.py:335
  522.3 12.3 %shard_map.281 = bf16[16,192,128]{2,1,0:T(8,128)(2,1)} custom-call(s32[1]{0:T(128)} %copy.174.length_ref, bf16[16,192,128]{2,1,0:T(8,128)(2,1)} %copy-done.2, f32[64,2048]{1,0:T(8,128)} %copy-done.3, f32[1,2048]{1,0:T(1,128)} %copy-done.4, bf16[16,64,128]{2,1,0:T(8,128)(2,1)} %copy-done.31, f32[32,2048]{1,0:T(8,128)} %get-tuple-element.47.cosine_ref, ...), custom_call_target="tpu_custom_call" | custom-call | tf_op jit(solution)/shard_map/pallas_call | solution.py:226
  564.5 5.7 fusion.85
  570.3 8.3 %all-to-all-done.4 = bf16[4,96,768]{2,1,0:T(8,128)(2,1)} async-done(((bf16[4,96,768]{2,1,0:T(8,128)(2,1)}), bf16[4,96,768]{2,1,0:T(8,128)(2,1)}, u32[]{:S(2)}, u32[]{:S(2)}) %all-to-all-start.4) | async-done | bytes 589856 | tf_op jit(solution)/shard_map/all_to_all | solution.py:301
  582.9 5.5 fusion.87
  588.5 5.8 fusion.86
  604.5 5.3 all-to-all-start.10
  617.6 41.6 %psum.7 = f32[768,18]{0,1:T(8,128)} all-reduce(f32[768,18]{0,1:T(8,128)} %pad_maximum_fusion.4), channel_id=1, replica_groups=mesh['dp'=2,'ctx'=4,'expert'=4] {'dp','ctx','expert'}, use_global_device_ids=true, to_apply=%region_23.24 | all-reduce | flops 13824 | bytes 110592 | tf_op jit(solution)/shard_map/psum | solution.py:474
  672.5 9.9 %reduce-scatter.20.cloned.1.call-done = bf16[24,768]{1,0:T(8,128)(2,1)} async-done(((bf16[96,768]{1,0:T(8,128)(2,1)}), bf16[24,768]{1,0:T(8,128)(2,1)}) %reduce-scatter.20.cloned.1.call-update) | async-done | bytes 36880 | tf_op jit(solution)/shard_map/reduce_scatter | solution.py:470
  (313 shorter events, 205.3 us)
Async XLA Ops:
  8.0 217.3 %copy-start = (bf16[2048,768]{1,0:T(8,128)(2,1)S(1)}, bf16[2048,768]{1,0:T(8,128)(2,1)}, u32[]{:S(2)}) copy-start(bf16[2048,768]{1,0:T(8,128)(2,1)} %param.32) | copy-start | bytes 9437188
  8.1 113.3 %all-gather.11.cloned.1.call-start = ((), (), s32[]{:S(2)}) async-start(), calls=%async_computation.29 | async-start | bytes 7077888 | tf_op jit(solution)/shard_map/all_gather | solution.py:308
  36.3 125.2 %all-gather.9.cloned.1.call-start = ((), (), s32[]{:S(2)}) async-start(), calls=%async_computation.28 | async-start | bytes 7077888 | tf_op jit(solution)/shard_map/all_gather | solution.py:308
  220.7 10.1 %all-to-all-start.7 = ((f32[4,1,96]{2,1,0:T(1,128)}), f32[4,1,96]{2,1,0:T(1,128)S(1)}, u32[]{:S(2)}, u32[]{:S(2)}) async-start(f32[4,1,96]{2,1,0:T(1,128)} %bitcast.47), calls=%async_computation.9 | async-start | bytes 4096 | tf_op jit(solution)/shard_map/all_to_all | solution.py:301
  234.2 9.1 %all-to-all-start.3 = ((f32[4,1,96]{2,1,0:T(1,128)}), f32[4,1,96]{2,1,0:T(1,128)S(1)}, u32[]{:S(2)}, u32[]{:S(2)}) async-start(f32[4,1,96]{2,1,0:T(1,128)} %all_to_all.48), calls=%async_computation.3 | async-start | bytes 4096 | tf_op jit(solution)/shard_map/all_to_all | solution.py:301
  237.8 60.4 %reduce-scatter.10.cloned.1.call-start = ((), (), s32[]{:S(2)}) async-start(), calls=%async_computation.20 | async-start | bytes 9437184 | tf_op jit(solution)/shard_map/reduce_scatter | solution.py:419
  277.9 34.0 %reduce-scatter.12.cloned.1.call-start = ((), (), s32[]{:S(2)}) async-start(), calls=%async_computation.21 | async-start | bytes 9437184 | tf_op jit(solution)/shard_map/reduce_scatter | solution.py:419
  298.1 159.0 %all-reduce.14.cloned.1.call-start = ((), (), s32[]{:S(2)}) async-start(), calls=%async_computation.31 | async-start | bytes 12582912
  311.9 222.7 %all-gather.7.cloned.1.call-start = ((), (), s32[]{:S(2)}) async-start(), calls=%async_computation.22 | async-start | bytes 3342336 | tf_op jit(solution)/shard_map/all_gather | solution.py:315
  312.5 226.6 %all-reduce.12.cloned.1.call-start = ((), (), s32[]{:S(2)}) async-start(), calls=%async_computation.30 | async-start | bytes 1572864
  317.8 146.5 %copy-start.12 = (bf16[8,128,768]{2,1,0:T(8,128)(2,1)S(1)}, bf16[8,128,768]{2,1,0:T(8,128)(2,1)}, u32[]{:S(2)}) copy-start(bf16[8,128,768]{2,1,0:T(8,128)(2,1)} %slice.111) | copy-start | bytes 4718596
  320.7 146.0 %copy-start.44 = (f32[128]{0:T(128)S(1)}, f32[128]{0:T(128)}, u32[]{:S(2)}) copy-start(f32[128]{0:T(128)} %copy-done.43) | copy-start | bytes 1540
  459.6 33.3 %all-to-all-start.6 = ((bf16[4,96,768]{2,1,0:T(8,128)(2,1)}), bf16[4,96,768]{2,1,0:T(8,128)(2,1)}, u32[]{:S(2)}, u32[]{:S(2)}) async-start(bf16[4,96,768]{2,1,0:T(8,128)(2,1)} %bitcast.239), calls=%async_computation.8 | async-start | bytes 1179648 | tf_op jit(solution)/shard_map/all_to_all | solution.py:301
  464.2 130.0 %reduce-scatter.22.cloned.1.call-start = ((), (), s32[]{:S(2)}) async-start(), calls=%async_computation.27 | async-start | bytes 491520 | tf_op jit(solution)/shard_map/reduce_scatter | solution.py:487
  500.3 21.3 %all-to-all-start.8 = ((bf16[16,64,128]{2,1,0:T(8,128)(2,1)}), bf16[16,64,128]{2,1,0:T(8,128)(2,1)S(1)}, u32[]{:S(2)}, u32[]{:S(2)}) async-start(bf16[16,64,128]{2,1,0:T(8,128)(2,1)} %concatenate.37), calls=%async_computation.10 | async-start | bytes 524288 | tf_op jit(solution)/shard_map/all_to_all | solution.py:335
  504.1 96.8 %reduce-scatter.14.cloned.1.call-start = ((), (), s32[]{:S(2)}) async-start(), calls=%async_computation.23 | async-start | bytes 884736 | tf_op jit(solution)/shard_map/reduce_scatter | solution.py:462
  541.3 8.3 %all-to-all-start.11 = ((bf16[8,24,256]{2,1,0:T(8,128)(2,1)}), bf16[8,24,256]{2,1,0:T(8,128)(2,1)S(1)}, u32[]{:S(2)}, u32[]{:S(2)}) async-start(bf16[8,24,256]{2,1,0:T(8,128)(2,1)} %dynamic-slice_bitcast_fusion.3), calls=%async_computation.17 | async-start | bytes 196608 | tf_op jit(solution)/shard_map/all_to_all | solution.py:484
  549.6 8.3 %all-to-all-start.12 = ((bf16[8,24,256]{2,1,0:T(8,128)(2,1)}), bf16[8,24,256]{2,1,0:T(8,128)(2,1)S(1)}, u32[]{:S(2)}, u32[]{:S(2)}) async-start(bf16[8,24,256]{2,1,0:T(8,128)(2,1)} %dynamic-slice_bitcast_fusion.2), calls=%async_computation.18 | async-start | bytes 196608 | tf_op jit(solution)/shard_map/all_to_all | solution.py:484
  558.0 20.7 %all-to-all-start.4 = ((bf16[4,96,768]{2,1,0:T(8,128)(2,1)}), bf16[4,96,768]{2,1,0:T(8,128)(2,1)}, u32[]{:S(2)}, u32[]{:S(2)}) async-start(bf16[4,96,768]{2,1,0:T(8,128)(2,1)} %bitcast.26), calls=%async_computation.5 | async-start | bytes 1179648 | tf_op jit(solution)/shard_map/all_to_all | solution.py:301
  562.1 50.1 %reduce-scatter.16.cloned.1.call-start = ((), (), s32[]{:S(2)}) async-start(), calls=%async_computation.24 | async-start | bytes 1769472 | tf_op jit(solution)/shard_map/reduce_scatter | solution.py:470
  578.6 25.8 %all-to-all-start.9 = ((bf16[16,192,128]{2,1,0:T(8,128)(2,1)}), bf16[16,192,128]{2,1,0:T(8,128)(2,1)}, u32[]{:S(2)}, u32[]{:S(2)}) async-start(bf16[16,192,128]{2,1,0:T(8,128)(2,1)} %shard_map.281), calls=%async_computation.11 | async-start | bytes 1572864 | tf_op jit(solution)/shard_map/all_to_all | solution.py:338
  604.5 60.1 %all-to-all-start.10 = ((f32[16,24,192]{2,1,0:T(8,128)}), f32[16,24,192]{2,1,0:T(8,128)}, u32[]{:S(2)}, u32[]{:S(2)}) async-start(f32[16,24,192]{2,1,0:T(8,128)} %bitcast.60), calls=%async_computation.13 | async-start | bytes 786432 | tf_op jit(solution)/shard_map/all_to_all | solution.py:463
  609.7 53.4 %reduce-scatter.18.cloned.1.call-start = ((), (), s32[]{:S(2)}) async-start(), calls=%async_computation.25 | async-start | bytes 737280 | tf_op jit(solution)/shard_map/reduce_scatter | solution.py:470
  612.2 70.2 %reduce-scatter.20.cloned.1.call-start = ((), (), s32[]{:S(2)}) async-start(), calls=%async_computation.26 | async-start | bytes 184320 | tf_op jit(solution)/shard_map/reduce_scatter | solution.py:470
  (58 other events, 1224.8 us)
Sparse Core Ops, SparseCore 0:
  36.4 51.3 all-gather.10
  117.0 44.4 all-gather.8
  278.0 13.1 reduce-scatter.9
  298.2 13.5 reduce-scatter.11
  315.2 141.8 all-reduce.13
  459.4 61.4 all-reduce.11
  523.2 19.2 reduce-scatter.21
  544.8 6.2 reduce-scatter.13
  565.2 8.3 reduce-scatter.15
  613.4 26.5 reduce-scatter.17
  663.3 19.0 reduce-scatter.19
Sparse Core Ops, SparseCore 1:
  316.2 89.8 all-gather.6

commit v2 on v1

--- a/solution.py
+++ b/solution.py
@@ -242,6 +242,579 @@
         ],
         compiler_params=pltpu.CompilerParams(vmem_limit_bytes=56 << 20),
     )(length, qkv, out, total, upstream, cosine, sine)
+
+
+MESH = pl.DeviceIdType.MESH
+ANY = pl.BlockSpec(memory_space=pl.ANY)
+VMEM = pl.BlockSpec(memory_space=pltpu.VMEM)
+DMA = pltpu.SemaphoreType.DMA
+
+
+def head_place(head, heads, ctx_size, expert_size):
+    per = expert_size - 1
+    if ctx_size <= expert_size and ctx_size * per == heads:
+        row = head // per
+        step = head % per
+        return row, step + jnp.where(step >= row, 1, 0)
+    return head // expert_size, head % expert_size
+
+
+def head_of(ctx, expert, heads, ctx_size, expert_size):
+    per = expert_size - 1
+    if ctx_size <= expert_size and ctx_size * per == heads:
+        head = ctx * per + expert - jnp.where(expert > ctx, 1, 0)
+        return jnp.where(expert == ctx, heads, head)
+    return ctx * expert_size + expert
+
+
+def greet(partners):
+    barrier = pltpu.get_barrier_semaphore()
+    for partner in partners:
+        pl.semaphore_signal(barrier, inc=1, device_id=partner, device_id_type=MESH)
+    pl.semaphore_wait(barrier, len(partners))
+
+
+def trade_kernel(heads, inward, in_ref, out_ref, send_sem, recv_sem):
+    ctx_size, expert_size = lax.axis_size("ctx"), lax.axis_size("expert")
+    count = ctx_size * expert_size
+    ctx, expert = lax.axis_index("ctx"), lax.axis_index("expert")
+    me = ctx * expert_size + expert
+    mine = head_of(ctx, expert, heads, ctx_size, expert_size)
+    holds = mine < heads
+    greet(
+        [
+            {"ctx": ((me + i) % count) // expert_size, "expert": ((me + i) % count) % expert_size}
+            for i in range(1, count)
+        ]
+    )
+
+    def copy(source, target, at, by, there):
+        return pltpu.make_async_remote_copy(
+            src_ref=in_ref.at[source],
+            dst_ref=out_ref.at[target],
+            send_sem=send_sem.at[at],
+            recv_sem=recv_sem.at[by],
+            device_id=there,
+            device_id_type=MESH,
+        )
+
+    if inward:
+        def sends():
+            for i in range(heads):
+                head = (me + i) % heads
+                row, column = head_place(head, heads, ctx_size, expert_size)
+                yield head != mine, copy(head, me, head, me, {"ctx": row, "expert": column})
+
+        for needed, one in sends():
+            pl.when(needed)(one.start)
+
+        @pl.when(holds)
+        def _():
+            out_ref[me] = in_ref[mine % heads]
+
+        @pl.when(jnp.logical_not(holds))
+        def _():
+            out_ref[...] = jnp.zeros_like(out_ref)
+
+        for i in range(1, count):
+            source = (me + count - i) % count
+            pl.when(holds)(copy(0, source, 0, source, {"ctx": ctx, "expert": expert}).wait_recv)
+        for needed, one in sends():
+            pl.when(needed)(one.wait_send)
+    else:
+        def sends():
+            for i in range(1, count):
+                there = (me + i) % count
+                yield copy(
+                    there,
+                    mine % heads,
+                    i,
+                    mine % heads,
+                    {"ctx": there // expert_size, "expert": there % expert_size},
+                )
+
+        for one in sends():
+            pl.when(holds)(one.start)
+
+        @pl.when(holds)
+        def _():
+            out_ref[mine % heads] = in_ref[me]
+
+        for i in range(heads):
+            head = (me + i) % heads
+            pl.when(head != mine)(copy(0, head, 0, head, {"ctx": ctx, "expert": expert}).wait_recv)
+        for one in sends():
+            pl.when(holds)(one.wait_send)
+
+
+def trade(blocks, heads, count, inward, number):
+    lead = count if inward else heads
+    return pl.pallas_call(
+        functools.partial(trade_kernel, heads, inward),
+        out_shape=jax.ShapeDtypeStruct((lead,) + blocks.shape[1:], blocks.dtype),
+        in_specs=[VMEM],
+        out_specs=VMEM,
+        scratch_shapes=[DMA((count,)), DMA((count,))],
+        compiler_params=pltpu.CompilerParams(
+            collective_id=number, has_side_effects=True, vmem_limit_bytes=32 << 20
+        ),
+    )(blocks)
+
+
+def across(axis, bit):
+    index = lax.axis_index(axis)
+    return index + bit * (1 - 2 * ((index // bit) % 2))
+
+
+def flip(index, mask):
+    bit = 1
+    while bit <= mask:
+        if mask & bit:
+            index = index + bit * (1 - 2 * ((index // bit) % 2))
+        bit *= 2
+    return index
+
+
+def plan(expert_size, ctx_size, chunk, rows):
+    bits = [1 << b for b in range(ctx_size.bit_length() - 1)]
+    items = []
+    for step in range(expert_size):
+        items.append((step, None, chunk, bits if step % 2 == 0 else bits[::-1]))
+    half = rows // 2
+    items.append((None, 0, half, bits))
+    items.append((None, half, rows - half, bits[::-1]))
+    return items, bits
+
+
+def spread_kernel(
+    rows_ref, flat_ref, gate_ref, out_ref, gates_ref, z_send, z_recv, send, recv, pair_recv, gate_send,
+    gate_recv, gate_z_send, gate_z_recv, local_sem,
+):
+    dp_size, ctx_size, expert_size = (lax.axis_size(a) for a in ("dp", "ctx", "expert"))
+    dp, ctx, expert = (lax.axis_index(a) for a in ("dp", "ctx", "expert"))
+    chunk, rows = rows_ref.shape[1], flat_ref.shape[0]
+    items, bits = plan(expert_size, ctx_size, chunk, rows)
+    plane_size = dp_size * ctx_size
+    own = dp * ctx_size + ctx
+
+    def z_at(step):
+        return (expert + step) % expert_size
+
+    def z_from(step):
+        return (expert + expert_size - step) % expert_size
+
+    plane = [(d, c) for d in range(dp_size) for c in range(ctx_size) if (d, c) != (0, 0)]
+    greet(
+        [{"expert": z_at(step)} for step in range(1, expert_size)]
+        + [{"dp": (dp + d) % dp_size, "ctx": flip(ctx, c)} for d, c in plane]
+    )
+
+    def region(item):
+        step, first, size, _ = item
+        if step is None:
+            return pl.ds(expert_size * chunk + first, size)
+        return pl.ds(pl.multiple_of(z_from(step) * chunk, 16), size)
+
+    def z_copy(step, landing=False):
+        place = z_from(step) if landing else expert
+        return pltpu.make_async_remote_copy(
+            src_ref=rows_ref.at[z_at(step)],
+            dst_ref=out_ref.at[own, pl.ds(pl.multiple_of(place * chunk, 16), chunk)],
+            send_sem=z_send.at[step],
+            recv_sem=z_recv.at[step],
+            device_id={"expert": z_at(step)},
+            device_id_type=MESH,
+        )
+
+    def gate_z(step, landing=False):
+        return pltpu.make_async_remote_copy(
+            src_ref=gate_ref.at[z_at(step)],
+            dst_ref=gates_ref.at[own, z_from(step) if landing else expert],
+            send_sem=gate_z_send.at[step],
+            recv_sem=gate_z_recv.at[step],
+            device_id={"expert": z_at(step)},
+            device_id_type=MESH,
+        )
+
+    def gate_plane(d, c, block):
+        return pltpu.make_async_remote_copy(
+            src_ref=gates_ref.at[block],
+            dst_ref=gates_ref.at[block],
+            send_sem=gate_send.at[d, c],
+            recv_sem=gate_recv.at[d, c],
+            device_id={"dp": (dp + d) % dp_size, "ctx": flip(ctx, c)},
+            device_id_type=MESH,
+        )
+
+    for step in range(1, expert_size):
+        gate_z(step).start()
+        z_copy(step).start()
+
+    def source(number):
+        step, first, size, _ = items[number]
+        if step is None:
+            return flat_ref.at[pl.ds(first, size)]
+        if step == 0:
+            return rows_ref.at[expert]
+        return out_ref.at[own, region(items[number])]
+
+    def passing(number, mask, bit, origin):
+        block = dp * ctx_size + flip(ctx, mask)
+        here = out_ref.at[block, region(items[number])]
+        return pltpu.make_async_remote_copy(
+            src_ref=source(number) if origin else here,
+            dst_ref=here,
+            send_sem=send.at[number, mask, bits.index(bit)],
+            recv_sem=recv.at[number, mask ^ bit],
+            device_id={"ctx": flip(ctx, bit)},
+            device_id_type=MESH,
+        )
+
+    def crossing(number, mask, other, origin):
+        block = dp * ctx_size + flip(ctx, mask)
+        here = out_ref.at[block, region(items[number])]
+        return pltpu.make_async_remote_copy(
+            src_ref=source(number) if origin else here,
+            dst_ref=here,
+            send_sem=send.at[number, mask, len(bits) + other - 1],
+            recv_sem=pair_recv.at[number, mask, other - 1],
+            device_id={"dp": (dp + other) % dp_size},
+            device_id_type=MESH,
+        )
+
+    def arrived(number, mask):
+        block = dp * ctx_size + flip(ctx, mask)
+        here = out_ref.at[block, region(items[number])]
+        pltpu.make_async_remote_copy(
+            src_ref=here, dst_ref=here, send_sem=send.at[0, 0, 0], recv_sem=recv.at[number, mask],
+            device_id={"ctx": ctx}, device_id_type=MESH,
+        ).wait_recv()
+
+    started = []
+
+    def begin(number):
+        for bit in items[number][3]:
+            one = passing(number, 0, bit, True)
+            one.start()
+            started.append(one)
+        for other in range(1, dp_size):
+            one = crossing(number, 0, other, True)
+            one.start()
+            started.append(one)
+
+    def forward(number):
+        order = items[number][3]
+        masks = [0]
+        for place, bit in enumerate(order):
+            for mask in [m | bit for m in masks]:
+                arrived(number, mask)
+                for later in order[place + 1 :]:
+                    one = passing(number, mask, later, False)
+                    one.start()
+                    started.append(one)
+                for other in range(1, dp_size):
+                    one = crossing(number, mask, other, False)
+                    one.start()
+                    started.append(one)
+            masks = masks + [m | bit for m in masks]
+
+    ready = [0, expert_size, expert_size + 1]
+    for number in ready:
+        begin(number)
+    kept = [
+        pltpu.make_async_copy(source(number), out_ref.at[own, region(items[number])], local_sem.at[i])
+        for i, number in enumerate(ready)
+    ]
+    for one in kept:
+        one.start()
+    gates_ref[own, expert] = gate_ref[expert]
+    waiting = list(ready)
+    for step in range(1, expert_size):
+        z_copy(step, True).wait_recv()
+        begin(step)
+        waiting.append(step)
+        forward(waiting.pop(0))
+    for step in range(1, expert_size):
+        gate_z(step, True).wait_recv()
+    for d, c in plane:
+        gate_plane(d, c, own).start()
+    for number in waiting:
+        forward(number)
+    for d, c in plane:
+        gate_plane(d, c, ((dp + d) % dp_size) * ctx_size + flip(ctx, c)).wait_recv()
+        gate_plane(d, c, own).wait_send()
+    for number in range(len(items)):
+        for mask in range(ctx_size):
+            for other in range(1, dp_size):
+                block = ((dp + dp_size - other) % dp_size) * ctx_size + flip(ctx, mask)
+                here = out_ref.at[block, region(items[number])]
+                pltpu.make_async_remote_copy(
+                    src_ref=here, dst_ref=here, send_sem=send.at[0, 0, 0],
+                    recv_sem=pair_recv.at[number, mask, other - 1], device_id={"dp": dp}, device_id_type=MESH,
+                ).wait_recv()
+    for one in started:
+        one.wait_send()
+    for step in range(1, expert_size):
+        z_copy(step).wait_send()
+        gate_z(step).wait_send()
+    for one in kept:
+        one.wait()
+
+
+def spread(rows, flat, gate, sizes, number):
+    dp_size, ctx_size, expert_size = sizes
+    chunk, width = rows.shape[1:]
+    count = expert_size + 2
+    links = max(ctx_size.bit_length() - 1 + dp_size - 1, 1)
+    block = expert_size * chunk + flat.shape[0]
+    return pl.pallas_call(
+        spread_kernel,
+        out_shape=(
+            jax.ShapeDtypeStruct((dp_size * ctx_size, block, width), rows.dtype),
+            jax.ShapeDtypeStruct((dp_size * ctx_size,) + gate.shape, gate.dtype),
+        ),
+        in_specs=[VMEM, VMEM, VMEM],
+        out_specs=(ANY, VMEM),
+        scratch_shapes=[
+            DMA((expert_size,)),
+            DMA((expert_size,)),
+            DMA((count, ctx_size, links)),
+            DMA((count, ctx_size)),
+            DMA((count, ctx_size, dp_size)),
+            DMA((dp_size, ctx_size)),
+            DMA((dp_size, ctx_size)),
+            DMA((expert_size,)),
+            DMA((expert_size,)),
+            DMA((3,)),
+        ],
+        compiler_params=pltpu.CompilerParams(
+            collective_id=number, has_side_effects=True, vmem_limit_bytes=32 << 20
+        ),
+    )(rows, flat, gate)
+
+
+def home_kernel(
+    depth, part_ref, dot_ref, rows_ref, flat_ref, dots_ref, mine, theirs, dot_in, dot_sum, mine_sem,
+    pair_send, pair_recv, send, recv, z_send, z_recv, dot_send, dot_recv, dot_z_send, dot_z_recv,
+    *arrivals,
+):
+    dp_size, ctx_size, expert_size = (lax.axis_size(a) for a in ("dp", "ctx", "expert"))
+    dp, ctx, expert = (lax.axis_index(a) for a in ("dp", "ctx", "expert"))
+    chunk, rows = rows_ref.shape[1], flat_ref.shape[0]
+    items, bits = plan(expert_size, ctx_size, chunk, rows)
+    own = dp * ctx_size + ctx
+    other = (dp + 1) % dp_size
+
+    def z_at(step):
+        return (expert + step) % expert_size
+
+    def z_from(step):
+        return (expert + expert_size - step) % expert_size
+
+    plane = [(d, c) for d in range(dp_size) for c in range(ctx_size) if (d, c) != (0, 0)]
+    greet(
+        [{"expert": z_at(step)} for step in range(1, expert_size)]
+        + [{"dp": (dp + d) % dp_size, "ctx": flip(ctx, c)} for d, c in plane]
+    )
+
+    def region(number):
+        step, start, size, _ = items[number]
+        if step is None:
+            return pl.ds(expert_size * chunk + start, size)
+        return pl.ds(pl.multiple_of(z_at(step) * chunk, 16), size)
+
+    starts = [0]
+    for item in items:
+        starts.append(starts[-1] + item[2])
+
+    def held(number):
+        return pl.ds(starts[number], items[number][2])
+
+    def load(number, mask):
+        return pltpu.make_async_copy(
+            part_ref.at[dp * ctx_size + flip(ctx, mask), region(number)],
+            mine.at[mask, held(number)],
+            mine_sem.at[number, mask],
+        )
+
+    def cross(number, mask):
+        return pltpu.make_async_remote_copy(
+            src_ref=part_ref.at[other * ctx_size + flip(ctx, mask), region(number)],
+            dst_ref=theirs.at[mask, held(number)],
+            send_sem=pair_send.at[number, mask],
+            recv_sem=pair_recv.at[number, mask],
+            device_id={"dp": other},
+            device_id_type=MESH,
+        )
+
+    def dot_plane(d, c):
+        return pltpu.make_async_remote_copy(
+            src_ref=dot_ref.at[((dp + d) % dp_size) * ctx_size + flip(ctx, c)],
+            dst_ref=dot_in.at[d, c],
+            send_sem=dot_send.at[d, c],
+            recv_sem=dot_recv.at[d, c],
+            device_id={"dp": (dp + d) % dp_size, "ctx": flip(ctx, c)},
+            device_id_type=MESH,
+        )
+
+    def dot_z(step, landing=False):
+        return pltpu.make_async_remote_copy(
+            src_ref=dot_sum.at[z_at(step)],
+            dst_ref=dots_ref.at[z_from(step) if landing else expert],
+            send_sem=dot_z_send.at[step],
+            recv_sem=dot_z_recv.at[step],
+            device_id={"expert": z_at(step)},
+            device_id_type=MESH,
+        )
+
+    order = list(range(1, expert_size)) + [0, expert_size, expert_size + 1]
+    for number in order:
+        for mask in range(ctx_size):
+            cross(number, mask).start()
+            load(number, mask).start()
+    for d, c in plane:
+        dot_plane(d, c).start()
+
+    def stage(number, place):
+        order = items[number][3][::-1]
+        done = sum(order[:place])
+        bit = order[place]
+        rest = [m for m in range(ctx_size) if not m & (done | bit)]
+        return bit, [(m | bit, m) for m in rest]
+
+    def hop(number, place, index):
+        bit, moves = stage(number, place)
+        source = moves[index][0]
+        return pltpu.make_async_remote_copy(
+            src_ref=mine.at[source, held(number)],
+            dst_ref=arrivals[place].at[index, held(number)],
+            send_sem=send.at[number, source],
+            recv_sem=recv.at[number, place, index],
+            device_id={"ctx": flip(ctx, bit)},
+            device_id_type=MESH,
+        )
+
+    def z_copy(number, landing=False):
+        return pltpu.make_async_remote_copy(
+            src_ref=mine.at[0, held(number)],
+            dst_ref=rows_ref.at[z_from(number) if landing else expert],
+            send_sem=z_send.at[number],
+            recv_sem=z_recv.at[number],
+            device_id={"expert": z_at(number)},
+            device_id_type=MESH,
+        )
+
+    def add(number, mask, buffer, index):
+        at = held(number)
+        mine[mask, at] = (mine[mask, at].astype(f32) + buffer[index, at].astype(f32)).astype(mine.dtype)
+
+    def pair(number):
+        leaving = [source for source, _ in stage(number, 0)[1]]
+        for mask in leaving + [m for m in range(ctx_size) if m not in leaving]:
+            load(number, mask).wait()
+            cross(number, mask).wait_recv()
+            add(number, mask, theirs, mask)
+            if mask in leaving:
+                hop(number, 0, leaving.index(mask)).start()
+
+    def step(number, place):
+        _, moves = stage(number, place)
+        for index, (_, target) in enumerate(moves):
+            hop(number, place, index).wait_recv()
+        following = stage(number, place + 1)[1] if place + 1 < depth else []
+        leaving = [source for source, _ in following]
+        targets = [target for _, target in moves]
+        for mask in leaving + [m for m in targets if m not in leaving]:
+            add(number, mask, arrivals[place], targets.index(mask))
+            if mask in leaving:
+                hop(number, place + 1, leaving.index(mask)).start()
+
+    def finish(number):
+        kind = items[number][0]
+        if kind is None:
+            start, size = items[number][1], items[number][2]
+            flat_ref[pl.ds(start, size)] = mine[0, held(number)]
+        elif kind == 0:
+            rows_ref[expert] = mine[0, held(number)]
+        else:
+            z_copy(number).start()
+
+    for tick in range(len(order) + depth):
+        for place in reversed(range(depth + 1)):
+            index = tick - place
+            if not 0 <= index < len(order):
+                continue
+            number = order[index]
+            if place == 0:
+                pair(number)
+            else:
+                step(number, place - 1)
+            if place == depth:
+                finish(number)
+
+    total_dots = dot_ref[own]
+    for d, c in plane:
+        dot_plane(d, c).wait_recv()
+        total_dots = total_dots + dot_in[d, c]
+    dot_sum[...] = total_dots
+    for number in range(1, expert_size):
+        dot_z(number).start()
+    dots_ref[expert] = dot_sum[expert]
+
+    for number in range(1, expert_size):
+        z_copy(number, True).wait_recv()
+        dot_z(number, True).wait_recv()
+    for number in range(1, expert_size):
+        z_copy(number).wait_send()
+        dot_z(number).wait_send()
+    for d, c in plane:
+        dot_plane(d, c).wait_send()
+    for number in order:
+        for mask in range(ctx_size):
+            cross(number, mask).wait_send()
+        for place in range(depth):
+            for index in range(len(stage(number, place)[1])):
+                hop(number, place, index).wait_send()
+
+
+def bring_home(part, dots, rows, sizes, number):
+    dp_size, ctx_size, expert_size = sizes
+    block, width = part.shape[1:]
+    chunk = (block - rows) // expert_size
+    count = expert_size + 2
+    depth = ctx_size.bit_length() - 1
+    buffer = (ctx_size, block, width)
+    return pl.pallas_call(
+        functools.partial(home_kernel, depth),
+        out_shape=(
+            jax.ShapeDtypeStruct((expert_size, chunk, width), part.dtype),
+            jax.ShapeDtypeStruct((rows, width), part.dtype),
+            jax.ShapeDtypeStruct(dots.shape[1:], dots.dtype),
+        ),
+        in_specs=[ANY, VMEM],
+        out_specs=(VMEM, VMEM, VMEM),
+        scratch_shapes=[
+            pltpu.VMEM(buffer, part.dtype),
+            pltpu.VMEM(buffer, part.dtype),
+            pltpu.VMEM((dp_size, ctx_size) + dots.shape[1:], dots.dtype),
+            pltpu.VMEM(dots.shape[1:], dots.dtype),
+            DMA((count, ctx_size)),
+            DMA((count, ctx_size)),
+            DMA((count, ctx_size)),
+            DMA((count, ctx_size)),
+            DMA((count, depth, max(ctx_size // 2, 1))),
+            DMA((count,)),
+            DMA((count,)),
+            DMA((dp_size, ctx_size)),
+            DMA((dp_size, ctx_size)),
+            DMA((expert_size,)),
+            DMA((expert_size,)),
+        ]
+        + [pltpu.VMEM((ctx_size >> (place + 1),) + buffer[1:], part.dtype) for place in range(depth)],
+        compiler_params=pltpu.CompilerParams(
+            collective_id=number, has_side_effects=True, vmem_limit_bytes=56 << 20
+        ),
+    )(part, dots)
 
 
 def local(
@@ -297,22 +870,27 @@
     ).reshape(rows, TOP, EXPERTS * PLACES)
     either = jnp.any(dispatch, axis=1).astype(bf16)
 
-    def to_experts(flat):
-        return lax.all_to_all(
-            flat.reshape((expert_size, -1) + flat.shape[1:]), "expert", 0, 0
-        )
-
-    def spread(flat):
+    sizes = (dp_size, ctx_size, expert_size)
+
+    def place_rows(flat):
         placed = jnp.einsum("ts,td->sd", either, flat, preferred_element_type=f32).astype(bf16)
-        mine = to_experts(placed).reshape(-1, width)
-        return lax.all_gather(jnp.concatenate([mine, flat], axis=0), PLANE, axis=0)
-
-    up_all = spread(d_branch_low)
+        return placed.reshape(expert_size, -1, width)
+
+    def to_experts(blocks):
+        here = lax.axis_index("expert")
+        taken = [lax.dynamic_index_in_dim(blocks, here, 0, False)]
+        for step in range(1, expert_size):
+            sent = lax.dynamic_index_in_dim(blocks, (here + step) % expert_size, 0, False)
+            ring = [(i, (i + step) % expert_size) for i in range(expert_size)]
+            taken.append(lax.ppermute(sent, "expert", ring))
+        return jnp.take(jnp.stack(taken), (here - jnp.arange(expert_size)) % expert_size, axis=0)
+
+    up_mine = to_experts(place_rows(d_branch_low)).reshape(-1, width)
+    up_all = lax.all_gather(jnp.concatenate([up_mine, d_branch_low], axis=0), PLANE, axis=0)
 
     scale_one = rms_scale(inputs)
     normal_one = inputs * scale_one
     normed_low = (normal_one * norm1_gain).astype(bf16)
-    normed_all = lax.all_gather(normed_low, SLOT, axis=0, tiled=True)
     cosine, sine = rope_tables(positions)
 
     def project(weight):
@@ -330,20 +908,20 @@
     key = rotated(project(key_weight)).astype(bf16)
     value = project(value_weight).astype(bf16)
 
-    def to_heads(blocks):
-        spare = jnp.zeros((slot_size - heads,) + blocks.shape[1:], blocks.dtype)
-        return lax.all_to_all(jnp.concatenate([blocks, spare], axis=0), SLOT, 0, 0)
-
-    def from_heads(blocks):
-        return lax.all_to_all(blocks, SLOT, 0, 0)[:heads]
+    def to_heads(blocks, number):
+        return trade(blocks, heads, slot_size, True, number)
+
+    def from_heads(blocks, number):
+        return trade(blocks, heads, slot_size, False, number)
 
     def by_block(flat_t):
         return jnp.transpose(flat_t.reshape(-1, slot_size, rows), (1, 0, 2))
 
-    qkv = to_heads(jnp.concatenate([query, key, value], axis=1))
+    qkv = to_heads(jnp.concatenate([query, key, value], axis=1), 1)
+    normed_all = lax.all_gather(normed_low, SLOT, axis=0, tiled=True)
     out_t, log_total = attend(qkv, lengths)
     attended = jnp.transpose(
-        from_heads(by_block(out_t.astype(bf16))).reshape(width, rows)
+        from_heads(by_block(out_t.astype(bf16)), 2).reshape(width, rows)
     )
     attn_out = jnp.dot(attended, output_weight, preferred_element_type=f32)
     hidden_in = inputs + valid * attn_out
@@ -356,10 +934,18 @@
     shifted = jnp.exp(chosen - jnp.max(chosen, axis=-1, keepdims=True))
     gate_weights = shifted / jnp.sum(shifted, axis=-1, keepdims=True)
 
-    in_all = spread(normed_two_low)
     gate_rows = jnp.sum(jnp.where(dispatch, gate_weights[:, :, None], 0.0), axis=(0, 1))
-    gate_all = lax.all_gather(to_experts(gate_rows).reshape(-1), PLANE, axis=0)
     placed_rows = EXPERTS * PLACES
+
+    def tiled(row):
+        row = row.reshape(row.shape[:-1] + (expert_size, 1, -1))
+        return jnp.pad(row, [(0, 0)] * (row.ndim - 2) + [(0, 7), (0, 128 - row.shape[-1])])
+
+    def flat_row(tile):
+        return tile[..., 0, : own * PLACES].reshape(tile.shape[:-3] + (placed_rows,))
+
+    in_all, gate_all = spread(place_rows(normed_two_low), normed_two_low, tiled(gate_rows), sizes, 3)
+    gate_all = flat_row(gate_all)
 
     def by_expert(both):
         cut = both[:, :placed_rows].reshape((plane_size * expert_size, own, PLACES) + both.shape[2:])
@@ -412,28 +998,30 @@
         1.0,
     )
 
-    def home(expert_part, shared_part):
-        both = jnp.concatenate(
+    def joined(expert_part, shared_part):
+        return jnp.concatenate(
             [by_source(expert_part), shared_part.reshape(plane_size, rows, width)], axis=1
         ).astype(bf16)
-        both = lax.psum_scatter(both, "dp", scatter_dimension=0, tiled=True)
-        both = lax.psum_scatter(both, "ctx", scatter_dimension=0, tiled=True)[0]
-        back = to_experts(both[:placed_rows]).reshape(placed_rows, width)
-        spread_rows = jnp.dot(either, back, preferred_element_type=f32)
-        return spread_rows + both[placed_rows:].astype(f32)
-
-    d_gate_rows = lax.psum_scatter(d_gate_part, PLANE, scatter_dimension=0, tiled=True)[0]
-    d_gate_rows = to_experts(d_gate_rows).reshape(-1)
+
+    def collect(back, flat):
+        spread_rows = jnp.dot(either, back.reshape(placed_rows, width), preferred_element_type=f32)
+        return spread_rows + flat.astype(f32)
+
+    back, flat, d_gate_rows = bring_home(joined(d_rows, shared_d), tiled(d_gate_part), rows, sizes, 4)
+    d_gate_rows = flat_row(d_gate_rows)
+    out_back, out_flat, _ = bring_home(
+        joined(result * gate_factor, shared_result), tiled(d_gate_part), rows, sizes, 5
+    )
     d_gates = jnp.sum(jnp.where(dispatch, d_gate_rows, 0.0), axis=-1)
     d_chosen = gate_weights * (
         d_gates - jnp.sum(gate_weights * d_gates, axis=-1, keepdims=True)
     )
     d_logits = jnp.sum(picked * d_chosen[:, :, None], axis=1).astype(bf16)
     d_router = jnp.einsum("td,te->de", normed_two_low, d_logits, preferred_element_type=f32)
-    d_normed_two = home(d_rows, shared_d) + jnp.einsum(
+    d_normed_two = collect(back, flat) + jnp.einsum(
         "te,de->td", d_logits, router_weight, preferred_element_type=f32
     )
-    output_rows = hidden_in + valid * home(result * gate_factor, shared_result)
+    output_rows = hidden_in + valid * collect(out_back, out_flat)
     output_rows = output_rows.astype(bf16)[None]
     d_gain_two = jnp.sum(d_normed_two * normal_two, axis=0)
     d_hidden_in = upstream + rms_back(normal_two, scale_two, norm2_gain, d_normed_two)
@@ -441,13 +1029,14 @@
     d_attn_low = (valid * d_hidden_in).astype(bf16)
     d_output_weight = jnp.einsum("td,te->de", attended, d_attn_low, preferred_element_type=f32)
     d_attended = jnp.einsum("te,de->dt", d_attn_low, output_weight, preferred_element_type=f32)
-    d_attended = to_heads(d_attended.astype(bf16).reshape(heads, HEAD_DIM, rows))
+    d_attended = to_heads(d_attended.astype(bf16).reshape(heads, HEAD_DIM, rows), 6)
     all_cosine, all_sine = rope_tables(jnp.arange(slot_size * rows, dtype=jnp.int32))
     d_qkv = attend_back(qkv, lengths, out_t, log_total, d_attended, all_cosine, all_sine)
+    d_mine = from_heads(d_qkv, 7)
     head_grad = jnp.einsum(
         "bet,btd->ed", d_qkv, normed_all.reshape(slot_size, rows, width), preferred_element_type=f32
     )
-    d_own = jnp.swapaxes(from_heads(d_qkv).reshape(heads, 3, HEAD_DIM, rows), 0, 1)
+    d_own = jnp.swapaxes(d_mine.reshape(heads, 3, HEAD_DIM, rows), 0, 1)
     d_own = d_own.reshape(3, width, rows)
     d_normed = jnp.zeros((width, rows), f32)
     for weight, grad in zip((query_weight, key_weight, value_weight), d_own):
@@ -460,9 +1049,9 @@
     shard = width // (dp_size * slot_size)
     head_grad = jnp.transpose(head_grad).reshape(-1, 3 * HEAD_DIM)
     head_grad = lax.psum_scatter(head_grad, "dp", scatter_dimension=0, tiled=True)
-    head_grad = lax.all_to_all(head_grad.reshape(slot_size, shard, 3 * HEAD_DIM), SLOT, 0, 0)
+    head_grad = from_heads(head_grad.reshape(slot_size, shard, 3 * HEAD_DIM), 8)
     head_grad = jnp.transpose(
-        head_grad[:heads].reshape(heads, shard, 3, HEAD_DIM), (2, 1, 0, 3)
+        head_grad.reshape(heads, shard, 3, HEAD_DIM), (2, 1, 0, 3)
     ).reshape(3, shard, width)
 
     def scatter(grad):

time: 699 us -> 589 us (0.84)
  Pallas kernels: 18.8 us -> 278 us
  waiting for transfers between devices: 247 us -> 16.3 us
  blocking collectives: 164 us -> 40.9 us
  starting transfers between devices: 37.8 us -> 13.3 us
  local copies, waits for them, and re-layouts: 66.4 us -> 81 us
    pallas_call x0 -> x8, Pallas kernels: none -> 259 us  [the longest x2 141 us: bring_home(): pl.pallas_call(functools.partial(home_kernel, depth), out_shape=(jax.Shap...]
    unnamed x14 -> x9, waiting for transfers between devices: 136 us -> 0.76 us
    all_to_all x4 -> x0, blocking collectives: 76.2 us -> none  [the longest x2 38 us: to_experts(): lax.all_to_all(flat.reshape((expert_size, -1) + flat.shape[1:]), 'expert'...]
    all_to_all x7 -> x0, waiting for transfers between devices: 52.9 us -> none  [the longest x4 36.6 us: to_experts(): lax.all_to_all(flat.reshape((expert_size, -1) + flat.shape[1:]), 'expert'...]
    all_to_all x7 -> x0, starting transfers between devices: 30.3 us -> none  [the longest x4 16.9 us: to_experts(): lax.all_to_all(flat.reshape((expert_size, -1) + flat.shape[1:]), 'expert'...]
    all_gather x2 -> x1, waiting for transfers between devices: 28.7 us -> 0.01 us  [local(): lax.all_gather(jnp.concatenate([up_mine, d_branch_low], axis=0), PLANE, a...]
    unnamed x1 -> x0, blocking collectives: 26.5 us -> none
    all_gather x1 -> x0, blocking collectives: 19.8 us -> none  [local(): gate_all = lax.all_gather(to_experts(gate_rows).reshape(-1), PLANE, axis=0)]
  transfers between devices with their start and end apart: 21 -> 13, of which waited for: 12 -> 4; matrix products, arithmetic and copies ran while one was open for 21% -> 33% of each run, Pallas kernels for 3% -> 48%
where the time goes in v2:
time: 589 us; the launch traced here: 582 us
  Pallas kernels  278 us (47%)
  matrix products  92.2 us (16%)
  local copies, waits for them, and re-layouts  81 us (14%)
  other arithmetic  43.8 us (7%)
  blocking collectives  40.9 us (7%)
  waiting for transfers between devices  16.3 us (3%)
  between operations  16 us (3%)
  starting transfers between devices  13.3 us (2%)
    pallas_call x2, Pallas kernels, bring_home(): pl.pallas_call(functools.partial(home_kernel, depth), out_shape=(jax.Shap...  141 us
    pallas_call x5, Pallas kernels, trade(): pl.pallas_call(functools.partial(trade_kernel, heads, inward), out_shape=...  66.9 us
    dot_general x18, matrix products, dot(): return jnp.einsum(spec, a, b, preferred_element_type=f32)  65.5 us
    pallas_call x1, Pallas kernels, spread(): pl.pallas_call(spread_kernel, out_shape=(jax.ShapeDtypeStruct((dp_size *...  51.2 us
    psum x1, blocking collectives, local(): lax.psum(jnp.concatenate([d_router, d_gain_one[:, None], d_gain_two[:, No...  40.9 us
    pallas_call x1, Pallas kernels, attend_back(): pl.pallas_call(functools.partial(attend_back_kernel, step), out_shape=jax...  12.4 us
  transfers between devices with their start and end apart: 13, of which 4 were waited for; matrix products, arithmetic and copies ran while one was open for 33% of the time, Pallas kernels for 48%

profile of v2, /device:TPU:0, one launch (start us, length us, event | category | flops | bytes accessed | tf_op | source)
XLA Modules:
  0.0 581.7 jit_solution(14016089583533579107)
XLA Ops:
  15.2 5.1 collective-permute-start.2
  24.9 8.2 %collective-permute-done.1 = bf16[96,768]{1,0:T(8,128)(2,1)} collective-permute-done((bf16[96,768]{1,0:T(8,128)(2,1)}, bf16[96,768]{1,0:T(8,128)(2,1)}, u32[]{:S(2)}, u32[]{:S(2)}) %collective-permute-start.1) | collective-permute-done | bytes 147488 | tf_op jit(solution)/shard_map/ppermute | solution.py:885
  59.1 15.3 %shard_map.280.qkv_ref = bf16[16,192,128]{2,1,0:T(8,128)(2,1)S(1)} custom-call(bf16[12,192,128]{2,1,0:T(8,128)(2,1)} %constant_dynamic-update-slice_fusion.in_ref), custom_call_target="tpu_custom_call" | custom-call | tf_op jit(solution)/shard_map/pallas_call | solution.py:352
  74.4 6.4 %shard_map.281 = (f32[64,2048]{1,0:T(8,128)S(1)}, f32[1,2048]{1,0:T(1,128)S(1)}) custom-call(s32[1]{0:T(128)} %copy.153.length_ref, bf16[16,192,128]{2,1,0:T(8,128)(2,1)S(1)} %shard_map.280.qkv_ref), custom_call_target="tpu_custom_call" | custom-call | tf_op jit(solution)/shard_map/pallas_call | solution.py:116
  81.8 12.4 %shard_map.282 = bf16[12,64,128]{2,1,0:T(8,128)(2,1)S(1)} custom-call(bf16[16,64,128]{2,1,0:T(8,128)(2,1)S(1)} %bitcast_bitcast_fusion.in_ref), custom_call_target="tpu_custom_call" | custom-call | tf_op jit(solution)/shard_map/pallas_call | solution.py:352
  103.1 51.2 %shard_map.283 = (bf16[8,512,768]{2,1,0:T(8,128)(2,1)S(1)}, f32[8,4,8,128]{3,2,1,0:T(8,128)S(1)}) custom-call(bf16[4,96,768]{2,1,0:T(8,128)(2,1)S(1)} %bitcast.206, bf16[128,768]{1,0:T(8,128)(2,1)S(1)} %multiply_convert_fusion.8.flat_ref, f32[4,8,128]{2,1,0:T(8,128)S(1)} %pad.9.gate_ref), custom_call_target="tpu_custom_call" | custom-call | tf_op jit(solution)/shard_map/pallas_call | solution.py:570
  169.2 4.8 copy.114
  182.5 5.3 multiply_convert_fusion.3
  191.0 4.9 convert_bitcast_fusion
  195.9 4.7 copy.117
  200.6 7.3 %fusion.1 = (bf16[4,768,768]{2,1,0:T(8,128)(2,1)}, f32[4,768]{1,0:T(4,128)}, bf16[4,768,768]{2,1,0:T(8,128)(2,1)}) fusion(f32[4,32,24,768]{3,2,1,0:T(8,128)S(1)} %copy.117, f32[4,768]{1,0:T(4,128)S(1)} %mul.379, bf16[4,768,256]{2,1,0:T(8,128)(2,1)S(1)} %copy-done.11, bf16[4,2048,768]{2,1,0:T(8,128)(2,1)} %param.29, s32[]{:T(128)S(6)} %select_n.95), kind=kOutput, calls=%fused_computation.5 | convolution fusion | flops 1222112256 | bytes 22044676 | tf_op jit(solution)/shard_map/erf,efd->erd/dot_general | solution.py:966
  214.5 6.9 %multiply_convert_fusion.1 = (bf16[4,768,256]{2,1,0:T(8,128)(2,1)S(1)}, bf16[4,768,256]{2,1,0:T(8,128)(2,1)S(1)}) fusion(f32[4,768,256]{2,1,0:T(8,128)} %copy-done.67, f32[4,768,256]{2,1,0:T(8,128)} %get-tuple-element.68, bf16[4,768,768]{2,1,0:T(8,128)(2,1)} %get-tuple-element.41, bf16[4,2048,768]{2,1,0:T(8,128)(2,1)} %param.29, s32[]{:T(128)S(6)} %select_n.95), kind=kOutput, calls=%fused_computation.11 | convolution fusion | flops 1217396736 | bytes 15728644 | tf_op jit(solution)/shard_map/erd,efd->erf/dot_general | solution.py:966
  238.5 73.3 %shard_map.285 = (bf16[4,96,768]{2,1,0:T(8,128)(2,1)}, bf16[128,768]{1,0:T(8,128)(2,1)}, f32[4,8,128]{2,1,0:T(8,128)}) custom-call(bf16[8,512,768]{2,1,0:T(8,128)(2,1)} %pad_maximum_fusion.1.part_ref, f32[8,4,8,128]{3,2,1,0:T(8,128)} %pad.10.dot_ref), custom_call_target="tpu_custom_call" | custom-call | tf_op jit(solution)/shard_map/pallas_call | solution.py:787
  327.7 5.3 copy.116
  335.3 8.3 %shard_map.286.upstream_ref = bf16[16,64,128]{2,1,0:T(8,128)(2,1)S(1)} custom-call(bf16[12,64,128]{2,1,0:T(8,128)(2,1)S(1)} %bitcast.211), custom_call_target="tpu_custom_call" | custom-call | tf_op jit(solution)/shard_map/pallas_call | solution.py:352
  344.4 12.4 %shard_map.287.in_ref = bf16[16,192,128]{2,1,0:T(8,128)(2,1)} custom-call(s32[1]{0:T(128)} %copy.153.length_ref, bf16[16,192,128]{2,1,0:T(8,128)(2,1)} %copy-done.1, f32[64,2048]{1,0:T(8,128)} %copy-done.4, f32[1,2048]{1,0:T(1,128)} %copy-done.7, bf16[16,64,128]{2,1,0:T(8,128)(2,1)} %copy-done.6, f32[32,2048]{1,0:T(8,128)} %get-tuple-element.62.cosine_ref, ...), custom_call_target="tpu_custom_call" | custom-call | tf_op jit(solution)/shard_map/pallas_call | solution.py:226
  357.9 15.8 %shard_map.288 = bf16[12,192,128]{2,1,0:T(8,128)(2,1)S(1)} custom-call(bf16[16,192,128]{2,1,0:T(8,128)(2,1)S(1)} %copy-done.2), custom_call_target="tpu_custom_call" | custom-call | tf_op jit(solution)/shard_map/pallas_call | solution.py:352
  380.1 6.0 %pad_maximum_fusion.part_ref = bf16[8,512,768]{2,1,0:T(8,128)(2,1)} fusion(bf16[8,128,768]{2,1,0:T(8,128)(2,1)} %convolution_convert_fusion, bf16[8,384,768]{2,1,0:T(8,128)(2,1)} %bitcast.220), kind=kLoop, calls=%fused_computation.8 | loop fusion | flops 12582912 | bytes 12582912 | tf_op jit(solution)/shard_map/concatenate | solution.py:1002
  389.6 68.1 %shard_map.284 = (bf16[4,96,768]{2,1,0:T(8,128)(2,1)}, bf16[128,768]{1,0:T(8,128)(2,1)}, f32[4,8,128]{2,1,0:T(8,128)}) custom-call(bf16[8,512,768]{2,1,0:T(8,128)(2,1)} %pad_maximum_fusion.part_ref, f32[8,4,8,128]{3,2,1,0:T(8,128)} %pad.10.dot_ref), custom_call_target="tpu_custom_call" | custom-call | tf_op jit(solution)/shard_map/pallas_call | solution.py:787
  458.3 40.9 %psum.7 = f32[768,18]{0,1:T(8,128)} all-reduce(f32[768,18]{0,1:T(8,128)} %pad_maximum_fusion.4), channel_id=1, replica_groups=mesh['dp'=2,'ctx'=4,'expert'=4] {'dp','ctx','expert'}, use_global_device_ids=true, to_apply=%region_18.19 | all-reduce | flops 13824 | bytes 110592 | tf_op jit(solution)/shard_map/psum | solution.py:1063
  507.9 6.0 %fusion.89 = f32[4,256,768]{2,1,0:T(8,128)} fusion(bf16[4,768,256]{2,1,0:T(8,128)(2,1)} %get-tuple-element.67, bf16[4,768,768]{2,1,0:T(8,128)(2,1)} %get-tuple-element.41), kind=kOutput, calls=%fused_computation.193 | convolution fusion | flops 1207959552 | bytes 9437184 | tf_op jit(solution)/shard_map/erf,erd->efd/dot_general | solution.py:966
  513.9 5.9 %fusion.87 = f32[4,768,256]{2,1,0:T(8,128)} fusion(bf16[4,768,768]{2,1,0:T(8,128)(2,1)} %bitcast.213, bf16[4,768,256]{2,1,0:T(8,128)(2,1)S(1)} %copy-done.13), kind=kOutput, calls=%fused_computation.191 | convolution fusion | flops 1207959552 | bytes 9437184 | tf_op jit(solution)/shard_map/erd,erf->edf/dot_general | solution.py:966
  521.8 6.2 %fusion.88 = f32[4,768,256]{2,1,0:T(8,128)} fusion(bf16[4,768,768]{2,1,0:T(8,128)(2,1)} %bitcast.214, bf16[4,768,256]{2,1,0:T(8,128)(2,1)} %copy-done.16), kind=kOutput, calls=%fused_computation.192 | convolution fusion | flops 1207959552 | bytes 9437184 | tf_op jit(solution)/shard_map/erd,erf->edf/dot_general | solution.py:966
  549.6 15.1 %shard_map.289 = f32[12,24,192]{2,1,0:T(8,128)S(1)} custom-call(f32[16,24,192]{2,1,0:T(8,128)S(1)} %bitcast.210), custom_call_target="tpu_custom_call" | custom-call | tf_op jit(solution)/shard_map/pallas_call | solution.py:352
  (304 shorter events, 170.0 us)
Async XLA Ops:
  7.2 221.7 %copy-start = (bf16[2048,768]{1,0:T(8,128)(2,1)S(1)}, bf16[2048,768]{1,0:T(8,128)(2,1)}, u32[]{:S(2)}) copy-start(bf16[2048,768]{1,0:T(8,128)(2,1)} %param.32) | copy-start | bytes 9437188
  7.2 181.2 %all-gather.6.cloned.1.call-start = ((), (), s32[]{:S(2)}) async-start(), calls=%async_computation.13 | async-start | bytes 7077888 | tf_op jit(solution)/shard_map/all_gather | solution.py:889
  9.2 85.1 %copy-start.52 = (f32[128]{0:T(128)}, f32[128]{0:T(128)S(1)}, u32[]{:S(2)}) copy-start(f32[128]{0:T(128)S(1)} %get-tuple-element.39) | copy-start | bytes 1540
  10.9 89.2 %copy-start.55 = (s32[128,2]{0,1:T(2,128)}, s32[128,2]{0,1:T(2,128)S(1)}, u32[]{:S(2)}) copy-start(s32[128,2]{0,1:T(2,128)S(1)} %copy.112) | copy-start | bytes 3076
  15.2 9.7 %collective-permute-start.2 = (bf16[96,768]{1,0:T(8,128)(2,1)}, bf16[96,768]{1,0:T(8,128)(2,1)}, u32[]{:S(2)}, u32[]{:S(2)}) collective-permute-start(bf16[96,768]{1,0:T(8,128)(2,1)} %get-tuple-element.56), channel_id=1, source_target_pairs={{0,3},{1,0},{2,1},{3,2},{4,7},{5,4},{6,5},{7,6},{8,11},{9,8},{10,9... | collective-permute-start | bytes 442376 | tf_op jit(solution)/shard_map/ppermute | solution.py:885
  20.3 12.8 %collective-permute-start.1 = (bf16[96,768]{1,0:T(8,128)(2,1)}, bf16[96,768]{1,0:T(8,128)(2,1)}, u32[]{:S(2)}, u32[]{:S(2)}) collective-permute-start(bf16[96,768]{1,0:T(8,128)(2,1)} %get-tuple-element.57), channel_id=1, source_target_pairs={{0,2},{1,3},{2,0},{3,1},{4,6},{5,7},{6,4},{7,5},{8,10},{9,11},{10,... | collective-permute-start | bytes 442376 | tf_op jit(solution)/shard_map/ppermute | solution.py:885
  20.3 12.8 %collective-permute-start = (bf16[96,768]{1,0:T(8,128)(2,1)}, bf16[96,768]{1,0:T(8,128)(2,1)}, u32[]{:S(2)}, u32[]{:S(2)}) collective-permute-start(bf16[96,768]{1,0:T(8,128)(2,1)} %get-tuple-element.58), channel_id=1, source_target_pairs={{0,1},{1,2},{2,3},{3,0},{4,5},{5,6},{6,7},{7,4},{8,9},{9,10},{10,1... | collective-permute-start | bytes 442376 | tf_op jit(solution)/shard_map/ppermute | solution.py:885
  39.7 463.0 %all-gather.4.cloned.1.call-start = ((), (), s32[]{:S(2)}) async-start(), calls=%async_computation.7 | async-start | bytes 3342336 | tf_op jit(solution)/shard_map/all_gather | solution.py:921
  40.8 465.7 %reduce-scatter.10.cloned.1.call-start = ((), (), s32[]{:S(2)}) async-start(), calls=%async_computation.9 | async-start | bytes 1769472 | tf_op jit(solution)/shard_map/reduce_scatter | solution.py:1059
  100.0 58.8 %copy-start.49 = (f32[128,2]{0,1:T(2,128)}, f32[128,2]{0,1:T(2,128)S(1)}, u32[]{:S(2)}) copy-start(f32[128,2]{0,1:T(2,128)S(1)} %select_reduce_fusion.3) | copy-start | bytes 3076
  100.0 58.7 %copy-start.57 = (f32[128]{0:T(128)}, f32[128]{0:T(128)S(1)}, u32[]{:S(2)}) copy-start(f32[128]{0:T(128)S(1)} %reduce_max.9) | copy-start | bytes 1540
  238.5 75.9 %copy-start.56 = (s32[128,2]{0,1:T(2,128)S(1)}, s32[128,2]{0,1:T(2,128)}, u32[]{:S(2)}) copy-start(s32[128,2]{0,1:T(2,128)} %copy-done.55) | copy-start | bytes 3076
  238.5 76.8 %copy-start.50 = (f32[128,2]{0,1:T(2,128)S(1)}, f32[128,2]{0,1:T(2,128)}, u32[]{:S(2)}) copy-start(f32[128,2]{0,1:T(2,128)} %copy-done.49) | copy-start | bytes 3076
  238.5 76.8 %copy-start.58 = (f32[128]{0:T(128)S(1)}, f32[128]{0:T(128)}, u32[]{:S(2)}) copy-start(f32[128]{0:T(128)} %copy-done.57) | copy-start | bytes 1540
  238.5 80.2 %copy-start.46 = (f32[768]{0:T(1024)S(1)}, f32[768]{0:T(1024)}, u32[]{:S(2)}) copy-start(f32[768]{0:T(1024)} %param.25) | copy-start | bytes 9220
  325.0 203.0 %all-reduce.7.cloned.1.call-start = ((), (), s32[]{:S(2)}) async-start(), calls=%async_computation.14 | async-start | bytes 1572864
  380.0 153.7 %reduce-scatter.16.cloned.1.call-start = ((), (), s32[]{:S(2)}) async-start(), calls=%async_computation.12 | async-start | bytes 491520 | tf_op jit(solution)/shard_map/reduce_scatter | solution.py:1076
  389.4 152.8 %reduce-scatter.12.cloned.1.call-start = ((), (), s32[]{:S(2)}) async-start(), calls=%async_computation.10 | async-start | bytes 737280 | tf_op jit(solution)/shard_map/reduce_scatter | solution.py:1059
  389.5 68.1 %copy-start.54 = (f32[768]{0:T(1024)S(1)}, f32[768]{0:T(1024)}, u32[]{:S(2)}) copy-start(f32[768]{0:T(1024)} %get-tuple-element.33) | copy-start | bytes 9220
  389.5 111.1 %copy-start.15 = (f32[128,768]{1,0:T(8,128)S(1)}, f32[128,768]{1,0:T(8,128)}, u32[]{:S(2)}) copy-start(f32[128,768]{1,0:T(8,128)} %copy-done.14) | copy-start | bytes 1179652
  506.5 42.0 %reduce-scatter.8.cloned.1.call-start = ((), (), s32[]{:S(2)}) async-start(), calls=%async_computation.8 | async-start | bytes 884736 | tf_op jit(solution)/shard_map/reduce_scatter | solution.py:1051
  530.1 8.6 %all-to-all-start = ((bf16[8,24,256]{2,1,0:T(8,128)(2,1)}), bf16[8,24,256]{2,1,0:T(8,128)(2,1)S(1)}, u32[]{:S(2)}, u32[]{:S(2)}) async-start(bf16[8,24,256]{2,1,0:T(8,128)(2,1)} %dynamic-slice_bitcast_fusion.4), calls=%async_computation.4 | async-start | bytes 196608 | tf_op jit(solution)/shard_map/all_to_all | solution.py:1073
  538.7 8.3 %all-to-all-start.1 = ((bf16[8,24,256]{2,1,0:T(8,128)(2,1)}), bf16[8,24,256]{2,1,0:T(8,128)(2,1)S(1)}, u32[]{:S(2)}, u32[]{:S(2)}) async-start(bf16[8,24,256]{2,1,0:T(8,128)(2,1)} %dynamic-slice_bitcast_fusion.3), calls=%async_computation.5 | async-start | bytes 196608 | tf_op jit(solution)/shard_map/all_to_all | solution.py:1073
  542.1 31.2 %reduce-scatter.14.cloned.1.call-start = ((), (), s32[]{:S(2)}) async-start(), calls=%async_computation.11 | async-start | bytes 184320 | tf_op jit(solution)/shard_map/reduce_scatter | solution.py:1059
  (57 other events, 512.5 us)
Sparse Core Ops, SparseCore 0:
  39.9 50.7 all-gather.5
  94.1 82.4 all-gather.3
  325.1 9.6 reduce-scatter.9
  380.1 52.7 all-reduce.6
  435.1 21.1 reduce-scatter.15
  506.6 24.9 reduce-scatter.11
  533.9 7.9 reduce-scatter.7
  545.2 19.7 reduce-scatter.13

commit v3 on v2

--- a/solution.py
+++ b/solution.py
@@ -19,6 +19,7 @@
 masked_value = -1e30
 PLANE = ("dp", "ctx")
 SLOT = ("ctx", "expert")
+AHEAD = 2
 bf16 = jnp.bfloat16
 f32 = jnp.float32
 
@@ -387,14 +388,13 @@
 
 
 def spread_kernel(
-    rows_ref, flat_ref, gate_ref, out_ref, gates_ref, z_send, z_recv, send, recv, pair_recv, gate_send,
+    rows_ref, flat_ref, gate_ref, out_ref, flats_ref, gates_ref, z_send, z_recv, send, recv, pair_recv, gate_send,
     gate_recv, gate_z_send, gate_z_recv, local_sem,
 ):
     dp_size, ctx_size, expert_size = (lax.axis_size(a) for a in ("dp", "ctx", "expert"))
     dp, ctx, expert = (lax.axis_index(a) for a in ("dp", "ctx", "expert"))
     chunk, rows = rows_ref.shape[1], flat_ref.shape[0]
     items, bits = plan(expert_size, ctx_size, chunk, rows)
-    plane_size = dp_size * ctx_size
     own = dp * ctx_size + ctx
 
     def z_at(step):
@@ -409,17 +409,17 @@
         + [{"dp": (dp + d) % dp_size, "ctx": flip(ctx, c)} for d, c in plane]
     )
 
-    def region(item):
-        step, first, size, _ = item
+    def landed(number, block):
+        step, first, size, _ = items[number]
         if step is None:
-            return pl.ds(expert_size * chunk + first, size)
-        return pl.ds(pl.multiple_of(z_from(step) * chunk, 16), size)
+            return flats_ref.at[block, pl.ds(first, size)]
+        return out_ref.at[block, z_from(step)]
 
     def z_copy(step, landing=False):
         place = z_from(step) if landing else expert
         return pltpu.make_async_remote_copy(
             src_ref=rows_ref.at[z_at(step)],
-            dst_ref=out_ref.at[own, pl.ds(pl.multiple_of(place * chunk, 16), chunk)],
+            dst_ref=out_ref.at[own, place],
             send_sem=z_send.at[step],
             recv_sem=z_recv.at[step],
             device_id={"expert": z_at(step)},
@@ -456,11 +456,11 @@
             return flat_ref.at[pl.ds(first, size)]
         if step == 0:
             return rows_ref.at[expert]
-        return out_ref.at[own, region(items[number])]
+        return landed(number, own)
 
     def passing(number, mask, bit, origin):
         block = dp * ctx_size + flip(ctx, mask)
-        here = out_ref.at[block, region(items[number])]
+        here = landed(number, block)
         return pltpu.make_async_remote_copy(
             src_ref=source(number) if origin else here,
             dst_ref=here,
@@ -472,7 +472,7 @@
 
     def crossing(number, mask, other, origin):
         block = dp * ctx_size + flip(ctx, mask)
-        here = out_ref.at[block, region(items[number])]
+        here = landed(number, block)
         return pltpu.make_async_remote_copy(
             src_ref=source(number) if origin else here,
             dst_ref=here,
@@ -484,7 +484,7 @@
 
     def arrived(number, mask):
         block = dp * ctx_size + flip(ctx, mask)
-        here = out_ref.at[block, region(items[number])]
+        here = landed(number, block)
         pltpu.make_async_remote_copy(
             src_ref=here, dst_ref=here, send_sem=send.at[0, 0, 0], recv_sem=recv.at[number, mask],
             device_id={"ctx": ctx}, device_id_type=MESH,
@@ -502,44 +502,50 @@
             one.start()
             started.append(one)
 
-    def forward(number):
+    def forward(number, place):
         order = items[number][3]
         masks = [0]
-        for place, bit in enumerate(order):
-            for mask in [m | bit for m in masks]:
-                arrived(number, mask)
-                for later in order[place + 1 :]:
-                    one = passing(number, mask, later, False)
-                    one.start()
-                    started.append(one)
-                for other in range(1, dp_size):
-                    one = crossing(number, mask, other, False)
-                    one.start()
-                    started.append(one)
+        for bit in order[:place]:
             masks = masks + [m | bit for m in masks]
+        for mask in [m | order[place] for m in masks]:
+            arrived(number, mask)
+            for later in order[place + 1 :]:
+                one = passing(number, mask, later, False)
+                one.start()
+                started.append(one)
+            for other in range(1, dp_size):
+                one = crossing(number, mask, other, False)
+                one.start()
+                started.append(one)
 
     ready = [0, expert_size, expert_size + 1]
-    for number in ready:
-        begin(number)
     kept = [
-        pltpu.make_async_copy(source(number), out_ref.at[own, region(items[number])], local_sem.at[i])
+        pltpu.make_async_copy(source(number), landed(number, own), local_sem.at[i])
         for i, number in enumerate(ready)
     ]
-    for one in kept:
-        one.start()
-    gates_ref[own, expert] = gate_ref[expert]
-    waiting = list(ready)
-    for step in range(1, expert_size):
-        z_copy(step, True).wait_recv()
-        begin(step)
-        waiting.append(step)
-        forward(waiting.pop(0))
-    for step in range(1, expert_size):
-        gate_z(step, True).wait_recv()
-    for d, c in plane:
-        gate_plane(d, c, own).start()
-    for number in waiting:
-        forward(number)
+    order = ready + list(range(1, expert_size))
+    depth = len(bits)
+    for tick in range(len(order) + AHEAD + depth):
+        for place in range(depth + 1):
+            index = tick if place == 0 else tick - AHEAD - place + 1
+            if not 0 <= index < len(order):
+                continue
+            number = order[index]
+            if place:
+                forward(number, place - 1)
+                continue
+            if number not in ready:
+                z_copy(number, True).wait_recv()
+            begin(number)
+            if index == len(ready) - 1:
+                for one in kept:
+                    one.start()
+                gates_ref[own, expert] = gate_ref[expert]
+            if index == len(order) - 1:
+                for step in range(1, expert_size):
+                    gate_z(step, True).wait_recv()
+                for d, c in plane:
+                    gate_plane(d, c, own).start()
     for d, c in plane:
         gate_plane(d, c, ((dp + d) % dp_size) * ctx_size + flip(ctx, c)).wait_recv()
         gate_plane(d, c, own).wait_send()
@@ -547,7 +553,7 @@
         for mask in range(ctx_size):
             for other in range(1, dp_size):
                 block = ((dp + dp_size - other) % dp_size) * ctx_size + flip(ctx, mask)
-                here = out_ref.at[block, region(items[number])]
+                here = landed(number, block)
                 pltpu.make_async_remote_copy(
                     src_ref=here, dst_ref=here, send_sem=send.at[0, 0, 0],
                     recv_sem=pair_recv.at[number, mask, other - 1], device_id={"dp": dp}, device_id_type=MESH,
@@ -566,15 +572,16 @@
     chunk, width = rows.shape[1:]
     count = expert_size + 2
     links = max(ctx_size.bit_length() - 1 + dp_size - 1, 1)
-    block = expert_size * chunk + flat.shape[0]
+    plane_size = dp_size * ctx_size
     return pl.pallas_call(
-        spread_kernel,
+        functools.partial(spread_kernel),
         out_shape=(
-            jax.ShapeDtypeStruct((dp_size * ctx_size, block, width), rows.dtype),
-            jax.ShapeDtypeStruct((dp_size * ctx_size,) + gate.shape, gate.dtype),
+            jax.ShapeDtypeStruct((plane_size,) + rows.shape, rows.dtype),
+            jax.ShapeDtypeStruct((plane_size,) + flat.shape, flat.dtype),
+            jax.ShapeDtypeStruct((plane_size,) + gate.shape, gate.dtype),
         ),
         in_specs=[VMEM, VMEM, VMEM],
-        out_specs=(ANY, VMEM),
+        out_specs=(ANY, ANY, VMEM),
         scratch_shapes=[
             DMA((expert_size,)),
             DMA((expert_size,)),
@@ -593,15 +600,39 @@
     )(rows, flat, gate)
 
 
-def home_kernel(
-    depth, part_ref, dot_ref, rows_ref, flat_ref, dots_ref, mine, theirs, dot_in, dot_sum, mine_sem,
-    pair_send, pair_recv, send, recv, z_send, z_recv, dot_send, dot_recv, dot_z_send, dot_z_recv,
-    *arrivals,
-):
+def pieces(kinds, expert_size, ctx_size):
+    bits = [1 << b for b in range(ctx_size.bit_length() - 1)]
+    moving, staying = [], []
+    for array, (by_expert, rows) in enumerate(kinds):
+        if by_expert:
+            for step in range(expert_size):
+                order = bits if (step + array) % 2 == 0 else bits[::-1]
+                (moving if step else staying).append((array, step, 0, rows, order))
+        else:
+            half = rows // 2
+            staying.append((array, None, 0, half, bits))
+            staying.append((array, None, half, rows - half, bits[::-1]))
+    return moving + staying, bits
+
+
+def home_kernel(kinds, has_dots, has_shared, depth, *refs):
+    rest = iter(refs)
+
+    def take(count):
+        return [next(rest) for _ in range(count)]
+
+    parts = take(len(kinds))
+    dot_ref = next(rest) if has_dots else None
+    grads = take(3) if has_shared else []
+    outs = take(len(kinds))
+    dots_ref = next(rest) if has_dots else None
+    grads_out = take(3) if has_shared else []
+    mine, theirs, mine_sem, pair_send, pair_recv, send, recv, z_send, z_recv = take(9)
+    arrivals = take(depth)
+
     dp_size, ctx_size, expert_size = (lax.axis_size(a) for a in ("dp", "ctx", "expert"))
     dp, ctx, expert = (lax.axis_index(a) for a in ("dp", "ctx", "expert"))
-    chunk, rows = rows_ref.shape[1], flat_ref.shape[0]
-    items, bits = plan(expert_size, ctx_size, chunk, rows)
+    items, _ = pieces(kinds, expert_size, ctx_size)
     own = dp * ctx_size + ctx
     other = (dp + 1) % dp_size
 
@@ -611,35 +642,39 @@
     def z_from(step):
         return (expert + expert_size - step) % expert_size
 
+    def plane_from(d, c):
+        return ((dp + dp_size - d) % dp_size) * ctx_size + flip(ctx, c)
+
+    def plane_at(d, c):
+        return ((dp + d) % dp_size) * ctx_size + flip(ctx, c)
+
     plane = [(d, c) for d in range(dp_size) for c in range(ctx_size) if (d, c) != (0, 0)]
-    greet(
-        [{"expert": z_at(step)} for step in range(1, expert_size)]
-        + [{"dp": (dp + d) % dp_size, "ctx": flip(ctx, c)} for d, c in plane]
-    )
-
-    def region(number):
-        step, start, size, _ = items[number]
-        if step is None:
-            return pl.ds(expert_size * chunk + start, size)
-        return pl.ds(pl.multiple_of(z_at(step) * chunk, 16), size)
+    partners = {(d, c): {"dp": (dp + d) % dp_size, "ctx": flip(ctx, c)} for d, c in plane}
+    greet([{"expert": z_at(step)} for step in range(1, expert_size)] + list(partners.values()))
 
     starts = [0]
     for item in items:
-        starts.append(starts[-1] + item[2])
+        starts.append(starts[-1] + item[3])
 
     def held(number):
-        return pl.ds(starts[number], items[number][2])
+        return pl.ds(starts[number], items[number][3])
+
+    def piece(number, block):
+        array, step, first, size, _ = items[number]
+        if step is None:
+            return parts[array].at[block, pl.ds(first, size)]
+        return parts[array].at[block, z_at(step)]
 
     def load(number, mask):
         return pltpu.make_async_copy(
-            part_ref.at[dp * ctx_size + flip(ctx, mask), region(number)],
+            piece(number, dp * ctx_size + flip(ctx, mask)),
             mine.at[mask, held(number)],
             mine_sem.at[number, mask],
         )
 
     def cross(number, mask):
         return pltpu.make_async_remote_copy(
-            src_ref=part_ref.at[other * ctx_size + flip(ctx, mask), region(number)],
+            src_ref=piece(number, other * ctx_size + flip(ctx, mask)),
             dst_ref=theirs.at[mask, held(number)],
             send_sem=pair_send.at[number, mask],
             recv_sem=pair_recv.at[number, mask],
@@ -647,60 +682,117 @@
             device_id_type=MESH,
         )
 
-    def dot_plane(d, c):
-        return pltpu.make_async_remote_copy(
-            src_ref=dot_ref.at[((dp + d) % dp_size) * ctx_size + flip(ctx, c)],
-            dst_ref=dot_in.at[d, c],
-            send_sem=dot_send.at[d, c],
-            recv_sem=dot_recv.at[d, c],
-            device_id={"dp": (dp + d) % dp_size, "ctx": flip(ctx, c)},
-            device_id_type=MESH,
-        )
-
-    def dot_z(step, landing=False):
-        return pltpu.make_async_remote_copy(
-            src_ref=dot_sum.at[z_at(step)],
-            dst_ref=dots_ref.at[z_from(step) if landing else expert],
-            send_sem=dot_z_send.at[step],
-            recv_sem=dot_z_recv.at[step],
-            device_id={"expert": z_at(step)},
-            device_id_type=MESH,
-        )
-
-    order = list(range(1, expert_size)) + [0, expert_size, expert_size + 1]
-    for number in order:
+    for number in range(len(items)):
         for mask in range(ctx_size):
             cross(number, mask).start()
             load(number, mask).start()
-    for d, c in plane:
-        dot_plane(d, c).start()
+
+    if has_dots:
+        dot_in, dot_sum, dot_send, dot_recv, dot_z_send, dot_z_recv = take(6)
+
+        def dot_plane(d, c):
+            return pltpu.make_async_remote_copy(
+                src_ref=dot_ref.at[plane_at(d, c)],
+                dst_ref=dot_in.at[d, c],
+                send_sem=dot_send.at[d, c],
+                recv_sem=dot_recv.at[d, c],
+                device_id=partners[d, c],
+                device_id_type=MESH,
+            )
+
+        def dot_z(step, landing=False):
+            return pltpu.make_async_remote_copy(
+                src_ref=dot_sum.at[z_at(step)],
+                dst_ref=dots_ref.at[z_from(step) if landing else expert],
+                send_sem=dot_z_send.at[step],
+                recv_sem=dot_z_recv.at[step],
+                device_id={"expert": z_at(step)},
+                device_id_type=MESH,
+            )
+
+        for d, c in plane:
+            dot_plane(d, c).start()
+
+    if has_shared:
+        grad_in, column_sum = take(3), take(2)
+        grad_send, grad_recv, column_send, column_recv, grad_sem = take(5)
+        part = grads[0].shape[2]
+
+        def grad_z(kind, step):
+            return pltpu.make_async_remote_copy(
+                src_ref=grads[kind].at[z_at(step)],
+                dst_ref=grad_in[kind].at[step],
+                send_sem=grad_send.at[kind, step],
+                recv_sem=grad_recv.at[kind, step],
+                device_id={"expert": z_at(step)},
+                device_id_type=MESH,
+            )
+
+        def grad_own(kind):
+            return pltpu.make_async_copy(
+                grads[kind].at[expert], grad_in[kind].at[0], grad_sem.at[kind]
+            )
+
+        def column(kind, d, c, landing=False):
+            at = plane_from(d, c) if landing else own
+            return pltpu.make_async_remote_copy(
+                src_ref=column_sum[kind].at[plane_at(d, c)],
+                dst_ref=grads_out[kind].at[:, pl.ds(pl.multiple_of(at * part, 128), part)],
+                send_sem=column_send.at[kind, d, c],
+                recv_sem=column_recv.at[kind, d, c],
+                device_id=partners[d, c],
+                device_id_type=MESH,
+            )
+
+        for kind in range(3):
+            grad_own(kind).start()
+            for step in range(1, expert_size):
+                grad_z(kind, step).start()
+
+        def sum_grads():
+            for kind in range(3):
+                grad_own(kind).wait()
+                total = grad_in[kind][0].astype(f32)
+                for step in range(1, expert_size):
+                    grad_z(kind, step).wait_recv()
+                    total = total + grad_in[kind][step].astype(f32)
+                if kind == 2:
+                    grads_out[2][...] = total
+                    continue
+                shard = grads_out[kind].shape[0]
+                for block in range(dp_size * ctx_size):
+                    column_sum[kind][block] = total[block * shard : (block + 1) * shard]
+                for d, c in plane:
+                    column(kind, d, c).start()
+                here = pl.ds(pl.multiple_of(own * part, 128), part)
+                grads_out[kind][:, here] = column_sum[kind][own]
 
     def stage(number, place):
-        order = items[number][3][::-1]
+        order = items[number][4][::-1]
         done = sum(order[:place])
         bit = order[place]
-        rest = [m for m in range(ctx_size) if not m & (done | bit)]
-        return bit, [(m | bit, m) for m in rest]
+        kept = [m for m in range(ctx_size) if not m & (done | bit)]
+        return bit, [(m | bit, m) for m in kept]
 
     def hop(number, place, index):
         bit, moves = stage(number, place)
-        source = moves[index][0]
         return pltpu.make_async_remote_copy(
-            src_ref=mine.at[source, held(number)],
+            src_ref=mine.at[moves[index][0], held(number)],
             dst_ref=arrivals[place].at[index, held(number)],
-            send_sem=send.at[number, source],
+            send_sem=send.at[number, moves[index][0]],
             recv_sem=recv.at[number, place, index],
             device_id={"ctx": flip(ctx, bit)},
             device_id_type=MESH,
         )
 
     def z_copy(number, landing=False):
+        array, step = items[number][:2]
         return pltpu.make_async_remote_copy(
             src_ref=mine.at[0, held(number)],
-            dst_ref=rows_ref.at[z_from(number) if landing else expert],
+            dst_ref=outs[array].at[z_from(step) if landing else expert],
             send_sem=z_send.at[number],
             recv_sem=z_recv.at[number],
-            device_id={"expert": z_at(number)},
+            device_id={"expert": z_at(step)},
             device_id_type=MESH,
         )
 
@@ -718,33 +810,31 @@
                 hop(number, 0, leaving.index(mask)).start()
 
     def step(number, place):
-        _, moves = stage(number, place)
-        for index, (_, target) in enumerate(moves):
+        targets = [target for _, target in stage(number, place)[1]]
+        leaving = []
+        if place + 1 < depth:
+            leaving = [source for source, _ in stage(number, place + 1)[1]]
+        for index in range(len(targets)):
             hop(number, place, index).wait_recv()
-        following = stage(number, place + 1)[1] if place + 1 < depth else []
-        leaving = [source for source, _ in following]
-        targets = [target for _, target in moves]
         for mask in leaving + [m for m in targets if m not in leaving]:
             add(number, mask, arrivals[place], targets.index(mask))
             if mask in leaving:
                 hop(number, place + 1, leaving.index(mask)).start()
 
     def finish(number):
-        kind = items[number][0]
-        if kind is None:
-            start, size = items[number][1], items[number][2]
-            flat_ref[pl.ds(start, size)] = mine[0, held(number)]
-        elif kind == 0:
-            rows_ref[expert] = mine[0, held(number)]
+        array, step_z, first, size, _ = items[number]
+        if step_z is None:
+            outs[array][pl.ds(first, size)] = mine[0, held(number)]
+        elif step_z == 0:
+            outs[array][expert] = mine[0, held(number)]
         else:
             z_copy(number).start()
 
-    for tick in range(len(order) + depth):
-        for place in reversed(range(depth + 1)):
-            index = tick - place
-            if not 0 <= index < len(order):
+    for tick in range(len(items) + AHEAD + depth):
+        for place in range(depth + 1):
+            number = tick if place == 0 else tick - AHEAD - place + 1
+            if not 0 <= number < len(items):
                 continue
-            number = order[index]
             if place == 0:
                 pair(number)
             else:
@@ -752,24 +842,38 @@
             if place == depth:
                 finish(number)
 
-    total_dots = dot_ref[own]
-    for d, c in plane:
-        dot_plane(d, c).wait_recv()
-        total_dots = total_dots + dot_in[d, c]
-    dot_sum[...] = total_dots
-    for number in range(1, expert_size):
-        dot_z(number).start()
-    dots_ref[expert] = dot_sum[expert]
-
-    for number in range(1, expert_size):
+    if has_dots:
+        total = dot_ref[own]
+        for d, c in plane:
+            dot_plane(d, c).wait_recv()
+            total = total + dot_in[d, c]
+        dot_sum[...] = total
+        for step_z in range(1, expert_size):
+            dot_z(step_z).start()
+        dots_ref[expert] = dot_sum[expert]
+    if has_shared:
+        sum_grads()
+
+    moving = [n for n in range(len(items)) if items[n][1]]
+    for number in moving:
         z_copy(number, True).wait_recv()
-        dot_z(number, True).wait_recv()
-    for number in range(1, expert_size):
+    if has_dots:
+        for step_z in range(1, expert_size):
+            dot_z(step_z, True).wait_recv()
+            dot_z(step_z).wait_send()
+        for d, c in plane:
+            dot_plane(d, c).wait_send()
+    if has_shared:
+        for kind in range(3):
+            for step_z in range(1, expert_size):
+                grad_z(kind, step_z).wait_send()
+            if kind < 2:
+                for d, c in plane:
+                    column(kind, d, c, True).wait_recv()
+                    column(kind, d, c).wait_send()
+    for number in moving:
         z_copy(number).wait_send()
-        dot_z(number).wait_send()
-    for d, c in plane:
-        dot_plane(d, c).wait_send()
-    for number in order:
+    for number in range(len(items)):
         for mask in range(ctx_size):
             cross(number, mask).wait_send()
         for place in range(depth):
@@ -777,44 +881,259 @@
                 hop(number, place, index).wait_send()
 
 
-def bring_home(part, dots, rows, sizes, number):
+def bring_home(parts, sizes, number, dots=None, grads=None):
     dp_size, ctx_size, expert_size = sizes
-    block, width = part.shape[1:]
-    chunk = (block - rows) // expert_size
-    count = expert_size + 2
-    depth = ctx_size.bit_length() - 1
-    buffer = (ctx_size, block, width)
-    return pl.pallas_call(
-        functools.partial(home_kernel, depth),
-        out_shape=(
-            jax.ShapeDtypeStruct((expert_size, chunk, width), part.dtype),
-            jax.ShapeDtypeStruct((rows, width), part.dtype),
-            jax.ShapeDtypeStruct(dots.shape[1:], dots.dtype),
-        ),
-        in_specs=[ANY, VMEM],
-        out_specs=(VMEM, VMEM, VMEM),
-        scratch_shapes=[
-            pltpu.VMEM(buffer, part.dtype),
-            pltpu.VMEM(buffer, part.dtype),
+    assert dp_size == 2
+    width, dtype = parts[0].shape[-1], parts[0].dtype
+    kinds = tuple((part.ndim == 4, part.shape[-2]) for part in parts)
+    items, bits = pieces(kinds, expert_size, ctx_size)
+    count, depth = len(items), len(bits)
+    buffer = (ctx_size, sum(item[3] for item in items), width)
+    out_shape = [jax.ShapeDtypeStruct(part.shape[1:], dtype) for part in parts]
+    operands, in_specs = list(parts), [ANY] * len(parts)
+    scratch = [
+        pltpu.VMEM(buffer, dtype),
+        pltpu.VMEM(buffer, dtype),
+        DMA((count, ctx_size)),
+        DMA((count, ctx_size)),
+        DMA((count, ctx_size)),
+        DMA((count, ctx_size)),
+        DMA((count, depth, max(ctx_size // 2, 1))),
+        DMA((count,)),
+        DMA((count,)),
+    ]
+    scratch += [pltpu.VMEM((ctx_size >> (place + 1),) + buffer[1:], dtype) for place in range(depth)]
+    if dots is not None:
+        operands.append(dots)
+        in_specs.append(VMEM)
+        out_shape.append(jax.ShapeDtypeStruct(dots.shape[1:], dots.dtype))
+        scratch += [
             pltpu.VMEM((dp_size, ctx_size) + dots.shape[1:], dots.dtype),
             pltpu.VMEM(dots.shape[1:], dots.dtype),
-            DMA((count, ctx_size)),
-            DMA((count, ctx_size)),
-            DMA((count, ctx_size)),
-            DMA((count, ctx_size)),
-            DMA((count, depth, max(ctx_size // 2, 1))),
-            DMA((count,)),
-            DMA((count,)),
             DMA((dp_size, ctx_size)),
             DMA((dp_size, ctx_size)),
             DMA((expert_size,)),
             DMA((expert_size,)),
         ]
-        + [pltpu.VMEM((ctx_size >> (place + 1),) + buffer[1:], part.dtype) for place in range(depth)],
+    if grads is not None:
+        operands += list(grads)
+        in_specs += [ANY] * 3
+        plane_size, part = dp_size * ctx_size, grads[0].shape[2]
+        shard = grads[0].shape[1] // plane_size
+        columns = jax.ShapeDtypeStruct((shard, plane_size * part), f32)
+        out_shape += [columns, columns, jax.ShapeDtypeStruct(grads[2].shape[1:], f32)]
+        scratch += [pltpu.VMEM(grad.shape, grad.dtype) for grad in grads]
+        scratch += [pltpu.VMEM((plane_size, shard, part), f32)] * 2
+        scratch += [
+            DMA((3, expert_size)),
+            DMA((3, expert_size)),
+            DMA((2, dp_size, ctx_size)),
+            DMA((2, dp_size, ctx_size)),
+            DMA((3,)),
+        ]
+    return pl.pallas_call(
+        functools.partial(home_kernel, kinds, dots is not None, grads is not None, depth),
+        out_shape=out_shape,
+        in_specs=in_specs,
+        out_specs=[VMEM] * len(out_shape),
+        scratch_shapes=scratch,
         compiler_params=pltpu.CompilerParams(
-            collective_id=number, has_side_effects=True, vmem_limit_bytes=56 << 20
+            collective_id=number, has_side_effects=True, vmem_limit_bytes=58 << 20
         ),
-    )(part, dots)
+    )(*operands)
+
+
+NT = (((1,), (1,)), ((), ()))
+TN = (((0,), (0,)), ((), ()))
+
+
+def contract(a, b, dims=(((1,), (0,)), ((), ()))):
+    return lax.dot_general(a, b, dims, preferred_element_type=f32)
+
+
+def branch(rows, d_out, gate_w, up_w, down_w):
+    gate_lin, up_lin = contract(rows, gate_w), contract(rows, up_w)
+    sigmoid = 1.0 / (1.0 + jnp.exp(-gate_lin))
+    silu = gate_lin * sigmoid
+    hidden = (silu * up_lin).astype(bf16)
+    d_hidden = contract(d_out, down_w, NT)
+    d_gate = (d_hidden * up_lin * (sigmoid + silu * (1.0 - sigmoid))).astype(bf16)
+    d_up = (d_hidden * silu).astype(bf16)
+    result = contract(hidden, down_w)
+    d_rows = contract(d_gate, gate_w, NT) + contract(d_up, up_w, NT)
+    d_lin = contract(rows, jnp.concatenate([d_gate, d_up], axis=1), TN)
+    d_down = contract(hidden, d_out, TN)
+    return result, d_rows, d_lin, d_down
+
+
+def experts_kernel(
+    plane_ref, rows_ref, up_ref, scale_ref, gate_w, up_w, down_w, result_ref, d_rows_ref, dots_ref, gate_grad,
+    up_grad, down_grad, rows_f32, up_f32,
+):
+    planes, expert_size = rows_ref.shape[:2]
+    sources = planes * expert_size
+    group, width, part = gate_w.shape
+    rows_in = rows_ref.at[:, :, 0]
+
+    @pl.when(pl.program_id(1) == 0)
+    def _():
+        for grad in (gate_grad, up_grad, down_grad):
+            grad[...] = jnp.zeros_like(grad)
+
+    def unpack(source, carry):
+        there = pl.ds(pl.multiple_of(source * PLACES, 8), PLACES)
+        at = source // expert_size, source % expert_size
+        rows, up = rows_in[at].astype(f32), up_ref.at[:, :, 0][at].astype(f32)
+        for i in range(group):
+            rows_f32[i, there] = rows[i * PLACES : (i + 1) * PLACES]
+            up_f32[i, there] = up[i * PLACES : (i + 1) * PLACES]
+        return carry
+
+    lax.fori_loop(0, sources, unpack, 0)
+    for i in range(group):
+        rows, up = rows_f32[i].astype(bf16), up_f32[i]
+        scale = scale_ref[i][:, :, None]
+        by_source = (sources, PLACES, width)
+        d_out = (up.reshape(by_source) * scale).reshape(up.shape).astype(bf16)
+        result, d_rows, d_lin, d_down = branch(rows, d_out, gate_w[i], up_w[i], down_w[i])
+        gate_grad[i] += d_lin[:, :part]
+        up_grad[i] += d_lin[:, part:]
+        down_grad[i] += d_down
+        dots_ref[i] = jnp.sum((result * up).reshape(by_source), axis=-1)
+        up_f32[i] = (result.reshape(by_source) * scale).reshape(up.shape)
+        rows_f32[i] = d_rows
+
+    def pack(source, carry):
+        there = pl.ds(pl.multiple_of(source * PLACES, 8), PLACES)
+        at = source // expert_size, source % expert_size
+        result_ref.at[:, :, 0][at] = jnp.concatenate([up_f32[i, there] for i in range(group)]).astype(bf16)
+        d_rows_ref.at[:, :, 0][at] = jnp.concatenate([rows_f32[i, there] for i in range(group)]).astype(bf16)
+        return carry
+
+    lax.fori_loop(0, sources, pack, 0)
+
+
+def experts(plane, rows, up, scale, gate_w, up_w, down_w):
+    plane_size, expert_size, chunk, width = rows.shape
+    own, sources = scale.shape[:2]
+    part = gate_w.shape[2] // plane_size
+    group = 2
+    planes = max(16 // expert_size, 1)
+    steps = plane_size // planes
+    paired = (plane_size, expert_size, own // group, group * PLACES, width)
+    rows_spec = pl.BlockSpec((planes, expert_size, 1) + paired[3:], lambda g, c, p: (c, 0, g, 0, 0))
+    dots_spec = pl.BlockSpec((group, sources // steps, PLACES), lambda g, c, p: (g, c, 0))
+    column = lambda g, c, p: (g, 0, p[0])
+    whole = lambda g, c, p: (g, 0, 0)
+    result, d_rows, dots, *grads = pl.pallas_call(
+        experts_kernel,
+        grid_spec=pltpu.PrefetchScalarGridSpec(
+            num_scalar_prefetch=1,
+            grid=(own // group, steps),
+            in_specs=[
+                rows_spec,
+                rows_spec,
+                dots_spec,
+                pl.BlockSpec((group, width, part), column),
+                pl.BlockSpec((group, width, part), column),
+                pl.BlockSpec((group, part, width), lambda g, c, p: (g, p[0], 0)),
+            ],
+            out_specs=[
+                rows_spec,
+                rows_spec,
+                dots_spec,
+                pl.BlockSpec((group, width, part), whole),
+                pl.BlockSpec((group, width, part), whole),
+                pl.BlockSpec((group, part, width), whole),
+            ],
+            scratch_shapes=[
+                pltpu.VMEM((group, sources // steps * PLACES, width), f32),
+                pltpu.VMEM((group, sources // steps * PLACES, width), f32),
+            ],
+        ),
+        out_shape=[
+            jax.ShapeDtypeStruct(paired, bf16),
+            jax.ShapeDtypeStruct(paired, bf16),
+            jax.ShapeDtypeStruct(scale.shape, f32),
+            jax.ShapeDtypeStruct((own, width, part), f32),
+            jax.ShapeDtypeStruct((own, width, part), f32),
+            jax.ShapeDtypeStruct((own, part, width), f32),
+        ],
+        compiler_params=pltpu.CompilerParams(vmem_limit_bytes=62 << 20),
+    )(plane, rows.reshape(paired), up.reshape(paired), scale, gate_w, up_w, down_w)
+    return result.reshape(rows.shape), d_rows.reshape(rows.shape), dots, grads
+
+
+def shared_kernel(
+    plane_size, plane_ref, rows_ref, up_ref, gate_w, up_w, down_w, result_ref, d_rows_ref, gate_grad, up_grad,
+    down_grad, lin_sum, down_sum,
+):
+    planes, rows, width = rows_ref.shape
+    expert_size, column, part = gate_grad.shape
+    shard = column // plane_size
+    flat = (planes * rows, width)
+    result, d_rows, d_lin, d_down = branch(
+        rows_ref[...].reshape(flat), up_ref[...].reshape(flat), gate_w[...], up_w[...], down_w[...]
+    )
+    result_ref[...] = result.reshape(rows_ref.shape).astype(bf16)
+    d_rows_ref[...] = d_rows.reshape(rows_ref.shape).astype(bf16)
+
+    @pl.when(pl.program_id(0) == 0)
+    def _():
+        lin_sum[...] = jnp.zeros_like(lin_sum)
+        down_sum[...] = jnp.zeros_like(down_sum)
+
+    lin_sum[...] += d_lin
+    down_sum[...] += d_down
+
+    @pl.when(pl.program_id(0) == pl.num_programs(0) - 1)
+    def _():
+        for z in range(expert_size):
+            firsts = [(p * expert_size + z) * shard for p in range(plane_size)]
+            mine = jnp.concatenate([lin_sum[first : first + shard] for first in firsts]).astype(bf16)
+            gate_grad[z] = mine[:, :part]
+            up_grad[z] = mine[:, part:]
+        down_grad[...] = down_sum[...].astype(bf16).reshape(down_grad.shape)
+
+
+def shared(plane, rows, up, gate_w, up_w, down_w, expert_size):
+    plane_size, count, width = rows.shape
+    hidden_width = gate_w.shape[1]
+    part = hidden_width // plane_size
+    planes = 4
+    flat = pl.BlockSpec((planes, count, width), lambda c, p: (c, 0, 0))
+    columns = (expert_size, width // expert_size, part)
+    down = (expert_size, part // expert_size, width)
+    return pl.pallas_call(
+        functools.partial(shared_kernel, plane_size),
+        grid_spec=pltpu.PrefetchScalarGridSpec(
+            num_scalar_prefetch=1,
+            grid=(plane_size // planes,),
+            in_specs=[
+                flat,
+                flat,
+                pl.BlockSpec((width, part), lambda c, p: (0, p[0])),
+                pl.BlockSpec((width, part), lambda c, p: (0, p[0])),
+                pl.BlockSpec((part, width), lambda c, p: (p[0], 0)),
+            ],
+            out_specs=[
+                flat,
+                flat,
+                pl.BlockSpec(columns, lambda c, p: (0, 0, 0)),
+                pl.BlockSpec(columns, lambda c, p: (0, 0, 0)),
+                pl.BlockSpec(down, lambda c, p: (0, 0, 0)),
+            ],
+            scratch_shapes=[pltpu.VMEM((width, 2 * part), f32), pltpu.VMEM((part, width), f32)],
+        ),
+        out_shape=[
+            jax.ShapeDtypeStruct(rows.shape, bf16),
+            jax.ShapeDtypeStruct(rows.shape, bf16),
+            jax.ShapeDtypeStruct(columns, bf16),
+            jax.ShapeDtypeStruct(columns, bf16),
+            jax.ShapeDtypeStruct(down, bf16),
+        ],
+        compiler_params=pltpu.CompilerParams(vmem_limit_bytes=58 << 20),
+    )(plane, rows, up, gate_w, up_w, down_w)
 
 
 def local(
@@ -841,8 +1160,6 @@
     rows, width = tokens.shape[1:]
     heads = width // HEAD_DIM
     own = EXPERTS // expert_size
-    hidden_width = expert_gate.shape[2]
-    part = hidden_width // plane_size
     plane = lax.axis_index("dp") * ctx_size + lax.axis_index("ctx")
     first_row = (lax.axis_index("ctx") * expert_size + lax.axis_index("expert")) * rows
     positions = first_row + jnp.arange(rows, dtype=jnp.int32)
@@ -885,8 +1202,8 @@
             taken.append(lax.ppermute(sent, "expert", ring))
         return jnp.take(jnp.stack(taken), (here - jnp.arange(expert_size)) % expert_size, axis=0)
 
-    up_mine = to_experts(place_rows(d_branch_low)).reshape(-1, width)
-    up_all = lax.all_gather(jnp.concatenate([up_mine, d_branch_low], axis=0), PLANE, axis=0)
+    up_rows = lax.all_gather(to_experts(place_rows(d_branch_low)), PLANE, axis=0)
+    up_flat = lax.all_gather(d_branch_low, PLANE, axis=0)
 
     scale_one = rms_scale(inputs)
     normal_one = inputs * scale_one
@@ -944,74 +1261,26 @@
     def flat_row(tile):
         return tile[..., 0, : own * PLACES].reshape(tile.shape[:-3] + (placed_rows,))
 
-    in_all, gate_all = spread(place_rows(normed_two_low), normed_two_low, tiled(gate_rows), sizes, 3)
-    gate_all = flat_row(gate_all)
-
-    def by_expert(both):
-        cut = both[:, :placed_rows].reshape((plane_size * expert_size, own, PLACES) + both.shape[2:])
-        return jnp.swapaxes(cut, 0, 1).reshape((own, -1) + both.shape[2:])
-
-    def by_source(flat):
-        cut = flat.reshape((own, plane_size * expert_size, PLACES) + flat.shape[2:])
-        return jnp.swapaxes(cut, 0, 1).reshape((plane_size, placed_rows) + flat.shape[2:])
-
-    def column(weight):
-        return lax.dynamic_slice_in_dim(weight, plane * part, part, weight.ndim - 1)
-
-    def row(weight):
-        return lax.dynamic_slice_in_dim(weight, plane * part, part, weight.ndim - 2)
-
-    def branch(rows_in, up, gate_w, up_w, down_w, weight):
-        def dot(spec, a, b):
-            return jnp.einsum(spec, a, b, preferred_element_type=f32)
-
-        gate_lin, up_lin = dot("erd,edf->erf", rows_in, gate_w), dot("erd,edf->erf", rows_in, up_w)
-        sigmoid = 1.0 / (1.0 + jnp.exp(-gate_lin))
-        silu = gate_lin * sigmoid
-        hidden = (silu * up_lin).astype(bf16)
-        result = dot("erf,efd->erd", hidden, down_w)
-        d_out = (weight * up.astype(f32)).astype(bf16)
-        d_hidden = dot("erd,efd->erf", d_out, down_w)
-        d_gate = (d_hidden * up_lin * (sigmoid + silu * (1.0 - sigmoid))).astype(bf16)
-        d_up = (d_hidden * silu).astype(bf16)
-        d_in = dot("erf,edf->erd", d_gate, gate_w) + dot("erf,edf->erd", d_up, up_w)
-        grads = (
-            dot("erd,erf->edf", rows_in, d_gate),
-            dot("erd,erf->edf", rows_in, d_up),
-            dot("erf,erd->efd", hidden, d_out),
-        )
-        return result, d_in, grads
-
-    gate_factor = by_expert(gate_all)[:, :, None]
-    up_rows = by_expert(up_all)
-    result, d_rows, expert_grads = branch(
-        by_expert(in_all), up_rows, column(expert_gate), column(expert_up), row(expert_down),
-        gate_factor,
-    )
-    d_gate_part = by_source(jnp.sum(result * up_rows.astype(f32), axis=-1))
-    shared_result, shared_d, shared_grads = branch(
-        in_all[:, placed_rows:].reshape(1, -1, width),
-        up_all[:, placed_rows:].reshape(1, -1, width),
-        column(shared_gate)[None],
-        column(shared_up)[None],
-        row(shared_down)[None],
-        1.0,
-    )
-
-    def joined(expert_part, shared_part):
-        return jnp.concatenate(
-            [by_source(expert_part), shared_part.reshape(plane_size, rows, width)], axis=1
-        ).astype(bf16)
+    in_rows, in_flat, gate_all = spread(
+        place_rows(normed_two_low), normed_two_low, tiled(gate_rows), sizes, 3
+    )
+    sources = plane_size * expert_size
+    scale = jnp.swapaxes(flat_row(gate_all).reshape(sources, own, PLACES), 0, 1)
+    plane_at = plane.astype(jnp.int32)[None]
+    shared_result, shared_d, *shared_grads = shared(
+        plane_at, in_flat, up_flat, shared_gate, shared_up, shared_down, expert_size
+    )
+    result, d_rows, dots, expert_grads = experts(
+        plane_at, in_rows, up_rows, scale, expert_gate, expert_up, expert_down
+    )
+    dots = tiled(jnp.swapaxes(dots, 0, 1).reshape(plane_size, placed_rows))
 
     def collect(back, flat):
         spread_rows = jnp.dot(either, back.reshape(placed_rows, width), preferred_element_type=f32)
         return spread_rows + flat.astype(f32)
 
-    back, flat, d_gate_rows = bring_home(joined(d_rows, shared_d), tiled(d_gate_part), rows, sizes, 4)
+    back, flat, d_gate_rows = bring_home([d_rows, shared_d], sizes, 4, dots=dots)
     d_gate_rows = flat_row(d_gate_rows)
-    out_back, out_flat, _ = bring_home(
-        joined(result * gate_factor, shared_result), tiled(d_gate_part), rows, sizes, 5
-    )
     d_gates = jnp.sum(jnp.where(dispatch, d_gate_rows, 0.0), axis=-1)
     d_chosen = gate_weights * (
         d_gates - jnp.sum(gate_weights * d_gates, axis=-1, keepdims=True)
@@ -1021,8 +1290,6 @@
     d_normed_two = collect(back, flat) + jnp.einsum(
         "te,de->td", d_logits, router_weight, preferred_element_type=f32
     )
-    output_rows = hidden_in + valid * collect(out_back, out_flat)
-    output_rows = output_rows.astype(bf16)[None]
     d_gain_two = jnp.sum(d_normed_two * normal_two, axis=0)
     d_hidden_in = upstream + rms_back(normal_two, scale_two, norm2_gain, d_normed_two)
 
@@ -1033,6 +1300,26 @@
     all_cosine, all_sine = rope_tables(jnp.arange(slot_size * rows, dtype=jnp.int32))
     d_qkv = attend_back(qkv, lengths, out_t, log_total, d_attended, all_cosine, all_sine)
     d_mine = from_heads(d_qkv, 7)
+
+    shard = width // (dp_size * slot_size)
+    devices = (plane_size, expert_size)
+    small = jnp.concatenate(
+        [
+            d_router.reshape(devices + (1, shard * EXPERTS)),
+            d_gain_two.reshape(devices + (1, shard)),
+            jnp.zeros(devices + (1, width - shard * (EXPERTS + 1)), f32),
+        ],
+        axis=-1,
+    )
+    extra = jnp.concatenate([d_output_weight.reshape(devices + (shard, width)), small], axis=2)
+    extra = jnp.pad(extra, [(0, 0), (0, 0), (0, -(shard + 1) % 16), (0, 0)]).astype(bf16)
+    out_back, out_flat, extra, shared_gate_grad, shared_up_grad, shared_down_grad = bring_home(
+        [result, shared_result, extra], sizes, 5, grads=shared_grads
+    )
+    extra = jnp.sum(extra.astype(f32), axis=0)
+    output_rows = hidden_in + valid * collect(out_back, out_flat)
+    output_rows = output_rows.astype(bf16)[None]
+
     head_grad = jnp.einsum(
         "bet,btd->ed", d_qkv, normed_all.reshape(slot_size, rows, width), preferred_element_type=f32
     )
@@ -1046,51 +1333,28 @@
     input_grad = d_hidden_in + rms_back(normal_one, scale_one, norm1_gain, d_normed)
     input_grad = input_grad.astype(bf16)[None]
 
-    shard = width // (dp_size * slot_size)
     head_grad = jnp.transpose(head_grad).reshape(-1, 3 * HEAD_DIM)
     head_grad = lax.psum_scatter(head_grad, "dp", scatter_dimension=0, tiled=True)
     head_grad = from_heads(head_grad.reshape(slot_size, shard, 3 * HEAD_DIM), 8)
     head_grad = jnp.transpose(
         head_grad.reshape(heads, shard, 3, HEAD_DIM), (2, 1, 0, 3)
     ).reshape(3, shard, width)
-
-    def scatter(grad):
-        for axis in ("dp", "ctx", "expert"):
-            grad = lax.psum_scatter(grad, axis, scatter_dimension=0, tiled=True)
-        return grad
-
-    output_grad = scatter(d_output_weight.astype(bf16)).astype(f32)
-    small = lax.psum(
-        jnp.concatenate([d_router, d_gain_one[:, None], d_gain_two[:, None]], axis=1),
-        ("dp", "ctx", "expert"),
-    )
     linear = plane * expert_size + lax.axis_index("expert")
-    small = lax.dynamic_slice_in_dim(small, linear * shard, shard, 0)
-
-    def shared_columns(grad):
-        grad = grad[0].reshape(plane_size, expert_size, shard, part).astype(bf16)
-        grad = lax.psum_scatter(grad, "expert", scatter_dimension=1, tiled=True)[:, 0]
-        grad = lax.all_to_all(grad, PLANE, 0, 0)
-        return jnp.swapaxes(grad, 0, 1).reshape(shard, hidden_width).astype(f32)
-
-    shared_down_grad = lax.psum_scatter(
-        shared_grads[2][0].astype(bf16), "expert", scatter_dimension=0, tiled=True
-    ).astype(f32)
+    d_gain_one = lax.psum(d_gain_one, ("dp", "ctx", "expert"))
+    d_gain_one = lax.dynamic_slice_in_dim(d_gain_one, linear * shard, shard, 0)
     return (
         output_rows,
         input_grad,
-        small[:, EXPERTS],
+        d_gain_one,
         head_grad[0],
         head_grad[1],
         head_grad[2],
-        output_grad,
-        small[:, EXPERTS + 1],
-        small[:, :EXPERTS],
-        expert_grads[0],
-        expert_grads[1],
-        expert_grads[2],
-        shared_columns(shared_grads[0]),
-        shared_columns(shared_grads[1]),
+        extra[:shard],
+        extra[shard, shard * EXPERTS : shard * (EXPERTS + 1)],
+        extra[shard, : shard * EXPERTS].reshape(shard, EXPERTS),
+        *expert_grads,
+        shared_gate_grad,
+        shared_up_grad,
         shared_down_grad,
     )
 

time: 589 us -> 383 us (0.65); the launches traced: 582 us -> 383 us
  matrix products: 92.2 us -> 18.7 us
  local copies, waits for them, and re-layouts: 81 us -> 25.2 us
  other arithmetic: 43.8 us -> 11.1 us
  Pallas kernels: 278 us -> 258 us
  waiting for transfers between devices: 16.3 us -> 8.41 us
  starting transfers between devices: 13.3 us -> 7.18 us
    dot_general x18 -> x0, matrix products: 65.5 us -> none  [dot(): return jnp.einsum(spec, a, b, preferred_element_type=f32)]
    pallas_call x3 -> x5, Pallas kernels: 193 us -> 169 us  [the longest x2 98.1 us: bring_home(): pl.pallas_call(functools.partial(home_kernel, kinds, dots is not None, gr...]
    slice x6 -> x3, local copies, waits for them, and re-layouts: 10.6 us -> 0.84 us  [the longest x1 0.64 us: local(): extra[:shard]]
    concatenate x4 -> x1, other arithmetic: 10.6 us -> 1.61 us  [local(): jnp.concatenate([d_output_weight.reshape(devices + (shard, width)), small...]
    convert_element_type x3 -> x0, other arithmetic: 7.86 us -> none  [the longest x1 4.87 us: local(): d_gate_part = by_source(jnp.sum(result * up_rows.astype(f32), axis=-1))]
    all_to_all x2 -> x0, starting transfers between devices: 6.92 us -> none  [shared_columns(): grad = lax.all_to_all(grad, PLANE, 0, 0)]
    transpose x3 -> x1, local copies, waits for them, and re-layouts: 7.74 us -> 0.88 us  [local(): dots = tiled(jnp.swapaxes(dots, 0, 1).reshape(plane_size, placed_rows))]
    unnamed x6 -> x4, other arithmetic: 6.9 us -> 0.18 us
  transfers between devices with their start and end apart: 13 -> 7, of which waited for: 4 -> 2; matrix products, arithmetic and copies ran while one was open for 33% -> 10% of each run, Pallas kernels for 48% -> 64%
where the time goes in v3:
time: 383 us
  Pallas kernels  258 us (67%)
  blocking collectives  38.3 us (10%)
  local copies, waits for them, and re-layouts  25.2 us (7%)
  matrix products  18.7 us (5%)
  between operations  15.5 us (4%)
  other arithmetic  11.1 us (3%)
  waiting for transfers between devices  8.41 us (2%)
  starting transfers between devices  7.18 us (2%)
    pallas_call x2, Pallas kernels, bring_home(): pl.pallas_call(functools.partial(home_kernel, kinds, dots is not None, gr...  98.1 us
    pallas_call x5, Pallas kernels, trade(): pl.pallas_call(functools.partial(trade_kernel, heads, inward), out_shape=...  70.6 us
    pallas_call x1, Pallas kernels, spread(): pl.pallas_call(functools.partial(spread_kernel), out_shape=(jax.ShapeDtyp...  38.8 us
    psum x1, blocking collectives, local(): d_gain_one = lax.psum(d_gain_one, ('dp', 'ctx', 'expert'))  38.3 us
    pallas_call x1, Pallas kernels, experts(): pl.pallas_call(experts_kernel, grid_spec=pltpu.PrefetchScalarGridSpec(num...  23.8 us
    pallas_call x1, Pallas kernels, attend_back(): pl.pallas_call(functools.partial(attend_back_kernel, step), out_shape=jax...  12.3 us
    unnamed x77, local copies, waits for them, and re-layouts  10.4 us
    ppermute x3, waiting for transfers between devices, to_experts(): taken.append(lax.ppermute(sent, 'expert', ring))  8.31 us
  transfers between devices with their start and end apart: 7, of which 2 were waited for; matrix products, arithmetic and copies ran while one was open for 10% of the time, Pallas kernels for 64%

profile of v3, /device:TPU:0, one launch (start us, length us, event | category | flops | bytes accessed | tf_op | source)
XLA Modules:
  0.0 382.6 jit_solution(2653946433481029684)
XLA Ops:
  13.3 3.1 collective-permute-start
  16.4 2.6 collective-permute-start.1
  20.3 2.8 collective-permute-done
  23.2 5.5 %collective-permute-done.1 = bf16[96,768]{1,0:T(8,128)(2,1)S(1)} collective-permute-done((bf16[96,768]{1,0:T(8,128)(2,1)S(1)}, bf16[96,768]{1,0:T(8,128)(2,1)S(1)}, u32[]{:S(2)}, u32[]{:S(2)}) %collective-permute-start.1) | collective-permute-done | bytes 147488 | tf_op jit(solution)/shard_map/ppermute | solution.py:1202
  31.4 1.7 convolution_bitcast_fusion.2
  36.0 15.7 %shard_map.280.qkv_ref = bf16[16,192,128]{2,1,0:T(8,128)(2,1)S(1)} custom-call(bf16[12,192,128]{2,1,0:T(8,128)(2,1)S(1)} %constant_dynamic-update-slice_fusion.in_ref), custom_call_target="tpu_custom_call" | custom-call | tf_op jit(solution)/shard_map/pallas_call | solution.py:353
  51.6 6.4 %shard_map.281 = (f32[64,2048]{1,0:T(8,128)S(1)}, f32[1,2048]{1,0:T(1,128)S(1)}) custom-call(s32[1]{0:T(128)} %copy.123.length_ref, bf16[16,192,128]{2,1,0:T(8,128)(2,1)S(1)} %shard_map.280.qkv_ref), custom_call_target="tpu_custom_call" | custom-call | tf_op jit(solution)/shard_map/pallas_call | solution.py:117
  59.0 14.6 %shard_map.282 = bf16[12,64,128]{2,1,0:T(8,128)(2,1)S(1)} custom-call(bf16[16,64,128]{2,1,0:T(8,128)(2,1)S(1)} %bitcast_bitcast_fusion.in_ref), custom_call_target="tpu_custom_call" | custom-call | tf_op jit(solution)/shard_map/pallas_call | solution.py:353
  73.6 1.8 multiply_reduce_fusion.2
  76.5 38.8 %shard_map.283 = (bf16[8,4,96,768]{3,2,1,0:T(8,128)(2,1)S(1)}, bf16[8,128,768]{2,1,0:T(8,128)(2,1)S(1)}, f32[8,4,8,128]{3,2,1,0:T(8,128)S(1)}) custom-call(bf16[4,96,768]{2,1,0:T(8,128)(2,1)S(1)} %bitcast.139, bf16[128,768]{1,0:T(8,128)(2,1)S(1)} %multiply_convert_fusion.1.flat_ref, f32[4,8,128]{2,1,0:T(8,128)S(1)} %pad.13.gate_ref), custom_call_target="tpu_custom_call" | custom-call | tf_op jit(solution)/shard_map/pallas_call | solution.py:576
  115.3 2.2 copy-done.4
  120.2 1.8 multiply_sine_fusion
  122.0 8.1 %shard_map.285 = (bf16[8,128,768]{2,1,0:T(8,128)(2,1)}, bf16[8,128,768]{2,1,0:T(8,128)(2,1)}, bf16[4,192,256]{2,1,0:T(8,128)(2,1)}, bf16[4,192,256]{2,1,0:T(8,128)(2,1)}, bf16[4,64,768]{2,1,0:T(8,128)(2,1)}) custom-call(s32[1]{0:T(128)} %bitcast.13.plane_ref, bf16[8,128,768]{2,1,0:T(8,128)(2,1)} %copy-done.8, ...), custom_call_target="tpu_custom_call" | custom-call | tf_op jit(solution)/shard_map/pallas_call | solution.py:1107
  130.1 23.8 %shard_map.284 = (bf16[8,4,2,48,768]{4,3,2,1,0:T(8,128)(2,1)}, bf16[8,4,2,48,768]{4,3,2,1,0:T(8,128)(2,1)}, f32[4,32,24]{2,1,0:T(8,128)}, f32[4,768,256]{2,1,0:T...) custom-call(s32[1]{0:T(128)} %bitcast.13.plane_ref, bf16[8,4,2,48,768]{4,3,2,1,0:T(8,128)(2,1)} %bitcast.138, ...), custom_call_target="tpu_custom_call" | custom-call | tf_op jit(solution)/shard_map/pallas_call | solution.py:1028
  155.6 42.1 %shard_map.286 = (bf16[4,96,768]{2,1,0:T(8,128)(2,1)}, bf16[128,768]{1,0:T(8,128)(2,1)}, f32[4,8,128]{2,1,0:T(8,128)}) custom-call(bf16[8,4,96,768]{3,2,1,0:T(8,128)(2,1)} %bitcast.147, bf16[8,128,768]{2,1,0:T(8,128)(2,1)} %get-tuple-element.47.refs_1_, f32[8,4,8,128]{3,2,1,0:T(8,128)} %pad.14.refs_2_), custom_call_target="tpu_custom_call" | custom-call | tf_op jit(solution)/shard_map/pallas_call | solution.py:934
  202.3 6.5 %shard_map.288.upstream_ref = bf16[16,64,128]{2,1,0:T(8,128)(2,1)S(1)} custom-call(bf16[12,64,128]{2,1,0:T(8,128)(2,1)S(1)} %bitcast.144), custom_call_target="tpu_custom_call" | custom-call | tf_op jit(solution)/shard_map/pallas_call | solution.py:353
  209.5 12.3 %shard_map.289.in_ref = bf16[16,192,128]{2,1,0:T(8,128)(2,1)} custom-call(s32[1]{0:T(128)} %copy.123.length_ref, bf16[16,192,128]{2,1,0:T(8,128)(2,1)} %copy-done.1, f32[64,2048]{1,0:T(8,128)} %copy-done.5, f32[1,2048]{1,0:T(1,128)} %copy-done.10, bf16[16,64,128]{2,1,0:T(8,128)(2,1)} %copy-done.9, f32[32,2048]{1,0:T(8,128)} %get-tuple-element.127.cosine_ref, ...), custom_call_target="tpu_custom_call" | custom-call | tf_op jit(solution)/shard_map/pallas_call | solution.py:227
  222.9 20.4 %shard_map.290 = bf16[12,192,128]{2,1,0:T(8,128)(2,1)S(1)} custom-call(bf16[16,192,128]{2,1,0:T(8,128)(2,1)S(1)} %copy-done.2), custom_call_target="tpu_custom_call" | custom-call | tf_op jit(solution)/shard_map/pallas_call | solution.py:353
  243.5 3.5 convolution_bitcast_fusion
  247.8 1.8 fusion.51
  254.6 56.0 %shard_map.287 = (bf16[4,96,768]{2,1,0:T(8,128)(2,1)}, bf16[128,768]{1,0:T(8,128)(2,1)}, bf16[4,32,768]{2,1,0:T(8,128)(2,1)}, f32[24,2048]{1,0:T(8,128)}, f32[24,2048]{1,0:T(8,128)}, /*index=5*/f32[64,768]{1,0:T(8,128)}) custom-call(bf16[8,4,96,768]{3,2,1,0:T(8,128)(2,1)} %bitcast.146, bf16[8,128,768]{2,1,0:T(8,128)(2,1)} %get-tuple-element.45.refs_1_, ...), custom_call_target="tpu_custom_call" | custom-call | tf_op jit(solution)/shard_map/pallas_call | solution.py:934
  314.3 38.3 %psum.7 = f32[768]{0:T(1024)S(1)} all-reduce(f32[768]{0:T(1024)S(1)} %get-tuple-element.112), channel_id=1, replica_groups=mesh['dp'=2,'ctx'=4,'expert'=4] {'dp','ctx','expert'}, use_global_device_ids=true, to_apply=%region_17.18 | all-reduce | flops 768 | bytes 6144 | tf_op jit(solution)/shard_map/psum | solution.py:1343
  353.2 2.0 fusion.6
  357.7 13.5 %shard_map.291 = f32[12,24,192]{2,1,0:T(8,128)S(1)} custom-call(f32[16,24,192]{2,1,0:T(8,128)S(1)} %bitcast.143), custom_call_target="tpu_custom_call" | custom-call | tf_op jit(solution)/shard_map/pallas_call | solution.py:353
  (194 shorter events, 41.8 us)
Async XLA Ops:
  7.2 27.9 %copy-start = (bf16[768,768]{1,0:T(8,128)(2,1)S(1)}, bf16[768,768]{1,0:T(8,128)(2,1)}, u32[]{:S(2)}) copy-start(bf16[768,768]{1,0:T(8,128)(2,1)} %param.23) | copy-start | bytes 3538948
  7.2 5.6 %copy-start.20 = (bf16[1,128,768]{2,1,0:T(8,128)(2,1)S(1)}, bf16[1,128,768]{2,1,0:T(8,128)(2,1)}, u32[]{:S(2)}) copy-start(bf16[1,128,768]{2,1,0:T(8,128)(2,1)} %param.33) | copy-start | bytes 589828
  7.2 114.8 %all-gather.6.cloned.1.call-start = ((), (), s32[]{:S(2)}) async-start(), calls=%async_computation.2 | async-start | bytes 1769472 | tf_op jit(solution)/shard_map/all_gather | solution.py:1206
  9.8 120.3 %all-gather.4.cloned.1.call-start = ((), (), s32[]{:S(2)}) async-start(), calls=%async_computation.1 | async-start | bytes 5308416 | tf_op jit(solution)/shard_map/all_gather | solution.py:1205
  13.3 9.9 %collective-permute-start = (bf16[96,768]{1,0:T(8,128)(2,1)S(1)}, bf16[96,768]{1,0:T(8,128)(2,1)S(1)}, u32[]{:S(2)}, u32[]{:S(2)}) collective-permute-start(bf16[96,768]{1,0:T(8,128)(2,1)S(1)} %get-tuple-element.125), channel_id=1, source_target_pairs={{0,1},{1,2},{2,3},{3,0},{4,5},{5,6},{6,7},{7,4},{8,9},{9,10},{10,1... | collective-permute-start | bytes 442376 | tf_op jit(solution)/shard_map/ppermute | solution.py:1202
  16.4 12.3 %collective-permute-start.1 = (bf16[96,768]{1,0:T(8,128)(2,1)S(1)}, bf16[96,768]{1,0:T(8,128)(2,1)S(1)}, u32[]{:S(2)}, u32[]{:S(2)}) collective-permute-start(bf16[96,768]{1,0:T(8,128)(2,1)S(1)} %get-tuple-element.124), channel_id=1, source_target_pairs={{0,2},{1,3},{2,0},{3,1},{4,6},{5,7},{6,4},{7,5},{8,10},{9,11},{10,... | collective-permute-start | bytes 442376 | tf_op jit(solution)/shard_map/ppermute | solution.py:1202
  18.9 9.7 %collective-permute-start.2 = (bf16[96,768]{1,0:T(8,128)(2,1)S(1)}, bf16[96,768]{1,0:T(8,128)(2,1)S(1)}, u32[]{:S(2)}, u32[]{:S(2)}) collective-permute-start(bf16[96,768]{1,0:T(8,128)(2,1)S(1)} %get-tuple-element.123), channel_id=1, source_target_pairs={{0,3},{1,0},{2,1},{3,2},{4,7},{5,4},{6,5},{7,6},{8,11},{9,8},{10,9... | collective-permute-start | bytes 442376 | tf_op jit(solution)/shard_map/ppermute | solution.py:1202
  30.3 213.2 %all-gather.8.cloned.1.call-start = ((), (), s32[]{:S(2)}) async-start(), calls=%async_computation.3 | async-start | bytes 3342336 | tf_op jit(solution)/shard_map/all_gather | solution.py:1238
  31.3 325.3 %reduce-scatter.2.cloned.1.call-start = ((), (), s32[]{:S(2)}) async-start(), calls=%async_computation.4 | async-start | bytes 884736 | tf_op jit(solution)/shard_map/reduce_scatter | solution.py:1337
  51.6 23.8 %copy-start.1 = (bf16[16,192,128]{2,1,0:T(8,128)(2,1)}, bf16[16,192,128]{2,1,0:T(8,128)(2,1)S(1)}, u32[]{:S(2)}) copy-start(bf16[16,192,128]{2,1,0:T(8,128)(2,1)S(1)} %shard_map.280.qkv_ref) | copy-start | bytes 2359300
  58.1 15.4 %copy-start.10 = (f32[1,2048]{1,0:T(1,128)}, f32[1,2048]{1,0:T(1,128)S(1)}, u32[]{:S(2)}) copy-start(f32[1,2048]{1,0:T(1,128)S(1)} %get-tuple-element.57.total_ref) | copy-start | bytes 24580
  58.9 16.5 %copy-start.30 = (f32[768]{0:T(1024)S(1)}, f32[768]{0:T(1024)}, u32[]{:S(2)}) copy-start(f32[768]{0:T(1024)} %param.25) | copy-start | bytes 9220
  59.0 16.6 %copy-start.28 = (bf16[768,16]{0,1:T(8,128)(2,1)S(1)}, bf16[768,16]{0,1:T(8,128)(2,1)}, u32[]{:S(2)}) copy-start(bf16[768,16]{0,1:T(8,128)(2,1)} %param.26) | copy-start | bytes 73732
  75.4 46.6 %copy-start.11 = (f32[128,768]{1,0:T(8,128)}, f32[128,768]{1,0:T(8,128)S(1)}, u32[]{:S(2)}) copy-start(f32[128,768]{1,0:T(8,128)S(1)} %get-tuple-element.131) | copy-start | bytes 1179652
  155.6 43.2 %copy-start.33 = (s32[128,2]{0,1:T(2,128)S(1)}, s32[128,2]{0,1:T(2,128)}, u32[]{:S(2)}) copy-start(s32[128,2]{0,1:T(2,128)} %copy-done.32) | copy-start | bytes 3076
  155.6 44.6 %copy-start.12 = (f32[128,768]{1,0:T(8,128)S(1)}, f32[128,768]{1,0:T(8,128)}, u32[]{:S(2)}) copy-start(f32[128,768]{1,0:T(8,128)} %copy-done.11) | copy-start | bytes 1179652
  155.6 44.6 %copy-start.29 = (bf16[768,16]{0,1:T(8,128)(2,1)S(1)}, bf16[768,16]{0,1:T(8,128)(2,1)}, u32[]{:S(2)}) copy-start(bf16[768,16]{0,1:T(8,128)(2,1)} %param.26) | copy-start | bytes 73732
  222.9 20.6 %copy-start.3 = (bf16[16,192,128]{2,1,0:T(8,128)(2,1)S(1)}, bf16[16,192,128]{2,1,0:T(8,128)(2,1)}, u32[]{:S(2)}) copy-start(bf16[16,192,128]{2,1,0:T(8,128)(2,1)} %shard_map.289.in_ref) | copy-start | bytes 2359300
  247.8 3.9 %copy-start.27 = (bf16[25,768]{1,0:T(8,128)(2,1)S(1)}, bf16[25,768]{1,0:T(8,128)(2,1)}, u32[]{:S(2)}) copy-start(bf16[25,768]{1,0:T(8,128)(2,1)} %pad.19.clone) | copy-start | bytes 115204
  254.6 57.1 %copy-start.19 = (bf16[768,768]{1,0:T(8,128)(2,1)S(1)}, bf16[768,768]{1,0:T(8,128)(2,1)}, u32[]{:S(2)}) copy-start(bf16[768,768]{1,0:T(8,128)(2,1)} %param.22) | copy-start | bytes 3538948
  254.6 57.1 %copy-start.22 = (bf16[1,12,64,128]{3,2,0,1:T(8,128)(2,1)S(1)}, bf16[1,12,64,128]{3,2,0,1:T(8,128)(2,1)}, u32[]{:S(2)}) copy-start(bf16[1,12,64,128]{3,2,0,1:T(8,128)(2,1)} %get-tuple-element.120) | copy-start | bytes 589828
  312.2 41.0 %copy-start.26 = (bf16[128,768]{1,0:T(8,128)(2,1)S(1)}, bf16[128,768]{1,0:T(8,128)(2,1)}, u32[]{:S(2)}) copy-start(bf16[128,768]{1,0:T(8,128)(2,1)} %get-tuple-element.56) | copy-start | bytes 589828
  371.4 3.3 copy-start.24
  371.5 4.0 %copy-start.23 = (f32[64,768]{1,0:T(8,128)S(1)}, f32[64,768]{1,0:T(8,128)}, u32[]{:S(2)}) copy-start(f32[64,768]{1,0:T(8,128)} %get-tuple-element.163) | copy-start | bytes 589828
  (19 other events, 38.6 us)
Sparse Core Ops, SparseCore 0:
  10.5 28.4 all-gather.5
  41.4 43.2 all-gather.3
  88.1 71.5 all-gather.7
  247.1 8.1 reduce-scatter.1

commit v4 on v1

v4 whole, which is shorter than its diff:
```python
import functools

import jax
import jax.numpy as jnp
from jax import lax
from jax.experimental import pallas as pl
from jax.experimental.pallas import tpu as pltpu
from jax.sharding import PartitionSpec as P

HEAD_DIM = 64
EXPERTS = 16
TOP = 2
CAP = 22
PLACES = 24

norm_epsilon = 1e-06
rope_base = 10000.0
score_scale = 0.125
masked_value = -1e30
PLANE = ("dp", "ctx")
SLOT = ("ctx", "expert")
AHEAD = 2
bf16 = jnp.bfloat16
f32 = jnp.float32


def rms_scale(values):
    return lax.rsqrt(jnp.mean(values * values, axis=-1, keepdims=True) + norm_epsilon)


def rms_back(normal, scale, gain, upstream):
    lifted = upstream * gain
    return scale * (lifted - normal * jnp.mean(lifted * normal, axis=-1, keepdims=True))


def rope_tables(positions):
    half = HEAD_DIM // 2
    exponent = jnp.arange(half, dtype=f32) * (2.0 / HEAD_DIM)
    inverse_freq = rope_base ** (-exponent)
    angles = inverse_freq[:, None] * positions[None, :].astype(f32)
    return jnp.cos(angles), jnp.sin(angles)


def head_rows(qkv_ref, first, count):
    return jnp.concatenate(
        [qkv_ref[block, first : first + count, :] for block in range(qkv_ref.shape[0])], axis=1
    )


def live_keys(key_t, length):
    span = key_t.shape[1]
    place = lax.broadcasted_iota(jnp.int32, (8, span), 1)
    row = lax.broadcasted_iota(jnp.int32, (8, span), 0)
    bias = jnp.where((place >= length) & (row == 0), masked_value, 0.0)
    padded = jnp.concatenate(
        [key_t.astype(f32), bias, jnp.zeros((HEAD_DIM - 8, span), f32)], axis=0
    )
    return jnp.transpose(padded).astype(bf16)


def scaled_queries(query_t):
    span = query_t.shape[1]
    row = lax.broadcasted_iota(jnp.int32, (HEAD_DIM, span), 0)
    ones = jnp.where(row == 0, 1.0, 0.0)
    return jnp.concatenate([query_t.astype(f32) * score_scale, ones], axis=0).astype(bf16)


def causal(scores):
    key = lax.broadcasted_iota(jnp.int32, scores.shape, 0)
    query = lax.broadcasted_iota(jnp.int32, scores.shape, 1)
    return jnp.where(key <= query, scores, masked_value)


MESH = pl.DeviceIdType.MESH
ANY = pl.BlockSpec(memory_space=pl.ANY)
VMEM = pl.BlockSpec(memory_space=pltpu.VMEM)
SMEM = pl.BlockSpec(memory_space=pltpu.SMEM)
DMA = pltpu.SemaphoreType.DMA


def head_place(head, heads, ctx_size, expert_size):
    per = expert_size - 1
    if ctx_size <= expert_size and ctx_size * per == heads:
        row = head // per
        step = head % per
        return row, step + jnp.where(step >= row, 1, 0)
    return head // expert_size, head % expert_size


def head_of(ctx, expert, heads, ctx_size, expert_size):
    per = expert_size - 1
    if ctx_size <= expert_size and ctx_size * per == heads:
        head = ctx * per + expert - jnp.where(expert > ctx, 1, 0)
        return jnp.where(expert == ctx, heads, head)
    return ctx * expert_size + expert


def sizes_of():
    return tuple(lax.axis_size(a) for a in ("dp", "ctx", "expert"))


def greet(partners):
    barrier = pltpu.get_barrier_semaphore()
    for partner in partners:
        pl.semaphore_signal(barrier, inc=1, device_id=partner, device_id_type=MESH)
    pl.semaphore_wait(barrier, len(partners))


GROUP = 2


def flip(index, mask):
    bit = 1
    while bit <= mask:
        if mask & bit:
            index = index + bit * (1 - 2 * ((index // bit) % 2))
        bit *= 2
    return index


def bits_of(ctx_size):
    return [1 << b for b in range(ctx_size.bit_length() - 1)]


def group_bit(group, ctx_size):
    bits = bits_of(ctx_size)
    return bits[group % len(bits)]


def subsets(order):
    masks = [0]
    for bit in order:
        masks = masks + [m | bit for m in masks]
    return masks


class Piece:
    def __init__(self, array, kind, group, step, first, size, order):
        self.array, self.kind, self.group, self.step = array, kind, group, step
        self.first, self.size, self.order = first, size, order
        self.masks = subsets(order)


def pieces(kinds, expert_size, ctx_size):
    bits = bits_of(ctx_size)
    moving, staying = [], []
    for array, (kind, groups, rows) in enumerate(kinds):
        if kind == "flat":
            half = rows // 2
            staying.append(Piece(array, kind, None, None, 0, half, bits))
            staying.append(Piece(array, kind, None, None, half, rows - half, bits[::-1]))
            continue
        for step in range(expert_size):
            for group in range(groups or 1):
                if kind == "group":
                    order = [group_bit(group, ctx_size)]
                else:
                    order = bits if (step + array) % 2 == 0 else bits[::-1]
                (moving if step else staying).append(Piece(array, kind, group, step, 0, rows, order))
    return moving, staying


def plane_partners():
    dp_size, ctx_size, expert_size = sizes_of()
    dp, ctx, expert = (lax.axis_index(a) for a in ("dp", "ctx", "expert"))
    plane = [(d, c) for d in range(dp_size) for c in range(ctx_size) if (d, c) != (0, 0)]
    return [{"expert": (expert + step) % expert_size} for step in range(1, expert_size)] + [
        {"dp": (dp + d) % dp_size, "ctx": flip(ctx, c)} for d, c in plane
    ]


def spread_kernel(kinds, has_gate, *refs):
    greet(plane_partners())
    for _ in spread_steps(kinds, has_gate, refs):
        pass


def spread_steps(kinds, has_gate, refs):
    rest = iter(refs)

    def take(count):
        return [next(rest) for _ in range(count)]

    ins = take(len(kinds))
    gate_ref = next(rest) if has_gate else None
    outs = take(len(kinds))
    gates_ref = next(rest) if has_gate else None
    z_send, z_recv, send, recv, pair_recv, local_sem = take(6)
    if has_gate:
        gate_send, gate_recv, gate_z_send, gate_z_recv = take(4)
    dp_size, ctx_size, expert_size = (lax.axis_size(a) for a in ("dp", "ctx", "expert"))
    dp, ctx, expert = (lax.axis_index(a) for a in ("dp", "ctx", "expert"))
    moving, staying = pieces(kinds, expert_size, ctx_size)
    order = staying + moving
    own = dp * ctx_size + ctx
    other = (dp + 1) % dp_size

    def z_at(step):
        return (expert + step) % expert_size

    def z_from(step):
        return (expert + expert_size - step) % expert_size

    plane = [(d, c) for d in range(dp_size) for c in range(ctx_size) if (d, c) != (0, 0)]

    def landed(piece, core, mask, at=0):
        if piece.step is None:
            block = (dp if core == 0 else other) * ctx_size + flip(ctx, mask)
            return outs[piece.array].at[block, pl.ds(piece.first, piece.size)]
        return outs[piece.array].at[piece.group, core * 2 + (1 if mask ^ at else 0), z_from(piece.step)]

    def z_copy(piece, landing=False):
        place = z_from(piece.step) if landing else expert
        return pltpu.make_async_remote_copy(
            src_ref=ins[piece.array].at[z_at(piece.step), piece.group],
            dst_ref=outs[piece.array].at[piece.group, 0, place],
            send_sem=z_send.at[number[id(piece)]],
            recv_sem=z_recv.at[number[id(piece)]],
            device_id={"expert": z_at(piece.step)},
            device_id_type=MESH,
        )

    def gate_z(step, landing=False):
        return pltpu.make_async_remote_copy(
            src_ref=gate_ref.at[z_at(step)],
            dst_ref=gates_ref.at[own, z_from(step) if landing else expert],
            send_sem=gate_z_send.at[step],
            recv_sem=gate_z_recv.at[step],
            device_id={"expert": z_at(step)},
            device_id_type=MESH,
        )

    def gate_plane(d, c, block):
        return pltpu.make_async_remote_copy(
            src_ref=gates_ref.at[block],
            dst_ref=gates_ref.at[block],
            send_sem=gate_send.at[d, c],
            recv_sem=gate_recv.at[d, c],
            device_id={"dp": (dp + d) % dp_size, "ctx": flip(ctx, c)},
            device_id_type=MESH,
        )

    number = {id(piece): i for i, piece in enumerate(order)}
    def z_starts():
        if has_gate:
            for step in range(1, expert_size):
                gate_z(step).start()
        for piece in moving:
            z_copy(piece).start()

    def source(piece):
        if piece.step is None:
            return ins[piece.array].at[pl.ds(piece.first, piece.size)]
        if piece.step == 0:
            return ins[piece.array].at[expert, piece.group]
        return landed(piece, 0, 0)

    bits = bits_of(ctx_size)

    def passing(piece, mask, bit):
        return pltpu.make_async_remote_copy(
            src_ref=landed(piece, 0, mask) if mask else source(piece),
            dst_ref=landed(piece, 0, mask, bit),
            send_sem=send.at[number[id(piece)], mask, bits.index(bit)],
            recv_sem=recv.at[number[id(piece)], mask ^ bit],
            device_id={"ctx": flip(ctx, bit)},
            device_id_type=MESH,
        )

    def arrived(piece, mask):
        here = landed(piece, 0, mask)
        return pltpu.make_async_remote_copy(
            src_ref=here, dst_ref=here, send_sem=send.at[0, 0, 0],
            recv_sem=recv.at[number[id(piece)], mask], device_id={"ctx": ctx}, device_id_type=MESH,
        )

    def crossing(piece, mask, landing=False):
        if piece.step is None:
            there = landed(piece, 1 if landing else 0, mask)
        else:
            there = landed(piece, 1, mask)
        return pltpu.make_async_remote_copy(
            src_ref=landed(piece, 0, mask) if mask else source(piece),
            dst_ref=there,
            send_sem=send.at[number[id(piece)], mask, len(bits)],
            recv_sem=pair_recv.at[number[id(piece)], mask],
            device_id={"dp": other},
            device_id_type=MESH,
        )

    started = []

    def begin(one):
        one.start()
        started.append(one)

    def first(piece):
        for bit in piece.order:
            begin(passing(piece, 0, bit))
        begin(crossing(piece, 0))

    def forward(piece, place):
        bit = piece.order[place]
        for mask in [m | bit for m in subsets(piece.order[:place])]:
            arrived(piece, mask).wait_recv()
            for later in piece.order[place + 1 :]:
                begin(passing(piece, mask, later))
            begin(crossing(piece, mask))

    kept = [
        pltpu.make_async_copy(source(piece), landed(piece, 0, 0), local_sem.at[i])
        for i, piece in enumerate(staying)
    ]
    depth = len(bits)
    if has_gate:
        z_starts()
    for tick in range(len(order) + AHEAD + depth):
        for place in range(depth + 1):
            index = tick if place == 0 else tick - AHEAD - place + 1
            if not 0 <= index < len(order):
                continue
            piece = order[index]
            if place:
                if place <= len(piece.order):
                    forward(piece, place - 1)
                continue
            if piece.step:
                z_copy(piece, True).wait_recv()
            first(piece)
            if index == len(staying) - 1:
                for one in kept:
                    one.start()
                if has_gate:
                    gates_ref[own, expert] = gate_ref[expert]
                else:
                    yield
                    z_starts()
            if has_gate and index == len(order) - 1:
                for step in range(1, expert_size):
                    gate_z(step, True).wait_recv()
                for d, c in plane:
                    gate_plane(d, c, own).start()
        if tick >= len(staying) - 1:
            yield
    if has_gate:
        for d, c in plane:
            gate_plane(d, c, ((dp + d) % dp_size) * ctx_size + flip(ctx, c)).wait_recv()
            gate_plane(d, c, own).wait_send()
    for piece in order:
        for mask in piece.masks:
            crossing(piece, mask, True).wait_recv()
    for one in started:
        one.wait_send()
    for piece in moving:
        z_copy(piece).wait_send()
    if has_gate:
        for step in range(1, expert_size):
            gate_z(step).wait_send()
    for one in kept:
        one.wait()


def spread_plan(arrays, gate, sizes):
    dp_size, ctx_size, expert_size = sizes
    assert dp_size == 2
    plane_size = dp_size * ctx_size
    kinds, out_shape = [], []
    for array in arrays:
        if array.ndim == 4:
            kinds.append(("group", array.shape[1], array.shape[2]))
            shape = (array.shape[1], 4, expert_size) + array.shape[2:]
        else:
            kinds.append(("flat", None, array.shape[0]))
            shape = (plane_size,) + array.shape
        out_shape.append(jax.ShapeDtypeStruct(shape, array.dtype))
    moving, staying = pieces(kinds, expert_size, ctx_size)
    count = len(moving + staying)
    scratch = [
        DMA((count,)),
        DMA((count,)),
        DMA((count, ctx_size, len(bits_of(ctx_size)) + 1)),
        DMA((count, ctx_size)),
        DMA((count, ctx_size)),
        DMA((len(staying),)),
    ]
    if gate is not None:
        out_shape.append(jax.ShapeDtypeStruct((plane_size,) + gate.shape, gate.dtype))
        scratch += [DMA((dp_size, ctx_size))] * 2 + [DMA((expert_size,))] * 2
    return tuple(kinds), out_shape, scratch


def spread(arrays, gate, sizes, number):
    kinds, out_shape, scratch = spread_plan(arrays, gate, sizes)
    return pl.pallas_call(
        functools.partial(spread_kernel, kinds, True),
        out_shape=out_shape,
        in_specs=[VMEM] * (len(arrays) + 1),
        out_specs=[ANY] * len(arrays) + [VMEM],
        scratch_shapes=scratch,
        compiler_params=pltpu.CompilerParams(
            collective_id=number, has_side_effects=True, vmem_limit_bytes=32 << 20
        ),
    )(*arrays, gate)


def stage(piece, place):
    order = piece.order[::-1]
    done, bit = sum(order[:place]), order[place]
    kept = [m for m in piece.masks if not m & (done | bit)]
    return bit, [(m | bit, m) for m in kept]


def buffer_places(order):
    held, arriving, here, there = {}, {}, 0, 0
    for piece in order:
        for mask in piece.masks:
            held[id(piece), mask] = here
            here += piece.size
        for place in range(len(piece.order)):
            for index in range(len(stage(piece, place)[1])):
                arriving[id(piece), place, index] = there
                there += piece.size
    held["rows"], arriving["rows"] = here, there
    return held, arriving


def home_kernel(kinds, has_dots, has_shared, masks, ins, outs, *refs):
    ins += len(masks)
    outs += len(masks)
    refs = list(refs)
    carried, carried_out = refs[ins - len(masks) : ins], refs[ins + outs - len(masks) : ins + outs]
    carry = []
    if masks:
        carry = carry_copies(masks, carried, carried_out, *refs[-2:])
        del refs[-2:], refs[ins + outs - len(masks) : ins + outs], refs[ins - len(masks) : ins]
    greet(plane_partners())
    steps = home_steps(kinds, has_dots, has_shared, refs)
    next(steps)
    for one in carry:
        one.start()
    for _ in steps:
        pass
    for one in carry:
        one.wait()


def home_steps(kinds, has_dots, has_shared, refs):
    rest = iter(refs)

    def take(count):
        return [next(rest) for _ in range(count)]

    parts = take(len(kinds))
    dot_ref = next(rest) if has_dots else None
    grads = take(3) if has_shared else []
    outs = take(len(kinds))
    dots_ref = next(rest) if has_dots else None
    grads_out = take(3) if has_shared else []
    mine, theirs, arrivals, mine_sem, pair_send, pair_recv, send, recv, z_send, z_recv = take(10)

    dp_size, ctx_size, expert_size = (lax.axis_size(a) for a in ("dp", "ctx", "expert"))
    dp, ctx, expert = (lax.axis_index(a) for a in ("dp", "ctx", "expert"))
    moving, staying = pieces(kinds, expert_size, ctx_size)
    order = moving + staying
    number = {id(piece): i for i, piece in enumerate(order)}
    own = dp * ctx_size + ctx
    other = (dp + 1) % dp_size

    def z_at(step):
        return (expert + step) % expert_size

    def z_from(step):
        return (expert + expert_size - step) % expert_size

    def plane_from(d, c):
        return ((dp + dp_size - d) % dp_size) * ctx_size + flip(ctx, c)

    def plane_at(d, c):
        return ((dp + d) % dp_size) * ctx_size + flip(ctx, c)

    plane = [(d, c) for d in range(dp_size) for c in range(ctx_size) if (d, c) != (0, 0)]
    partners = {(d, c): {"dp": (dp + d) % dp_size, "ctx": flip(ctx, c)} for d, c in plane}
    held, arriving = buffer_places(order)

    def whole(piece, core, mask):
        if piece.kind == "group":
            return parts[piece.array].at[piece.group, core * 2 + (1 if mask else 0), z_at(piece.step)]
        block = (dp if core == 0 else other) * ctx_size + flip(ctx, mask)
        if piece.kind == "flat":
            return parts[piece.array].at[block, pl.ds(piece.first, piece.size)]
        return parts[piece.array].at[block, z_at(piece.step)]

    def at(piece, mask):
        return pl.ds(held[id(piece), mask], piece.size)

    def load(piece, mask):
        return pltpu.make_async_copy(
            whole(piece, 0, mask), mine.at[at(piece, mask)], mine_sem.at[number[id(piece)], mask]
        )

    def cross(piece, mask):
        return pltpu.make_async_remote_copy(
            src_ref=whole(piece, 1, mask),
            dst_ref=theirs.at[at(piece, mask)],
            send_sem=pair_send.at[number[id(piece)], mask],
            recv_sem=pair_recv.at[number[id(piece)], mask],
            device_id={"dp": other},
            device_id_type=MESH,
        )

    for piece in order:
        for mask in piece.masks:
            cross(piece, mask).start()
            load(piece, mask).start()

    if has_dots:
        dot_in, dot_sum, dot_send, dot_recv, dot_z_send, dot_z_recv = take(6)

        def dot_plane(d, c):
            return pltpu.make_async_remote_copy(
                src_ref=dot_ref.at[plane_at(d, c)],
                dst_ref=dot_in.at[d, c],
                send_sem=dot_send.at[d, c],
                recv_sem=dot_recv.at[d, c],
                device_id=partners[d, c],
                device_id_type=MESH,
            )

        def dot_z(step, landing=False):
            return pltpu.make_async_remote_copy(
                src_ref=dot_sum.at[z_at(step)],
                dst_ref=dots_ref.at[z_from(step) if landing else expert],
                send_sem=dot_z_send.at[step],
                recv_sem=dot_z_recv.at[step],
                device_id={"expert": z_at(step)},
                device_id_type=MESH,
            )

        for d, c in plane:
            dot_plane(d, c).start()

    if has_shared:
        grad_in, column_sum = take(3), take(2)
        grad_send, grad_recv, column_send, column_recv, grad_sem = take(5)
        part = grads[0].shape[2]

        def grad_z(kind, step):
            return pltpu.make_async_remote_copy(
                src_ref=grads[kind].at[z_at(step)],
                dst_ref=grad_in[kind].at[step],
                send_sem=grad_send.at[kind, step],
                recv_sem=grad_recv.at[kind, step],
                device_id={"expert": z_at(step)},
                device_id_type=MESH,
            )

        def grad_own(kind):
            return pltpu.make_async_copy(
                grads[kind].at[expert], grad_in[kind].at[0], grad_sem.at[kind]
            )

        def column(kind, d, c, landing=False):
            at = plane_from(d, c) if landing else own
            return pltpu.make_async_remote_copy(
                src_ref=column_sum[kind].at[plane_at(d, c)],
                dst_ref=grads_out[kind].at[:, pl.ds(pl.multiple_of(at * part, 128), part)],
                send_sem=column_send.at[kind, d, c],
                recv_sem=column_recv.at[kind, d, c],
                device_id=partners[d, c],
                device_id_type=MESH,
            )

        for kind in range(3):
            grad_own(kind).start()
            for step in range(1, expert_size):
                grad_z(kind, step).start()

        def sum_grads():
            for kind in range(3):
                grad_own(kind).wait()
                total = grad_in[kind][0].astype(f32)
                for step in range(1, expert_size):
                    grad_z(kind, step).wait_recv()
                    total = total + grad_in[kind][step].astype(f32)
                if kind == 2:
                    grads_out[2][...] = total
                    continue
                shard = grads_out[kind].shape[0]
                for block in range(dp_size * ctx_size):
                    column_sum[kind][block] = total[block * shard : (block + 1) * shard]
                for d, c in plane:
                    column(kind, d, c).start()
                here = pl.ds(pl.multiple_of(own * part, 128), part)
                grads_out[kind][:, here] = column_sum[kind][own]

    def hop(piece, place, index):
        bit, moves = stage(piece, place)
        return pltpu.make_async_remote_copy(
            src_ref=mine.at[at(piece, moves[index][0])],
            dst_ref=arrivals.at[pl.ds(arriving[id(piece), place, index], piece.size)],
            send_sem=send.at[number[id(piece)], moves[index][0]],
            recv_sem=recv.at[number[id(piece)], place, index],
            device_id={"ctx": flip(ctx, bit)},
            device_id_type=MESH,
        )

    def z_copy(piece, landing=False):
        place = z_from(piece.step) if landing else expert
        out = outs[piece.array]
        return pltpu.make_async_remote_copy(
            src_ref=mine.at[at(piece, 0)],
            dst_ref=out.at[place, piece.group] if piece.kind == "group" else out.at[place],
            send_sem=z_send.at[number[id(piece)]],
            recv_sem=z_recv.at[number[id(piece)]],
            device_id={"expert": z_at(piece.step)},
            device_id_type=MESH,
        )

    def add(here, buffer, there):
        mine[here] = (mine[here].astype(f32) + buffer[there].astype(f32)).astype(mine.dtype)

    def pair(piece):
        leaving = [source for source, _ in stage(piece, 0)[1]]
        for mask in leaving + [m for m in piece.masks if m not in leaving]:
            load(piece, mask).wait()
            cross(piece, mask).wait_recv()
            add(at(piece, mask), theirs, at(piece, mask))
            if mask in leaving:
                hop(piece, 0, leaving.index(mask)).start()

    def step(piece, place):
        targets = [target for _, target in stage(piece, place)[1]]
        leaving = []
        if place + 1 < len(piece.order):
            leaving = [source for source, _ in stage(piece, place + 1)[1]]
        for index in range(len(targets)):
            hop(piece, place, index).wait_recv()
        for mask in leaving + [m for m in targets if m not in leaving]:
            there = pl.ds(arriving[id(piece), place, targets.index(mask)], piece.size)
            add(at(piece, mask), arrivals, there)
            if mask in leaving:
                hop(piece, place + 1, leaving.index(mask)).start()

    def finish(piece):
        result, out = mine.at[at(piece, 0)], outs[piece.array]
        if piece.kind == "flat":
            out[pl.ds(piece.first, piece.size)] = result[...]
        elif piece.step:
            z_copy(piece).start()
        elif piece.kind == "group":
            out[expert, piece.group] = result[...]
        else:
            out[expert] = result[...]

    depth = max(len(piece.order) for piece in order)
    for tick in range(len(order) + AHEAD + depth):
        for place in range(depth + 1):
            index = tick if place == 0 else tick - AHEAD - place + 1
            if not 0 <= index < len(order) or place > len(order[index].order):
                continue
            if place == 0:
                pair(order[index])
            else:
                step(order[index], place - 1)
            if place == len(order[index].order):
                finish(order[index])
        yield

    if has_dots:
        total = dot_ref[own]
        for d, c in plane:
            dot_plane(d, c).wait_recv()
            total = total + dot_in[d, c]
        dot_sum[...] = total
        for step_z in range(1, expert_size):
            dot_z(step_z).start()
        dots_ref[expert] = dot_sum[expert]
    if has_shared:
        sum_grads()

    for piece in moving:
        z_copy(piece, True).wait_recv()
    if has_dots:
        for step_z in range(1, expert_size):
            dot_z(step_z, True).wait_recv()
            dot_z(step_z).wait_send()
        for d, c in plane:
            dot_plane(d, c).wait_send()
    if has_shared:
        for kind in range(3):
            for step_z in range(1, expert_size):
                grad_z(kind, step_z).wait_send()
            if kind < 2:
                for d, c in plane:
                    column(kind, d, c, True).wait_recv()
                    column(kind, d, c).wait_send()
    for piece in moving:
        z_copy(piece).wait_send()
    for piece in order:
        for mask in piece.masks:
            cross(piece, mask).wait_send()
        for place in range(len(piece.order)):
            for index in range(len(stage(piece, place)[1])):
                hop(piece, place, index).wait_send()


def home_plan(parts, sizes, dots=None, grads=None):
    dp_size, ctx_size, expert_size = sizes
    assert dp_size == 2
    width, dtype = parts[0].shape[-1], parts[0].dtype
    kinds, out_shape = [], []
    for part in parts:
        if part.ndim == 5:
            kinds.append(("group", part.shape[0], part.shape[3]))
            shape = (expert_size, part.shape[0]) + part.shape[3:]
        else:
            kinds.append(("plane" if part.ndim == 4 else "flat", None, part.shape[-2]))
            shape = part.shape[1:]
        out_shape.append(jax.ShapeDtypeStruct(shape, dtype))
    moving, staying = pieces(kinds, expert_size, ctx_size)
    held, arriving = buffer_places(moving + staying)
    count, depth = len(moving + staying), len(bits_of(ctx_size))
    operands, in_specs = list(parts), [ANY] * len(parts)
    scratch = [
        pltpu.VMEM((held["rows"], width), dtype),
        pltpu.VMEM((held["rows"], width), dtype),
        pltpu.VMEM((arriving["rows"], width), dtype),
        DMA((count, ctx_size)),
        DMA((count, ctx_size)),
        DMA((count, ctx_size)),
        DMA((count, ctx_size)),
        DMA((count, depth, max(ctx_size // 2, 1))),
        DMA((count,)),
        DMA((count,)),
    ]
    if dots is not None:
        operands.append(dots)
        in_specs.append(VMEM)
        out_shape.append(jax.ShapeDtypeStruct(dots.shape[1:], dots.dtype))
        scratch += [
            pltpu.VMEM((dp_size, ctx_size) + dots.shape[1:], dots.dtype),
            pltpu.VMEM(dots.shape[1:], dots.dtype),
            DMA((dp_size, ctx_size)),
            DMA((dp_size, ctx_size)),
            DMA((expert_size,)),
            DMA((expert_size,)),
        ]
    if grads is not None:
        operands += list(grads)
        in_specs += [ANY] * 3
        plane_size, part = dp_size * ctx_size, grads[0].shape[2]
        shard = grads[0].shape[1] // plane_size
        columns = jax.ShapeDtypeStruct((shard, plane_size * part), f32)
        out_shape += [columns, columns, jax.ShapeDtypeStruct(grads[2].shape[1:], f32)]
        scratch += [pltpu.VMEM(grad.shape, grad.dtype) for grad in grads]
        scratch += [pltpu.VMEM((plane_size, shard, part), f32)] * 2
        scratch += [
            DMA((3, expert_size)),
            DMA((3, expert_size)),
            DMA((2, dp_size, ctx_size)),
            DMA((2, dp_size, ctx_size)),
            DMA((3,)),
        ]
    return tuple(kinds), operands, in_specs, out_shape, scratch


def bring_home(parts, sizes, number, dots=None, grads=None, carried=(), masks=()):
    kinds, operands, in_specs, out_shape, scratch = home_plan(parts, sizes, dots, grads)
    ins, outs = len(operands), len(out_shape)
    carry_shapes = [jax.ShapeDtypeStruct(array.shape, array.dtype) for array in carried]
    carry_sems = [DMA((len(masks), len(masks[0])))] * 2 if masks else []
    got = pl.pallas_call(
        functools.partial(home_kernel, kinds, dots is not None, grads is not None, masks, ins, outs),
        out_shape=out_shape + carry_shapes,
        in_specs=in_specs + [ANY] * len(carried),
        out_specs=[VMEM] * outs + [ANY] * len(carried),
        scratch_shapes=scratch + carry_sems,
        compiler_params=pltpu.CompilerParams(
            collective_id=number, has_side_effects=True, vmem_limit_bytes=58 << 20
        ),
    )(*operands, *carried)
    return got


NT = (((1,), (1,)), ((), ()))
TN = (((0,), (0,)), ((), ()))


def contract(a, b, dims=(((1,), (0,)), ((), ()))):
    return lax.dot_general(a, b, dims, preferred_element_type=f32)


def branch(rows, d_out, gate_w, up_w, down_w):
    gate_lin, up_lin = contract(rows, gate_w), contract(rows, up_w)
    sigmoid = 1.0 / (1.0 + jnp.exp(-gate_lin))
    silu = gate_lin * sigmoid
    hidden = (silu * up_lin).astype(bf16)
    d_hidden = contract(d_out, down_w, NT)
    d_gate = (d_hidden * up_lin * (sigmoid + silu * (1.0 - sigmoid))).astype(bf16)
    d_up = (d_hidden * silu).astype(bf16)
    result = contract(hidden, down_w)
    d_rows = contract(d_gate, gate_w, NT) + contract(d_up, up_w, NT)
    d_lin = contract(rows, jnp.concatenate([d_gate, d_up], axis=1), TN)
    d_down = contract(hidden, d_out, TN)
    return result, d_rows, d_lin, d_down


def experts_kernel(slices, table_ref, rows_ref, up_ref, scale_ref, *refs):
    rest = iter(refs)

    def take(count):
        return [next(rest) for _ in range(count)]

    gate_ws, up_ws, down_ws = take(slices), take(slices), take(slices)
    result_ref, d_rows_ref, dots_ref = take(3)
    gate_grads, up_grads, down_grads = take(slices), take(slices), take(slices)
    rows_f32, up_f32 = take(2)
    sums = list(rest)
    blocks, expert_size = rows_ref.shape[1:3]
    sources = blocks * expert_size
    width, part = gate_ws[0].shape[1:]
    last_chunk = pl.program_id(1) == pl.num_programs(1) - 1

    def unpack(source, carry):
        there = pl.ds(pl.multiple_of(source * PLACES, 8), PLACES)
        at = 0, source // expert_size, source % expert_size
        rows, up = rows_ref[at].astype(f32), up_ref[at].astype(f32)
        for i in range(GROUP):
            rows_f32[i, there] = rows[i * PLACES : (i + 1) * PLACES]
            up_f32[i, there] = up[i * PLACES : (i + 1) * PLACES]
        return carry

    lax.fori_loop(0, sources, unpack, 0)
    for i in range(GROUP):
        rows, up = rows_f32[i].astype(bf16), up_f32[i]
        scale = scale_ref[0, i][:, :, None]
        by_source = (sources, PLACES, width)
        d_out = (up.reshape(by_source) * scale).reshape(up.shape).astype(bf16)
        result, d_rows, d_lin, d_down = branch(
            rows,
            d_out,
            jnp.concatenate([w[i] for w in gate_ws], axis=1),
            jnp.concatenate([w[i] for w in up_ws], axis=1),
            jnp.concatenate([w[i] for w in down_ws], axis=0),
        )
        if sums:

            @pl.when(pl.program_id(1) == 0)
            def _(i=i):
                for total in sums:
                    total[i] = jnp.zeros(total.shape[1:], f32)

            sums[0][i] += d_lin
            sums[1][i] += d_down
            d_lin, d_down = sums[0].at[i], sums[1].at[i]

        def write(i=i, d_lin=d_lin, d_down=d_down):
            for k in range(slices):
                gate_grads[k][i] = d_lin[:, k * part : (k + 1) * part].astype(bf16)
                up_grads[k][i] = d_lin[:, (slices + k) * part : (slices + k + 1) * part].astype(bf16)
                down_grads[k][i] = d_down[k * part : (k + 1) * part, :].astype(bf16)

        if sums:
            pl.when(last_chunk)(write)
        else:
            write()
        dots_ref[0, i] = jnp.sum((result * up).reshape(by_source), axis=-1)
        up_f32[i] = (result.reshape(by_source) * scale).reshape(up.shape)
        rows_f32[i] = d_rows

    def pack(source, carry):
        there = pl.ds(pl.multiple_of(source * PLACES, 8), PLACES)
        at = 0, source // expert_size, source % expert_size
        result_ref[at] = jnp.concatenate([up_f32[i, there] for i in range(GROUP)]).astype(bf16)
        d_rows_ref[at] = jnp.concatenate([rows_f32[i, there] for i in range(GROUP)]).astype(bf16)
        return carry

    lax.fori_loop(0, sources, pack, 0)


def experts(table, rows, up, scale, gate_w, up_w, down_w, part):
    groups, blocks, expert_size, size, width = rows.shape
    slices = table.shape[0] // groups
    chunk = max(16 // expert_size, 1)
    steps = blocks // chunk
    sources = chunk * expert_size
    rows_spec = pl.BlockSpec((1, chunk, expert_size, size, width), lambda g, c, t: (g, c, 0, 0, 0))
    dots_spec = pl.BlockSpec((1, GROUP, sources, PLACES), lambda g, c, t: (g, 0, c, 0))
    column = lambda k: lambda g, c, t: (g, 0, t[g * slices + k])
    row = lambda k: lambda g, c, t: (g, t[g * slices + k], 0)
    whole = lambda g, c, t: (g, 0, 0)
    columns = [pl.BlockSpec((GROUP, width, part), column(k)) for k in range(slices)]
    lin = jax.ShapeDtypeStruct((groups * GROUP, width, part), bf16)
    down = jax.ShapeDtypeStruct((groups * GROUP, part, width), bf16)
    accumulators = [
        pltpu.VMEM((GROUP, width, 2 * slices * part), f32),
        pltpu.VMEM((GROUP, slices * part, width), f32),
    ]
    out = pl.pallas_call(
        functools.partial(experts_kernel, slices),
        grid_spec=pltpu.PrefetchScalarGridSpec(
            num_scalar_prefetch=1,
            grid=(groups, steps),
            in_specs=[rows_spec, rows_spec, dots_spec]
            + columns * 2
            + [pl.BlockSpec((GROUP, part, width), row(k)) for k in range(slices)],
            out_specs=[rows_spec, rows_spec, dots_spec]
            + [pl.BlockSpec((GROUP, width, part), whole)] * (2 * slices)
            + [pl.BlockSpec((GROUP, part, width), whole)] * slices,
            scratch_shapes=[pltpu.VMEM((GROUP, sources * PLACES, width), f32)] * 2
            + (accumulators if steps > 1 else []),
        ),
        out_shape=[
            jax.ShapeDtypeStruct(rows.shape, bf16),
            jax.ShapeDtypeStruct(rows.shape, bf16),
            jax.ShapeDtypeStruct(scale.shape, f32),
        ]
        + [lin] * (2 * slices)
        + [down] * slices,
        compiler_params=pltpu.CompilerParams(vmem_limit_bytes=62 << 20),
    )(table, rows, up, scale, *[gate_w] * slices, *[up_w] * slices, *[down_w] * slices)
    result, d_rows, dots = out[:3]
    return result, d_rows, dots, [out[3 + kind * slices : 3 + (kind + 1) * slices] for kind in range(3)]


def shared_kernel(
    plane_size, plane_ref, rows_ref, up_ref, gate_w, up_w, down_w, result_ref, d_rows_ref, gate_grad, up_grad,
    down_grad, lin_sum, down_sum,
):
    planes, rows, width = rows_ref.shape
    expert_size, column, part = gate_grad.shape
    shard = column // plane_size
    flat = (planes * rows, width)
    result, d_rows, d_lin, d_down = branch(
        rows_ref[...].reshape(flat), up_ref[...].reshape(flat), gate_w[...], up_w[...], down_w[...]
    )
    result_ref[...] = result.reshape(rows_ref.shape).astype(bf16)
    d_rows_ref[...] = d_rows.reshape(rows_ref.shape).astype(bf16)

    @pl.when(pl.program_id(0) == 0)
    def _():
        lin_sum[...] = jnp.zeros_like(lin_sum)
        down_sum[...] = jnp.zeros_like(down_sum)

    lin_sum[...] += d_lin
    down_sum[...] += d_down

    @pl.when(pl.program_id(0) == pl.num_programs(0) - 1)
    def _():
        for z in range(expert_size):
            firsts = [(p * expert_size + z) * shard for p in range(plane_size)]
            mine = jnp.concatenate([lin_sum[first : first + shard] for first in firsts]).astype(bf16)
            gate_grad[z] = mine[:, :part]
            up_grad[z] = mine[:, part:]
        down_grad[...] = down_sum[...].astype(bf16).reshape(down_grad.shape)


def shared(plane, rows, up, gate_w, up_w, down_w, expert_size):
    plane_size, count, width = rows.shape
    hidden_width = gate_w.shape[1]
    part = hidden_width // plane_size
    planes = 4
    flat = pl.BlockSpec((planes, count, width), lambda c, p: (c, 0, 0))
    columns = (expert_size, width // expert_size, part)
    down = (expert_size, part // expert_size, width)
    return pl.pallas_call(
        functools.partial(shared_kernel, plane_size),
        grid_spec=pltpu.PrefetchScalarGridSpec(
            num_scalar_prefetch=1,
            grid=(plane_size // planes,),
            in_specs=[
                flat,
                flat,
                pl.BlockSpec((width, part), lambda c, p: (0, p[0])),
                pl.BlockSpec((width, part), lambda c, p: (0, p[0])),
                pl.BlockSpec((part, width), lambda c, p: (p[0], 0)),
            ],
            out_specs=[
                flat,
                flat,
                pl.BlockSpec(columns, lambda c, p: (0, 0, 0)),
                pl.BlockSpec(columns, lambda c, p: (0, 0, 0)),
                pl.BlockSpec(down, lambda c, p: (0, 0, 0)),
            ],
            scratch_shapes=[pltpu.VMEM((width, 2 * part), f32), pltpu.VMEM((part, width), f32)],
        ),
        out_shape=[
            jax.ShapeDtypeStruct(rows.shape, bf16),
            jax.ShapeDtypeStruct(rows.shape, bf16),
            jax.ShapeDtypeStruct(columns, bf16),
            jax.ShapeDtypeStruct(columns, bf16),
            jax.ShapeDtypeStruct(down, bf16),
        ],
        compiler_params=pltpu.CompilerParams(vmem_limit_bytes=58 << 20),
    )(plane, rows, up, gate_w, up_w, down_w)


def carry_copies(masks, sources, targets, send_sem, recv_sem):
    ctx = lax.axis_index("ctx")
    return [
        pltpu.make_async_remote_copy(
            src_ref=sources[array].at[pl.ds(g * GROUP, GROUP)],
            dst_ref=targets[array].at[pl.ds(g * GROUP, GROUP)],
            send_sem=send_sem.at[array, g],
            recv_sem=recv_sem.at[array, g],
            device_id={"ctx": flip(ctx, mask)},
            device_id_type=MESH,
        )
        for array, by_group in enumerate(masks)
        for g, mask in enumerate(by_group)
    ]


class Slot:
    def __init__(self, heads):
        _, self.ctx_size, self.expert_size = sizes_of()
        self.heads, self.count = heads, self.ctx_size * self.expert_size
        ctx, expert = lax.axis_index("ctx"), lax.axis_index("expert")
        self.me = ctx * self.expert_size + expert
        head = head_of(ctx, expert, heads, self.ctx_size, self.expert_size)
        self.holds = head < heads
        self.head = head % heads

    def device(self, place):
        return {"ctx": place // self.expert_size, "expert": place % self.expert_size}

    def partners(self):
        dp, ctx = lax.axis_index("dp"), lax.axis_index("ctx")
        dp_size = lax.axis_size("dp")
        return [self.device((self.me + i) % self.count) for i in range(1, self.count)] + [
            {"dp": (dp + d) % dp_size, "ctx": flip(ctx, c)} for d in range(1, dp_size) for c in range(self.ctx_size)
        ]

    def copy(self, source, target, send, recv, there):
        return pltpu.make_async_remote_copy(
            src_ref=source, dst_ref=target, send_sem=send, recv_sem=recv, device_id=there, device_id_type=MESH
        )

    def inward(self, blocks, landing, send, recv):
        for i in range(self.heads):
            head = (self.me + i) % self.heads
            row, column = head_place(head, self.heads, self.ctx_size, self.expert_size)
            one = self.copy(
                blocks.at[head], landing.at[self.me], send.at[head], recv.at[self.me],
                {"ctx": row, "expert": column},
            )
            yield jnp.logical_not(self.holds & (head == self.head)), one

    def inward_landed(self, landing, send, recv):
        for i in range(1, self.count):
            source = (self.me + self.count - i) % self.count
            here = landing.at[source]
            yield self.copy(here, here, send.at[0], recv.at[source], self.device(self.me))

    def outward(self, blocks, landing, send, recv, place):
        return self.copy(
            blocks.at[place], landing.at[self.head], send.at[place], recv.at[self.head], self.device(place)
        )

    def outward_landed(self, landing, send, recv):
        for head in range(self.heads):
            here = landing.at[head]
            one = self.copy(here, here, send.at[0], recv.at[head], self.device(self.me))
            yield jnp.logical_not(self.holds & (head == self.head)), one


def attend_kernel(step, heads, kinds, length_ref, blocks_ref, *refs):
    rest = iter(refs)

    def take(count):
        return [next(rest) for _ in range(count)]

    side_ins = take(len(kinds))
    qkv_ref, out_ref, total_ref, landed_ref = take(4)
    side_outs = take(len(kinds))
    key_ref, query_ref, value_ref, sent_ref = take(4)
    in_send, in_recv, out_send, out_recv = take(4)
    side = spread_steps(kinds, False, side_ins + side_outs + list(rest))

    slot = Slot(heads)
    rows = blocks_ref.shape[2]
    span = slot.count * rows
    greet(slot.partners())
    for needed, one in slot.inward(blocks_ref, qkv_ref, in_send, in_recv):
        pl.when(needed)(one.start)
    next(side)

    @pl.when(slot.holds)
    def _():
        qkv_ref[slot.me] = blocks_ref[slot.head]
        for one in slot.inward_landed(qkv_ref, in_send, in_recv):
            one.wait_recv()

    next(side)

    @pl.when(slot.holds)
    def _():
        key_ref[...] = live_keys(head_rows(qkv_ref, HEAD_DIM, HEAD_DIM), length_ref[0])
        query_ref[...] = scaled_queries(head_rows(qkv_ref, 0, HEAD_DIM))
        value_ref[...] = head_rows(qkv_ref, 2 * HEAD_DIM, HEAD_DIM)

    def query_block(q):
        here = pl.ds(q * step, step)
        query = query_ref[:, here]

        def absorb(k, state, masked):
            top, total, out = state
            there = pl.ds(k * step if masked else pl.multiple_of(k * step, step), step)
            scores = jnp.dot(key_ref[there, :], query, preferred_element_type=f32)
            if masked:
                scores = causal(scores)
            new_top = jnp.maximum(top, jnp.max(scores, axis=0, keepdims=True))
            shrink = jnp.exp(top - new_top)
            weights = jnp.exp(scores - new_top)
            total = total * shrink + jnp.sum(weights, axis=0, keepdims=True)
            out = out * shrink + jnp.dot(
                value_ref[:, there], weights.astype(bf16), preferred_element_type=f32
            )
            return new_top, total, out

        state = (
            jnp.full((1, step), masked_value, f32),
            jnp.zeros((1, step), f32),
            jnp.zeros((HEAD_DIM, step), f32),
        )
        state = absorb(q, state, True)
        if q:
            state = lax.fori_loop(0, q, lambda k, s: absorb(k, s, False), state)
        top, total, out = state
        out = out / total
        out_ref[:, here] = out
        total_ref[:, here] = top + jnp.log(total)
        for i in range(step // rows):
            place = q * (step // rows) + i
            sent_ref[place] = out[:, i * rows : (i + 1) * rows].astype(bf16)
            one = slot.outward(sent_ref, landed_ref, out_send, out_recv, place)
            pl.when(slot.me != place)(one.start)

    for q in range(span // step):
        pl.when(slot.holds)(functools.partial(query_block, q))
        next(side, None)

    @pl.when(slot.holds)
    def _():
        landed_ref[slot.head] = sent_ref[slot.me]

    for needed, one in slot.outward_landed(landed_ref, out_send, out_recv):
        pl.when(needed)(one.wait_recv)
    for _ in side:
        pass
    for needed, one in slot.inward(blocks_ref, qkv_ref, in_send, in_recv):
        pl.when(needed)(one.wait_send)
    for place in range(slot.count):
        one = slot.outward(sent_ref, landed_ref, out_send, out_recv, place)
        pl.when(slot.holds & (slot.me != place))(one.wait_send)


def attend(blocks, length, arrays, sizes, number):
    heads, _, rows = blocks.shape
    count = sizes[1] * sizes[2]
    span = count * rows
    step = min(512, span)
    kinds, side_shapes, side_scratch = spread_plan(arrays, None, sizes)
    out = pl.pallas_call(
        functools.partial(attend_kernel, step, heads, kinds),
        out_shape=[
            jax.ShapeDtypeStruct((count,) + blocks.shape[1:], bf16),
            jax.ShapeDtypeStruct((HEAD_DIM, span), f32),
            jax.ShapeDtypeStruct((1, span), f32),
            jax.ShapeDtypeStruct((heads, HEAD_DIM, rows), bf16),
        ]
        + side_shapes,
        in_specs=[SMEM] + [VMEM] * (1 + len(arrays)),
        out_specs=[VMEM] * 4 + [ANY] * len(arrays),
        scratch_shapes=[
            pltpu.VMEM((span, 2 * HEAD_DIM), bf16),
            pltpu.VMEM((2 * HEAD_DIM, span), bf16),
            pltpu.VMEM((HEAD_DIM, span), bf16),
            pltpu.VMEM((count, HEAD_DIM, rows), bf16),
        ]
        + [DMA((count,))] * 4
        + side_scratch,
        compiler_params=pltpu.CompilerParams(
            collective_id=number, has_side_effects=True, vmem_limit_bytes=56 << 20
        ),
    )(length, blocks, *arrays)
    return out[:4], out[4:]


def unrotate(grad_t, cosine, sine):
    half = HEAD_DIM // 2
    first, second = grad_t[:half], grad_t[half:]
    return jnp.concatenate(
        [first * cosine + second * sine, second * cosine - first * sine], axis=0
    )


def attend_back_kernel(
    step, heads, kinds, masks, length_ref, qkv_ref, out_ref, total_ref, cosine_ref, sine_ref, blocks_ref, *refs
):
    rest = iter(refs)

    def take(count):
        return [next(rest) for _ in range(count)]

    side_ins, carried = take(len(kinds)), take(len(masks))
    landed_ref = next(rest)
    side_outs, carried_out = take(len(kinds)), take(len(masks))
    upstream_ref, key_ref, query_ref, value_ref, key_t_ref, key_sum, value_sum, delta_ref, up_ref, sent_ref = take(10)
    in_send, in_recv, out_send, out_recv = take(4)
    carry = carry_copies(masks, carried, carried_out, *take(2)) if masks else []
    side = home_steps(kinds, False, False, side_ins + side_outs + list(rest))

    slot = Slot(heads)
    rows = blocks_ref.shape[2]
    span = slot.count * rows
    greet(slot.partners())
    for needed, one in slot.inward(blocks_ref, upstream_ref, in_send, in_recv):
        pl.when(needed)(one.start)

    @pl.when(slot.holds)
    def _():
        key_t = head_rows(qkv_ref, HEAD_DIM, HEAD_DIM)
        key_ref[...] = live_keys(key_t, length_ref[0])
        key_t_ref[...] = key_t
        query_ref[...] = scaled_queries(head_rows(qkv_ref, 0, HEAD_DIM))
        value_t = head_rows(qkv_ref, 2 * HEAD_DIM, HEAD_DIM)
        value_ref[...] = jnp.transpose(value_t.astype(f32)).astype(bf16)
        key_sum[...] = jnp.zeros_like(key_sum)
        value_sum[...] = jnp.zeros_like(value_sum)
        upstream_ref[slot.me] = blocks_ref[slot.head]
        for one in slot.inward_landed(upstream_ref, in_send, in_recv):
            one.wait_recv()
        upstream = head_rows(upstream_ref, 0, HEAD_DIM)
        up_ref[...] = upstream
        delta_ref[...] = jnp.sum(upstream.astype(f32) * out_ref[...], axis=0, keepdims=True)

    next(side)
    for one in carry:
        one.start()

    def query_block(q):
        here = pl.ds(q * step, step)
        query, up = query_ref[:, here], up_ref[:, here]
        total, delta = total_ref[:, here], delta_ref[:, here]

        def meet(k, query_sum, masked):
            there = pl.ds(k * step if masked else pl.multiple_of(k * step, step), step)
            scores = jnp.dot(key_ref[there, :], query, preferred_element_type=f32)
            if masked:
                scores = causal(scores)
            probs = jnp.exp(scores - total)
            d_probs = jnp.dot(value_ref[there, :], up, preferred_element_type=f32)
            d_scores = (probs * (d_probs - delta)).astype(bf16)
            key_sum[:, there] += contract(query[:HEAD_DIM], d_scores, NT)
            value_sum[:, there] += contract(up, probs.astype(bf16), NT)
            return query_sum + contract(key_t_ref[:, there], d_scores)

        query_sum = meet(q, jnp.zeros((HEAD_DIM, step), f32), True)
        if q:
            query_sum = lax.fori_loop(0, q, lambda k, s: meet(k, s, False), query_sum)
        cosine, sine = cosine_ref[:, here], sine_ref[:, here]
        grad = jnp.concatenate(
            [
                unrotate(query_sum * score_scale, cosine, sine),
                unrotate(key_sum[:, here], cosine, sine),
                value_sum[:, here],
            ],
            axis=0,
        ).astype(bf16)
        for i in range(step // rows):
            place = q * (step // rows) + i
            sent_ref[place] = grad[:, i * rows : (i + 1) * rows]
            one = slot.outward(sent_ref, landed_ref, out_send, out_recv, place)
            pl.when(slot.me != place)(one.start)

    for q in reversed(range(span // step)):
        pl.when(slot.holds)(functools.partial(query_block, q))
        next(side, None)

    @pl.when(slot.holds)
    def _():
        landed_ref[slot.head] = sent_ref[slot.me]

    for _ in side:
        pass
    for needed, one in slot.outward_landed(landed_ref, out_send, out_recv):
        pl.when(needed)(one.wait_recv)
    for one in carry:
        one.wait()
    for needed, one in slot.inward(blocks_ref, upstream_ref, in_send, in_recv):
        pl.when(needed)(one.wait_send)
    for place in range(slot.count):
        one = slot.outward(sent_ref, landed_ref, out_send, out_recv, place)
        pl.when(slot.holds & (slot.me != place))(one.wait_send)


def attend_back(qkv, length, out, total, blocks, tables, parts, carried, masks, sizes, number):
    heads, _, rows = blocks.shape
    count = qkv.shape[0]
    span = count * rows
    step = min(512, span)
    kinds, operands, side_specs, side_shapes, side_scratch = home_plan(parts, sizes)
    carry_shapes = [jax.ShapeDtypeStruct(array.shape, array.dtype) for array in carried]
    carry_sems = [DMA((len(masks), len(masks[0])))] * 2 if masks else []
    got = pl.pallas_call(
        functools.partial(attend_back_kernel, step, heads, kinds, masks),
        out_shape=[jax.ShapeDtypeStruct((heads,) + qkv.shape[1:], bf16)] + side_shapes + carry_shapes,
        in_specs=[SMEM] + [VMEM] * 6 + side_specs + [ANY] * len(carried),
        out_specs=[VMEM] * (1 + len(side_shapes)) + [ANY] * len(carried),
        scratch_shapes=[
            pltpu.VMEM(blocks.shape[:0] + (count,) + blocks.shape[1:], bf16),
            pltpu.VMEM((span, 2 * HEAD_DIM), bf16),
            pltpu.VMEM((2 * HEAD_DIM, span), bf16),
            pltpu.VMEM((span, HEAD_DIM), bf16),
            pltpu.VMEM((HEAD_DIM, span), bf16),
            pltpu.VMEM((HEAD_DIM, span), f32),
            pltpu.VMEM((HEAD_DIM, span), f32),
            pltpu.VMEM((1, span), f32),
            pltpu.VMEM((HEAD_DIM, span), bf16),
            pltpu.VMEM(qkv.shape, bf16),
        ]
        + [DMA((count,))] * 4
        + carry_sems
        + side_scratch,
        compiler_params=pltpu.CompilerParams(
            collective_id=number, has_side_effects=True, vmem_limit_bytes=58 << 20
        ),
    )(length, qkv, out, total, *tables, blocks, *operands, *carried)
    return got[0], got[1 : 1 + len(side_shapes)], got[1 + len(side_shapes) :]


EXACT = lax.Precision.HIGHEST


def expert_of_place(count, stride, own):
    expert = lax.broadcasted_iota(jnp.int32, (EXPERTS, count), 0)
    column = lax.broadcasted_iota(jnp.int32, (EXPERTS, count), 1)
    place = column - ((expert // own) * stride + (expert % own) * PLACES)
    inside = (place >= 0) & (place < PLACES)
    at = jnp.sum(jnp.where(inside, place, 0), axis=0, keepdims=True)
    return inside.astype(f32), at.astype(f32)


def spots(hits, earlier, count, stride, own):
    expert_at, place_at = expert_of_place(count, stride, own)
    low = expert_at.astype(bf16)
    hit = contract(hits.astype(bf16), low)
    before = contract(earlier.astype(bf16), low)
    return jnp.where((hit > 0.5) & (before == place_at), 1.0, 0.0)


def first_place(rows):
    return (lax.axis_index("ctx") * lax.axis_size("expert") + lax.axis_index("expert")) * rows


def live(length_ref, first_ref, shape):
    return first_ref[0] + lax.broadcasted_iota(jnp.int32, shape, 0) < length_ref[0]


def routing_kernel(length_ref, first_ref, routes_ref, cotangent_ref, branch_ref, rows_ref, hits_ref, earlier_ref):
    rows = routes_ref.shape[0]
    own = EXPERTS // rows_ref.shape[0]
    alive = live(length_ref, first_ref, (rows, 1))
    expert = lax.broadcasted_iota(jnp.int32, (rows, EXPERTS), 1)
    routes = routes_ref[...]
    named = (routes[:, 0:1] == expert) | (routes[:, 1:2] == expert)
    hits = jnp.where(named, 1.0, 0.0) * jnp.where(alive, 1.0, 0.0)
    token = lax.broadcasted_iota(jnp.int32, (rows, rows), 0)
    other = lax.broadcasted_iota(jnp.int32, (rows, rows), 1)
    earlier = contract(jnp.where(other < token, 1.0, 0.0).astype(bf16), hits.astype(bf16))
    hits_ref[...] = hits
    earlier_ref[...] = earlier
    branch = jnp.where(alive, cotangent_ref[...].astype(f32), 0.0).astype(bf16)
    branch_ref[...] = branch
    spread_out = spots(hits, earlier, EXPERTS * PLACES, own * PLACES, own)
    placed = contract(jnp.transpose(spread_out).astype(bf16), branch)
    rows_ref[...] = placed.astype(bf16).reshape(rows_ref.shape)


def routing(length, first, routes, cotangent, expert_size):
    rows, width = cotangent.shape
    return pl.pallas_call(
        routing_kernel,
        out_shape=(
            jax.ShapeDtypeStruct((rows, width), bf16),
            jax.ShapeDtypeStruct((expert_size, EXPERTS // expert_size * PLACES, width), bf16),
            jax.ShapeDtypeStruct((rows, EXPERTS), f32),
            jax.ShapeDtypeStruct((rows, EXPERTS), f32),
        ),
        in_specs=[SMEM, SMEM, VMEM, VMEM],
        out_specs=(VMEM,) * 4,
    )(length, first, routes, cotangent)


def project_kernel(tokens_ref, gain_ref, query_ref, key_ref, value_ref, cosine_ref, sine_ref, normed_ref, qkv_ref):
    inputs = tokens_ref[...].astype(f32)
    normed = (inputs * rms_scale(inputs) * gain_ref[...]).astype(bf16)
    normed_ref[...] = normed
    heads, _, rows = qkv_ref.shape
    half = HEAD_DIM // 2
    cosine, sine = cosine_ref[...], sine_ref[...]
    for kind, weight in enumerate((query_ref, key_ref, value_ref)):
        lin = jnp.transpose(contract(normed, weight[...]))
        for head in range(heads):
            mine = lin[head * HEAD_DIM : (head + 1) * HEAD_DIM]
            if kind < 2:
                first, second = mine[:half], mine[half:]
                mine = jnp.concatenate(
                    [first * cosine - second * sine, second * cosine + first * sine], axis=0
                )
            qkv_ref[head, kind * HEAD_DIM : (kind + 1) * HEAD_DIM, :] = mine.astype(bf16)


def project(tokens, gain, weights, tables):
    rows, width = tokens.shape
    return pl.pallas_call(
        project_kernel,
        out_shape=(
            jax.ShapeDtypeStruct((rows, width), bf16),
            jax.ShapeDtypeStruct((width // HEAD_DIM, 3 * HEAD_DIM, rows), bf16),
        ),
        in_specs=[VMEM] * 7,
        out_specs=(VMEM,) * 2,
        compiler_params=pltpu.CompilerParams(vmem_limit_bytes=32 << 20),
    )(tokens, gain, *weights, *tables)


def middle_kernel(
    length_ref, first_ref, tokens_ref, attended_ref, output_ref, gain_ref, router_ref, hits_ref, earlier_ref,
    hidden_ref, normed_ref, rows_ref, scale_ref, gates_ref, flat_ref,
):
    rows, width = tokens_ref.shape
    expert_size = rows_ref.shape[0]
    own = EXPERTS // expert_size
    attended = jnp.transpose(attended_ref[...].reshape(width, rows).astype(f32)).astype(bf16)
    flat_ref[...] = attended
    alive = live(length_ref, first_ref, (rows, 1))
    attn_out = contract(attended, output_ref[...])
    hidden = tokens_ref[...].astype(f32) + jnp.where(alive, attn_out, 0.0)
    hidden_ref[...] = hidden
    normed = (hidden * rms_scale(hidden) * gain_ref[...]).astype(bf16)
    normed_ref[...] = normed
    hits, earlier = hits_ref[...], earlier_ref[...]
    logits = contract(normed, router_ref[...])
    top = jnp.max(jnp.where(hits > 0.5, logits, masked_value), axis=1, keepdims=True)
    powers = jnp.where(hits > 0.5, jnp.exp(logits - top), 0.0)
    total = jnp.sum(powers, axis=1, keepdims=True)
    gates = powers / jnp.where(total > 0.0, total, 1.0)
    gates_ref[...] = gates
    spread_out = spots(hits, earlier, EXPERTS * PLACES, own * PLACES, own)
    placed = contract(jnp.transpose(spread_out).astype(bf16), normed)
    rows_ref[...] = placed.astype(bf16).reshape(rows_ref.shape)
    lanes = expert_size * 128
    expert_at, _ = expert_of_place(lanes, 128, own)
    by_place = jnp.dot(gates, expert_at, preferred_element_type=f32, precision=EXACT)
    at_place = spots(hits, earlier, lanes, 128, own) * by_place
    row = jnp.sum(at_place, axis=0, keepdims=True)
    for z in range(expert_size):
        scale_ref[z] = jnp.broadcast_to(row[:, z * 128 : (z + 1) * 128], (8, 128))


def middle(length, first, tokens, attended, output_weight, gain, router, hits, earlier, expert_size):
    rows, width = tokens.shape
    return pl.pallas_call(
        middle_kernel,
        out_shape=(
            jax.ShapeDtypeStruct((rows, width), f32),
            jax.ShapeDtypeStruct((rows, width), bf16),
            jax.ShapeDtypeStruct((expert_size, EXPERTS // expert_size * PLACES, width), bf16),
            jax.ShapeDtypeStruct((expert_size, 8, 128), f32),
            jax.ShapeDtypeStruct((rows, EXPERTS), f32),
            jax.ShapeDtypeStruct((rows, width), bf16),
        ),
        in_specs=[SMEM, SMEM] + [VMEM] * 7,
        out_specs=(VMEM,) * 6,
        compiler_params=pltpu.CompilerParams(vmem_limit_bytes=32 << 20),
    )(length, first, tokens, attended, output_weight, gain, router, hits, earlier)


def turn_kernel(
    length_ref, first_ref, back_ref, flat_ref, dots_ref, hits_ref, earlier_ref, gates_ref, normed_ref, hidden_ref,
    cotangent_ref, gain_ref, router_ref, output_ref, d_hidden_ref, d_attended_ref, d_attn_ref, router_grad, gain_grad,
):
    rows, width = normed_ref.shape
    expert_size = back_ref.shape[0]
    own = EXPERTS // expert_size
    alive = live(length_ref, first_ref, (rows, 1))
    hits, earlier, gates = hits_ref[...], earlier_ref[...], gates_ref[...]
    lanes = expert_size * 128
    expert_at, _ = expert_of_place(lanes, 128, own)
    row = jnp.concatenate([dots_ref[z, 0:1, :] for z in range(expert_size)], axis=1)
    at_place = jnp.where(spots(hits, earlier, lanes, 128, own) > 0.5, row, 0.0)
    d_gates = lax.dot_general(at_place, expert_at, NT, preferred_element_type=f32, precision=EXACT)
    mean = jnp.sum(gates * d_gates, axis=1, keepdims=True)
    d_logits = (gates * (d_gates - mean)).astype(bf16)
    normed = normed_ref[...]
    router_grad[...] = contract(normed, d_logits, TN)
    spread_out = spots(hits, earlier, EXPERTS * PLACES, own * PLACES, own).astype(bf16)
    placed = back_ref[...].reshape(EXPERTS * PLACES, width)
    d_normed = contract(spread_out, placed) + flat_ref[...].astype(f32)
    d_normed = d_normed + contract(d_logits, router_ref[...], NT)
    hidden = hidden_ref[...]
    scale = rms_scale(hidden)
    normal = hidden * scale
    gain_grad[...] = jnp.sum(d_normed * normal, axis=0, keepdims=True)
    d_hidden = cotangent_ref[...].astype(f32) + rms_back(normal, scale, gain_ref[...], d_normed)
    d_hidden_ref[...] = d_hidden
    d_attn = jnp.where(alive, d_hidden, 0.0).astype(bf16)
    d_attn_ref[...] = d_attn
    d_attended = jnp.transpose(contract(d_attn, output_ref[...], NT))
    d_attended_ref[...] = d_attended.astype(bf16).reshape(d_attended_ref.shape)


def turn(length, first, back, flat, dots, hits, earlier, gates, normed, hidden, cotangent, gain, router, output_weight):
    rows, width = normed.shape
    return pl.pallas_call(
        turn_kernel,
        out_shape=(
            jax.ShapeDtypeStruct((rows, width), f32),
            jax.ShapeDtypeStruct((width // HEAD_DIM, HEAD_DIM, rows), bf16),
            jax.ShapeDtypeStruct((rows, width), bf16),
            jax.ShapeDtypeStruct((width, EXPERTS), f32),
            jax.ShapeDtypeStruct((1, width), f32),
        ),
        in_specs=[SMEM, SMEM] + [VMEM] * 12,
        out_specs=(VMEM,) * 5,
        compiler_params=pltpu.CompilerParams(vmem_limit_bytes=32 << 20),
    )(length, first, back, flat, dots, hits, earlier, gates, normed, hidden, cotangent, gain, router, output_weight)


def join_kernel(
    length_ref, first_ref, back_ref, flat_ref, hits_ref, earlier_ref, hidden_ref, out_ref,
):
    rows, width = hidden_ref.shape
    own = EXPERTS // back_ref.shape[0]
    spread_out = spots(hits_ref[...], earlier_ref[...], EXPERTS * PLACES, own * PLACES, own).astype(bf16)
    mixed = contract(spread_out, back_ref[...].reshape(EXPERTS * PLACES, width)) + flat_ref[...].astype(f32)
    alive = live(length_ref, first_ref, (rows, 1))
    out_ref[...] = (hidden_ref[...] + jnp.where(alive, mixed, 0.0)).astype(bf16)


def join(length, first, back, flat, hits, earlier, hidden):
    return pl.pallas_call(
        join_kernel,
        out_shape=jax.ShapeDtypeStruct(hidden.shape, bf16),
        in_specs=[SMEM, SMEM] + [VMEM] * 5,
        out_specs=VMEM,
        compiler_params=pltpu.CompilerParams(vmem_limit_bytes=32 << 20),
    )(length, first, back, flat, hits, earlier, hidden)


def last_kernel(
    shard, grads_ref, query_ref, key_ref, value_ref, normed_ref, tokens_ref, gain_ref, d_hidden_ref, attended_ref,
    d_attn_ref, input_grad, gain_grad, sums_ref,
):
    rows, width = normed_ref.shape
    heads = grads_ref.shape[0]
    lins = []
    d_normed = jnp.zeros((width, rows), f32)
    for kind, weight in enumerate((query_ref, key_ref, value_ref)):
        at = slice(kind * HEAD_DIM, (kind + 1) * HEAD_DIM)
        lin = jnp.concatenate([grads_ref[head, at, :] for head in range(heads)], axis=0)
        lins.append(lin)
        d_normed = d_normed + contract(weight[...], lin)
    d_normed = jnp.transpose(d_normed)
    inputs = tokens_ref[...].astype(f32)
    scale = rms_scale(inputs)
    normal = inputs * scale
    gain_grad[...] = jnp.sum(d_normed * normal, axis=0, keepdims=True)
    d_inputs = d_hidden_ref[...] + rms_back(normal, scale, gain_ref[...], d_normed)
    input_grad[...] = d_inputs.astype(bf16)
    normed_t = jnp.transpose(normed_ref[...].astype(f32)).astype(bf16)
    attended_t = jnp.transpose(attended_ref[...].astype(f32)).astype(bf16)
    grads = [contract(normed_t, lin, NT) for lin in lins] + [contract(attended_t, d_attn_ref[...])]
    plane_size, expert_size, count, _ = sums_ref.shape
    for p in range(plane_size):
        for z in range(expert_size):
            first = (p * expert_size + z) * shard
            parts = [grad[first : first + shard] for grad in grads]
            if count > 4 * shard:
                parts.append(jnp.zeros((count - 4 * shard, width), f32))
            sums_ref[p, z] = jnp.concatenate(parts, axis=0).astype(bf16)


def last(grads, weights, normed, tokens, gain, d_hidden, attended, d_attn, sizes):
    rows, width = normed.shape
    dp_size, ctx_size, expert_size = sizes
    shard = width // (dp_size * ctx_size * expert_size)
    count = -(-4 * shard // 16) * 16
    return pl.pallas_call(
        functools.partial(last_kernel, shard),
        out_shape=(
            jax.ShapeDtypeStruct((rows, width), bf16),
            jax.ShapeDtypeStruct((1, width), f32),
            jax.ShapeDtypeStruct((dp_size * ctx_size, expert_size, count, width), bf16),
        ),
        in_specs=[VMEM] * 10,
        out_specs=(VMEM,) * 3,
        compiler_params=pltpu.CompilerParams(vmem_limit_bytes=48 << 20),
    )(grads, *weights, normed, tokens, gain, d_hidden, attended, d_attn)


def local(
    tokens,
    lengths,
    routes,
    norm1_gain,
    query_weight,
    key_weight,
    value_weight,
    output_weight,
    norm2_gain,
    router_weight,
    expert_gate,
    expert_up,
    expert_down,
    shared_gate,
    shared_up,
    shared_down,
    cotangent,
):
    sizes = dp_size, ctx_size, expert_size = sizes_of()
    plane_size, slot_size = dp_size * ctx_size, ctx_size * expert_size
    rows, width = tokens.shape[1:]
    heads, own, shard = width // HEAD_DIM, EXPERTS // expert_size, width // (dp_size * slot_size)
    plane = (lax.axis_index("dp") * ctx_size + lax.axis_index("ctx")).astype(jnp.int32)[None]
    first = first_place(rows).astype(jnp.int32)[None]
    tokens, routes, cotangent = tokens[0], routes[0], cotangent[0]
    gain_one, gain_two = norm1_gain[None], norm2_gain[None]
    weights = (query_weight, key_weight, value_weight)

    branch_rows, up_placed, hits, earlier = routing(lengths, first, routes, cotangent, expert_size)

    groups = own // GROUP
    other_core = (lax.axis_index("dp") + 1) % dp_size
    ctx = lax.axis_index("ctx")
    bits = bits_of(ctx_size)
    group_bits = [group_bit(g, ctx_size) for g in range(groups)]
    slice_masks = [subsets([bit for bit in bits if bit != mine]) for mine in group_bits]

    def grouped(placed):
        return placed.reshape(expert_size, groups, GROUP * PLACES, width)

    places = jnp.arange(rows, dtype=jnp.int32)
    normed, qkv = project(tokens, gain_one, weights, rope_tables(first[0] + places))
    (qkv, out_t, log_total, attended), (up_rows, up_flat) = attend(
        qkv, lengths, [grouped(up_placed), branch_rows], sizes, 1
    )
    hidden, normed_two, in_placed, scale, gates, attended = middle(
        lengths, first, tokens, attended, output_weight, gain_two, router_weight, hits, earlier, expert_size
    )

    in_rows, in_flat, scale = spread([grouped(in_placed), normed_two], scale, sizes, 3)
    sources = 4 * expert_size
    here = lax.axis_index("dp")
    blocks = jnp.stack(
        [
            jnp.stack([core * ctx_size + flip(ctx, mask) for core in (here, other_core) for mask in (0, bit)])
            for bit in group_bits
        ]
    )
    scale = jnp.take(scale[:, :, 0, : own * PLACES], blocks.reshape(-1), axis=0)
    scale = scale.reshape(groups, sources, groups, GROUP, PLACES)
    scale = jnp.stack([jnp.swapaxes(scale[g, :, g], 0, 1) for g in range(groups)])
    table = jnp.concatenate(
        [
            jnp.stack([here * ctx_size + flip(ctx, mask) for mask in masks])
            for masks in slice_masks
        ]
    ).astype(jnp.int32)
    shared_result, shared_d, *shared_grads = shared(
        plane, in_flat, up_flat, shared_gate, shared_up, shared_down, expert_size
    )
    part = shared_gate.shape[1] // plane_size
    result, d_rows, dots, slice_grads = experts(
        table, in_rows, up_rows, scale, expert_gate, expert_up, expert_down, part
    )
    dots = jnp.swapaxes(dots, 1, 2).reshape(groups, 4, expert_size, GROUP * PLACES)
    dots = jnp.stack(
        [
            jnp.pad(dots[g], [(0, 0), (0, 0), (g * GROUP * PLACES, (groups - 1 - g) * GROUP * PLACES)])
            for g in range(groups)
        ]
    )
    owner = blocks[:, :, None] == jnp.arange(plane_size)
    dots = jnp.sum(jnp.where(owner[..., None, None], dots[:, :, None], 0.0), axis=(0, 1))
    dots = jnp.pad(dots[:, :, None], [(0, 0), (0, 0), (0, 7), (0, 128 - own * PLACES)])
    back, flat, dots = bring_home([d_rows, shared_d], sizes, 4, dots=dots)

    d_hidden, d_attended, d_attn, router_grad, gain_two_grad = turn(
        lengths, first, back, flat, dots, hits, earlier, gates, normed_two, hidden, cotangent, gain_two,
        router_weight, output_weight,
    )

    all_tables = rope_tables(jnp.arange(slot_size * rows, dtype=jnp.int32))
    others = [
        (array, tuple(masks[k] for masks in slice_masks))
        for slices in slice_grads
        for k, array in enumerate(slices)
        if k
    ]
    early, late = others[: len(others) // 3], others[len(others) // 3 :]
    d_qkv, (out_back, out_flat), early_in = attend_back(
        qkv, lengths, out_t, log_total, d_attended, all_tables, [result, shared_result],
        [array for array, _ in early], tuple(masks for _, masks in early), sizes, 6,
    )
    output_rows = join(lengths, first, out_back, out_flat, hits, earlier, hidden)

    input_grad, gain_one_grad, sums = last(
        d_qkv, weights, normed, tokens, gain_one, d_hidden, attended, d_attn, sizes
    )
    devices = (plane_size, expert_size)
    small = jnp.concatenate(
        [
            router_grad.reshape(devices + (shard * EXPERTS,)),
            gain_one_grad.reshape(devices + (shard,)),
            gain_two_grad.reshape(devices + (shard,)),
        ],
        axis=-1,
    )
    small = jnp.pad(small, [(0, 0), (0, 0), (0, 1024 - small.shape[-1])])
    sums, small, shared_gate_grad, shared_up_grad, shared_down_grad, *late_in = bring_home(
        [sums], sizes, 8, dots=small.reshape(devices + (8, 128)), grads=shared_grads,
        carried=[array for array, _ in late], masks=tuple(masks for _, masks in late),
    )
    arrived = list(early_in) + list(late_in)
    count = len(arrived) // 3
    expert_grads = [
        sum((array.astype(f32) for array in arrived[kind * count : (kind + 1) * count]), slices[0].astype(f32))
        for kind, slices in enumerate(slice_grads)
    ]
    sums = jnp.sum(sums.astype(f32), axis=0)
    small = jnp.sum(small, axis=0).reshape(1024)
    routed = shard * EXPERTS
    return (
        output_rows[None],
        input_grad[None],
        small[routed : routed + shard],
        *(sums[kind * shard : (kind + 1) * shard] for kind in range(4)),
        small[routed + shard : routed + 2 * shard],
        small[:routed].reshape(shard, EXPERTS),
        *expert_grads,
        shared_gate_grad,
        shared_up_grad,
        shared_down_grad,
    )


def solution(mesh):
    tokens = P("dp", ("ctx", "expert"), None)
    whole = P()
    experts = P("expert", None, None)
    everywhere = ("dp", "ctx", "expert")
    return jax.shard_map(
        local,
        mesh=mesh,
        in_specs=(tokens, P("dp"), tokens)
        + (whole,) * 7
        + (experts,) * 3
        + (whole,) * 3
        + (tokens,),
        out_specs=(tokens, tokens, P(everywhere))
        + (P(everywhere, None),) * 4
        + (P(everywhere), P(everywhere, None))
        + (P("expert", None, PLANE),) * 2
        + (P("expert", PLANE, None),)
        + (P(everywhere, None),) * 3,
        check_vma=False,
    )
```

time: 699 us -> 328 us (0.47)
  Pallas kernels: 18.8 us -> 287 us
  waiting for transfers between devices: 247 us -> 0 us
  blocking collectives: 164 us -> 0 us
  matrix products: 96.8 us -> 0 us
  local copies, waits for them, and re-layouts: 66.4 us -> 26.2 us
  starting transfers between devices: 37.8 us -> 0 us
  other arithmetic: 43.2 us -> 12.1 us
  between operations: 17.2 us -> 2.11 us
    pallas_call x2 -> x13, Pallas kernels: 18.8 us -> 287 us  [the longest x2 107 us: bring_home(): pl.pallas_call(functools.partial(home_kernel, kinds, dots is not None, gr...]
    unnamed x14 -> x0, waiting for transfers between devices: 136 us -> none
    dot_general x35 -> x0, matrix products: 96.8 us -> none  [the longest x18 70.6 us: dot(): return jnp.einsum(spec, a, b, preferred_element_type=f32)]
    all_to_all x4 -> x0, blocking collectives: 76.2 us -> none  [the longest x2 38 us: to_experts(): lax.all_to_all(flat.reshape((expert_size, -1) + flat.shape[1:]), 'expert'...]
    all_to_all x9 -> x0, waiting for transfers between devices: 58.1 us -> none  [the longest x4 36.6 us: to_experts(): lax.all_to_all(flat.reshape((expert_size, -1) + flat.shape[1:]), 'expert'...]
    psum x1 -> x0, blocking collectives: 41.6 us -> none  [local(): lax.psum(jnp.concatenate([d_router, d_gain_one[:, None], d_gain_two[:, No...]
    all_to_all x9 -> x0, starting transfers between devices: 37 us -> none  [the longest x4 16.9 us: to_experts(): lax.all_to_all(flat.reshape((expert_size, -1) + flat.shape[1:]), 'expert'...]
    all_gather x3 -> x0, waiting for transfers between devices: 28.7 us -> none  [the longest x2 28.7 us: spread(): return lax.all_gather(jnp.concatenate([mine, flat], axis=0), PLANE, axis=0)]
  transfers between devices with their start and end apart: 21 -> 0, of which waited for: 12 -> 0; matrix products, arithmetic and copies ran while one was open for 21% -> 0% of each run, Pallas kernels for 3% -> 0%
where the time goes in v4:
time: 328 us; the launch traced here: 327 us
  Pallas kernels  287 us (88%)
  local copies, waits for them, and re-layouts  26.2 us (8%)
  other arithmetic  12.1 us (4%)
    pallas_call x2, Pallas kernels, bring_home(): pl.pallas_call(functools.partial(home_kernel, kinds, dots is not None, gr...  107 us
    pallas_call x1, Pallas kernels, attend_back(): pl.pallas_call(functools.partial(attend_back_kernel, step, heads, kinds,...  58.4 us
    pallas_call x1, Pallas kernels, attend(): pl.pallas_call(functools.partial(attend_kernel, step, heads, kinds), out_...  52.8 us
    pallas_call x1, Pallas kernels, spread(): pl.pallas_call(functools.partial(spread_kernel, kinds, True), out_shape=o...  25.7 us
    pallas_call x1, Pallas kernels, experts(): pl.pallas_call(functools.partial(experts_kernel, slices), grid_spec=pltpu...  21.5 us
    unnamed x122, local copies, waits for them, and re-layouts  20.5 us
    pallas_call x1, Pallas kernels, shared(): pl.pallas_call(functools.partial(shared_kernel, plane_size), grid_spec=pl...  8.09 us
    add x3, other arithmetic, local(): sum((array.astype(f32) for array in arrived[kind * count:(kind + 1) * cou...  7.58 us

profile of v4, /device:TPU:0, one launch (start us, length us, event | category | flops | bytes accessed | tf_op | source)
XLA Modules:
  0.0 326.9 jit_solution(9516673283173775271)
XLA Ops:
  1.9 1.3 copy-done.1
  3.2 1.3 copy-done.3
  4.4 1.3 copy-done.5
  10.5 2.5 shard_map.281
  13.0 52.8 %shard_map.282 = (bf16[16,192,128]{2,1,0:T(8,128)(2,1)}, f32[64,2048]{1,0:T(8,128)}, f32[1,2048]{1,0:T(1,128)}, bf16[12,64,128]{2,1,0:T(8,128)(2,1)}, bf16[2,4,4...) custom-call(s32[1]{0:T(128)S(6)} %copy.54.length_ref, bf16[12,192,128]{2,1,0:T(8,128)(2,1)} %copy-done.14, ...), custom_call_target="tpu_custom_call" | custom-call | tf_op jit(solution)/shard_map/pallas_call | solution.py:1164
  67.0 1.4 shard_map.283
  68.5 25.7 %shard_map.284 = (bf16[2,4,4,48,768]{4,3,2,1,0:T(8,128)(2,1)S(1)}, bf16[8,128,768]{2,1,0:T(8,128)(2,1)S(1)}, f32[8,4,8,128]{3,2,1,0:T(8,128)S(1)}) custom-call(bf16[4,2,48,768]{3,2,1,0:T(8,128)(2,1)S(1)} %bitcast.45, bf16[128,768]{1,0:T(8,128)(2,1)S(1)} %get-tuple-element.82.refs_1_.normed_ref, f32[4,8,128]{2,1,0:T(8,128)S(1)} %get-tuple-element.83.refs_2_), custom_call_target="tpu_custom_call" | custom-call | tf_op jit(solution)/shard_map/pallas_call | solution.py:394
  94.3 1.4 copy-done.7
  95.7 1.2 copy-done.10
  99.8 21.5 %shard_map.285 = (bf16[2,4,4,48,768]{4,3,2,1,0:T(8,128)(2,1)}, bf16[2,4,4,48,768]{4,3,2,1,0:T(8,128)(2,1)}, f32[2,2,16,24]{3,2,1,0:T(8,128)}, bf16[4,768,256]{2,...) custom-call(s32[4]{0:T(128)} %pad_add_fusion.1.table_ref, ...), custom_call_target="tpu_custom_call" | custom-call | tf_op jit(solution)/shard_map/pallas_call | solution.py:899
  123.9 8.1 %shard_map.286 = (bf16[8,128,768]{2,1,0:T(8,128)(2,1)}, bf16[8,128,768]{2,1,0:T(8,128)(2,1)}, bf16[4,192,256]{2,1,0:T(8,128)(2,1)}, bf16[4,192,256]{2,1,0:T(8,128)(2,1)}, bf16[4,64,768]{2,1,0:T(8,128)(2,1)}) custom-call(s32[1]{0:T(128)} %bitcast.5.plane_ref, bf16[8,128,768]{2,1,0:T(8,128)(2,1)} %copy-done.10, bf16[8,128,768]{2,1,0:T(8,128)(2,1)} %get-tuple-element.89.up_ref, ...), custom_call_target="tpu_custom_call" | custom-call | tf_op jit(solution)/shard_map/pallas_call | solution.py:966
  132.1 34.7 %shard_map.287 = (bf16[4,2,48,768]{3,2,1,0:T(8,128)(2,1)}, bf16[128,768]{1,0:T(8,128)(2,1)}, f32[4,8,128]{2,1,0:T(8,128)}) custom-call(bf16[2,4,4,48,768]{4,3,2,1,0:T(8,128)(2,1)} %get-tuple-element.87.refs_0_, bf16[8,128,768]{2,1,0:T(8,128)(2,1)} %get-tuple-element.90.refs_1_, f32[8,4,8,128]{3,2,1,0:T(8,128)} %pad.18.refs_2_), custom_call_target="tpu_custom_call" | custom-call | tf_op jit(solution)/shard_map/pallas_call | solution.py:772
  166.8 1.1 copy-done.17
  169.5 2.2 shard_map.288
  173.1 1.8 multiply_sine_fusion
  175.0 58.4 %shard_map.289 = (bf16[12,192,128]{2,1,0:T(8,128)(2,1)}, bf16[4,2,48,768]{3,2,1,0:T(8,128)(2,1)}, bf16[128,768]{1,0:T(8,128)(2,1)}, bf16[4,768,256]{2,1,0:T(8,128)(2,1)}) custom-call(s32[1]{0:T(128)S(6)} %copy.54.length_ref, bf16[16,192,128]{2,1,0:T(8,128)(2,1)} %get-tuple-element.75.qkv_ref, f32[64,2048]{1,0:T(8,128)} %get-tuple-element.76.out_ref, ...), custom_call_target="tpu_custom_call" | custom-call | tf_op jit(solution)/shard_map/pallas_call | solution.py:1306
  233.6 1.1 copy-done.16
  234.6 4.5 %shard_map.291 = (bf16[128,768]{1,0:T(8,128)(2,1)}, f32[1,768]{1,0:T(1,128)S(1)}, bf16[8,4,96,768]{3,2,1,0:T(8,128)(2,1)}) custom-call(bf16[12,192,128]{2,1,0:T(8,128)(2,1)S(1)} %copy-done.16, bf16[768,768]{1,0:T(8,128)(2,1)S(1)} %copy-done.2, bf16[768,768]{1,0:T(8,128)(2,1)S(1)} %copy-done.4, bf16[768,768]{1,0:T(8,128)(2,1)S(1)} %copy-done.6, ...), custom_call_target="tpu_custom_call" | custom-call | tf_op jit(solution)/shard_map/pallas_call | solution.py:1591
  240.3 72.6 %shard_map.292 = (bf16[4,96,768]{2,1,0:T(8,128)(2,1)}, f32[4,8,128]{2,1,0:T(8,128)}, f32[24,2048]{1,0:T(8,128)}, f32[24,2048]{1,0:T(8,128)}, f32[64,768]{1,0:T(8...) custom-call(bf16[8,4,96,768]{3,2,1,0:T(8,128)(2,1)} %get-tuple-element.109.refs_0_, ...), custom_call_target="tpu_custom_call" | custom-call | tf_op jit(solution)/shard_map/pallas_call | solution.py:772
  313.0 3.6 %convert_add_fusion = f32[4,256,768]{2,1,0:T(8,128)} fusion(bf16[4,256,768]{2,1,0:T(8,128)(2,1)} %get-tuple-element.125, bf16[4,256,768]{2,1,0:T(8,128)(2,1)S(1)} %copy-done.44), kind=kLoop, calls=%fused_computation.1 | loop fusion | flops 2359296 | bytes 6291456 | tf_op jit(solution)/shard_map/add | solution.py:1730
  316.6 2.0 convert_add_fusion.1
  318.6 1.0 copy-done.45
  319.6 2.0 convert_add_fusion.2
  323.8 1.1 shard_map.290
  (161 shorter events, 20.3 us)
Async XLA Ops:
  9.0 56.9 %copy-start.51 = (bf16[768,16]{0,1:T(8,128)(2,1)S(1)}, bf16[768,16]{0,1:T(8,128)(2,1)}, u32[]{:S(2)}) copy-start(bf16[768,16]{0,1:T(8,128)(2,1)} %param.26) | copy-start | bytes 73732
  9.0 57.1 %copy-start.53 = (f32[768]{0:T(1024)S(1)}, f32[768]{0:T(1024)}, u32[]{:S(2)}) copy-start(f32[768]{0:T(1024)} %param.25) | copy-start | bytes 9220
  9.0 57.1 %copy-start = (bf16[768,768]{1,0:T(8,128)(2,1)S(1)}, bf16[768,768]{1,0:T(8,128)(2,1)}, u32[]{:S(2)}) copy-start(bf16[768,768]{1,0:T(8,128)(2,1)} %output_ref.3) | copy-start | bytes 3538948
  9.0 57.1 %copy-start.9 = (bf16[1,128,768]{2,1,0:T(8,128)(2,1)S(1)}, bf16[1,128,768]{2,1,0:T(8,128)(2,1)}, u32[]{:S(2)}) copy-start(bf16[1,128,768]{2,1,0:T(8,128)(2,1)} %param.17) | copy-start | bytes 589828
  13.0 53.1 %copy-start.18 = (f32[128,16]{1,0:T(8,128)S(1)}, f32[128,16]{1,0:T(8,128)}, u32[]{:S(2)}) copy-start(f32[128,16]{1,0:T(8,128)} %get-tuple-element.79.hits_ref) | copy-start | bytes 24580
  13.0 53.1 %copy-start.19 = (f32[128,16]{1,0:T(8,128)S(1)}, f32[128,16]{1,0:T(8,128)}, u32[]{:S(2)}) copy-start(f32[128,16]{1,0:T(8,128)} %get-tuple-element.80.earlier_ref) | copy-start | bytes 24580
  67.0 29.8 %copy-start.35 = (f32[1,768]{1,0:T(1,128)}, f32[1,768]{1,0:T(1,128)S(1)}, u32[]{:S(2)}) copy-start(f32[1,768]{1,0:T(1,128)S(1)} %broadcast_in_dim.63.gain_ref) | copy-start | bytes 9220
  68.5 25.8 %copy-start.12 = (bf16[128,768]{1,0:T(8,128)(2,1)}, bf16[128,768]{1,0:T(8,128)(2,1)S(1)}, u32[]{:S(2)}) copy-start(bf16[128,768]{1,0:T(8,128)(2,1)S(1)} %get-tuple-element.82.refs_1_.normed_ref) | copy-start | bytes 589828
  68.5 28.4 %copy-start.25 = (bf16[128,768]{1,0:T(8,128)(2,1)}, bf16[128,768]{1,0:T(8,128)(2,1)S(1)}, u32[]{:S(2)}) copy-start(bf16[128,768]{1,0:T(8,128)(2,1)S(1)} %get-tuple-element.106.attended_ref) | copy-start | bytes 589828
  68.5 28.4 %copy-start.33 = (f32[128,16]{1,0:T(8,128)}, f32[128,16]{1,0:T(8,128)S(1)}, u32[]{:S(2)}) copy-start(f32[128,16]{1,0:T(8,128)S(1)} %get-tuple-element.95.gates_ref) | copy-start | bytes 24580
  132.0 34.7 %copy-start.11 = (bf16[1,128,768]{2,1,0:T(8,128)(2,1)S(1)}, bf16[1,128,768]{2,1,0:T(8,128)(2,1)}, u32[]{:S(2)}) copy-start(bf16[1,128,768]{2,1,0:T(8,128)(2,1)} %param.33) | copy-start | bytes 589828
  132.0 34.7 %copy-start.13 = (bf16[128,768]{1,0:T(8,128)(2,1)S(1)}, bf16[128,768]{1,0:T(8,128)(2,1)}, u32[]{:S(2)}) copy-start(bf16[128,768]{1,0:T(8,128)(2,1)} %copy-done.12) | copy-start | bytes 589828
  132.0 34.7 %copy-start.20 = (f32[128,16]{1,0:T(8,128)S(1)}, f32[128,16]{1,0:T(8,128)}, u32[]{:S(2)}) copy-start(f32[128,16]{1,0:T(8,128)} %get-tuple-element.80.earlier_ref) | copy-start | bytes 24580
  132.1 34.7 %copy-start.34 = (f32[128,16]{1,0:T(8,128)S(1)}, f32[128,16]{1,0:T(8,128)}, u32[]{:S(2)}) copy-start(f32[128,16]{1,0:T(8,128)} %copy-done.33) | copy-start | bytes 24580
  132.1 34.7 %copy-start.36 = (f32[1,768]{1,0:T(1,128)S(1)}, f32[1,768]{1,0:T(1,128)}, u32[]{:S(2)}) copy-start(f32[1,768]{1,0:T(1,128)} %copy-done.35) | copy-start | bytes 9220
  174.9 58.5 %copy-start.2 = (bf16[768,768]{1,0:T(8,128)(2,1)S(1)}, bf16[768,768]{1,0:T(8,128)(2,1)}, u32[]{:S(2)}) copy-start(bf16[768,768]{1,0:T(8,128)(2,1)} %query_ref.3) | copy-start | bytes 3538948
  174.9 58.5 %copy-start.4 = (bf16[768,768]{1,0:T(8,128)(2,1)S(1)}, bf16[768,768]{1,0:T(8,128)(2,1)}, u32[]{:S(2)}) copy-start(bf16[768,768]{1,0:T(8,128)(2,1)} %key_ref.3) | copy-start | bytes 3538948
  175.0 58.5 %copy-start.6 = (bf16[768,768]{1,0:T(8,128)(2,1)S(1)}, bf16[768,768]{1,0:T(8,128)(2,1)}, u32[]{:S(2)}) copy-start(bf16[768,768]{1,0:T(8,128)(2,1)} %value_ref.3) | copy-start | bytes 3538948
  175.0 58.5 %copy-start.22 = (f32[128,768]{1,0:T(8,128)S(1)}, f32[128,768]{1,0:T(8,128)}, u32[]{:S(2)}) copy-start(f32[128,768]{1,0:T(8,128)} %copy-done.21) | copy-start | bytes 1179652
  175.0 58.5 %copy-start.24 = (bf16[128,768]{1,0:T(8,128)(2,1)S(1)}, bf16[128,768]{1,0:T(8,128)(2,1)}, u32[]{:S(2)}) copy-start(bf16[128,768]{1,0:T(8,128)(2,1)} %copy-done.23) | copy-start | bytes 589828
  175.0 58.5 %copy-start.26 = (bf16[128,768]{1,0:T(8,128)(2,1)S(1)}, bf16[128,768]{1,0:T(8,128)(2,1)}, u32[]{:S(2)}) copy-start(bf16[128,768]{1,0:T(8,128)(2,1)} %copy-done.25) | copy-start | bytes 589828
  175.0 58.5 %copy-start.28 = (bf16[128,768]{1,0:T(8,128)(2,1)S(1)}, bf16[128,768]{1,0:T(8,128)(2,1)}, u32[]{:S(2)}) copy-start(bf16[128,768]{1,0:T(8,128)(2,1)} %copy-done.27) | copy-start | bytes 589828
  175.0 58.5 %copy-start.38 = (f32[1,768]{1,0:T(1,128)S(1)}, f32[1,768]{1,0:T(1,128)}, u32[]{:S(2)}) copy-start(f32[1,768]{1,0:T(1,128)} %copy-done.37) | copy-start | bytes 9220
  240.3 72.7 %copy-start.44 = (bf16[4,256,768]{2,1,0:T(8,128)(2,1)S(1)}, bf16[4,256,768]{2,1,0:T(8,128)(2,1)}, u32[]{:S(2)}) copy-start(bf16[4,256,768]{2,1,0:T(8,128)(2,1)} %get-tuple-element.124) | copy-start | bytes 4718596
  (34 other events, 65.2 us)
